TPU v7x, 1024 devices: a whole 8x8x8 slice. The times are simulated.
1024 devices in a mesh: blocks: 128 (over y, z, core), sub: 8 (over x).
Axes of the slice: x: 8, y: 8, z: 8, core: 2. Of those that a mesh axis runs over, the one named last changes fastest.
Arguments:
- state: float32 [128, 8, 3, 5, 4096], P('blocks', 'sub'), may hold values from -2.5 to 10, as said below
- neighbours: int32 [128, 8, 3, 6, 2], P('blocks', 'sub'), may hold values from 0 to 3, as said below
- counts: int32 [128, 8], P('blocks'), may hold values from 1 to 3, as said below
Outputs:
- new_state: float32 [128, 8, 3, 5, 4096], P('blocks', 'sub')
Inputs may be any that keep to these rules, and one draw needn't show every extreme that they name: `counts`: A device's live blocks are its slots 0 to count - 1; some device holds 3 blocks and some hold one. `neighbours`: component 0 is 0, 1 or 2 for a neighbour block on the device at blocks index - 1, the same, or + 1 (same sub index), and 3 for a face on the domain's boundary; component 1 is then a live slot of that device, and 0 on the boundary. Entries of slots that are not live follow the same rule. No entry points past either end of the blocks axis. Every slot holds a physical state: density and pressure (heat ratio 1.4) lie in [0.4, 2.5], each velocity component in [-1, 1].
All inputs are finite; a program needn't handle non-finite values.
Results may differ from a plain program's by a relative error of at most 0.0003.
Values sent between devices are 32-bit elements; how exact they have to be, the bound alone decides.
No kernel may reach another device: no remote copies, remote signals or barrier semaphores. Data moves between devices by JAX's collectives and lax.ppermute only.
A program may use at most 32 MiB of HBM per device.

v0:
```python
import jax
import jax.numpy as jnp
from jax import lax
from jax.sharding import PartitionSpec as P

EDGE = 16
FIELDS = 5
SLOTS = 3
MOVE = 1


heat_ratio = 1.4
courant = 0.07


def from_partner(value, axis, bit):
    mask = 2**bit
    pairs = [(source, source ^ mask) for source in range(lax.axis_size(axis))]
    return lax.ppermute(value, axis, pairs)


def with_halo(block, sides, width):
    for axis, dim in sides:
        count = lax.axis_size(axis)
        forward = [(i, i + 1) for i in range(count - 1)]
        backward = [(target, source) for source, target in forward]
        low = lax.ppermute(
            lax.slice_in_dim(block, block.shape[dim] - width, None, axis=dim), axis, forward
        )
        high = lax.ppermute(lax.slice_in_dim(block, 0, width, axis=dim), axis, backward)
        block = jnp.concatenate([low, block, high], axis=dim)
    return block


def block_faces(block):
    block_cube = block.reshape(FIELDS, EDGE, EDGE, EDGE)
    low_x = block_cube[:, 0:2]
    high_x = block_cube[:, EDGE - 2 :][:, ::-1]
    low_y = jnp.transpose(block_cube[:, :, 0:2], (0, 2, 1, 3))
    high_y = jnp.transpose(block_cube[:, :, EDGE - 2 :][:, :, ::-1], (0, 2, 1, 3))
    low_z = jnp.transpose(block_cube[:, :, :, 0:2], (0, 3, 1, 2))
    high_z = jnp.transpose(block_cube[:, :, :, EDGE - 2 :][:, :, :, ::-1], (0, 3, 1, 2))
    face_layers = jnp.stack([low_x, high_x, low_y, high_y, low_z, high_z], axis=0)
    return face_layers.reshape(6, FIELDS, 2 * EDGE * EDGE)


def pick_ghosts(window, face_links, slot_total):
    owner_code = face_links[..., 0]
    source = face_links[..., 1]
    own_slot = jnp.arange(slot_total, dtype=jnp.int32)[:, None]
    face_number = jnp.arange(6, dtype=jnp.int32)[None, :]
    boundary = owner_code == 3
    device = jnp.where(boundary, 1, owner_code)
    slot_index = jnp.where(boundary, own_slot, source)
    face_side = jnp.where(boundary, face_number, face_number ^ 1)
    flat_index = (device * slot_total + slot_index) * 6 + face_side
    flattened = window.reshape(3 * slot_total * 6, FIELDS, -1)
    picked = jnp.take(flattened, flat_index.reshape(-1), axis=0)
    return picked.reshape(slot_total, 6, FIELDS, -1)


def primitives(conserved_cells):
    density = conserved_cells[0]
    velocity = conserved_cells[1:4] / density
    pressure = (heat_ratio - 1.0) * (
        conserved_cells[4] - 0.5 * density * jnp.sum(velocity * velocity, axis=0)
    )
    return jnp.concatenate([density[None], velocity, pressure[None]], axis=0)


def side_terms(prim, component):
    density = prim[0]
    pressure = prim[4]
    normal = prim[component]
    kinetic = 0.5 * density * (prim[1] * prim[1] + prim[2] * prim[2] + prim[3] * prim[3])
    energy = pressure / (heat_ratio - 1.0) + kinetic
    sound = jnp.sqrt(heat_ratio * pressure / density)
    conserved_list = [density, density * prim[1], density * prim[2], density * prim[3], energy]
    flux_list = [value * normal for value in conserved_list]
    flux_list[component] = flux_list[component] + pressure
    flux_list[4] = flux_list[4] + pressure * normal
    return (normal, sound, conserved_list, flux_list)


def hll_flux(left_state, right_state, component):
    speed_left, sound_left, cons_left, flux_left = side_terms(left_state, component)
    speed_right, sound_right, cons_right, flux_right = side_terms(right_state, component)
    slow_speed = jnp.minimum(jnp.minimum(speed_left - sound_left, speed_right - sound_right), 0.0)
    fast_speed = jnp.maximum(jnp.maximum(speed_left + sound_left, speed_right + sound_right), 0.0)
    spread = fast_speed - slow_speed
    product = slow_speed * fast_speed
    outputs = [
        (
            fast_speed * flux_left[number]
            - slow_speed * flux_right[number]
            + product * (cons_right[number] - cons_left[number])
        )
        / spread
        for number in range(5)
    ]
    return jnp.stack(outputs, axis=0)


def cut_along(values, first_cell, last_cell, along):
    return lax.slice_in_dim(values, first_cell, last_cell, axis=along)


def minmod(first_diff, second_diff):
    smaller = jnp.where(jnp.abs(first_diff) < jnp.abs(second_diff), first_diff, second_diff)
    return jnp.where(first_diff * second_diff > 0, smaller, 0.0)


def line_change(prim, along, stride, component):
    length = prim.shape[along]
    differences = cut_along(prim, stride, length, along) - cut_along(
        prim, 0, length - stride, along
    )
    diff_length = differences.shape[along]
    slopes = minmod(
        cut_along(differences, 0, diff_length - stride, along),
        cut_along(differences, stride, diff_length, along),
    )
    centres = cut_along(prim, stride, length - stride, along)
    left_state = cut_along(centres + 0.5 * slopes, 0, (EDGE + 1) * stride, along)
    right_state = cut_along(centres - 0.5 * slopes, stride, (EDGE + 2) * stride, along)
    fluxes = hll_flux(left_state, right_state, component)
    return cut_along(fluxes, stride, (EDGE + 1) * stride, along) - cut_along(
        fluxes, 0, EDGE * stride, along
    )


def lane_swap(values):
    return jnp.transpose(values.reshape(FIELDS, EDGE, EDGE, EDGE), (0, 1, 3, 2)).reshape(
        FIELDS, EDGE, EDGE * EDGE
    )


def update_block(block, ghosts):
    plane = block.reshape(FIELDS, EDGE, EDGE * EDGE)
    prim_plane = primitives(plane)
    ghost_prim = primitives(jnp.transpose(ghosts, (1, 0, 2)))
    shaped = jnp.transpose(ghost_prim.reshape(FIELDS, 6, 2, EDGE * EDGE), (1, 0, 2, 3))
    padded = jnp.concatenate(
        [shaped[0][:, 1:2], shaped[0][:, 0:1], prim_plane, shaped[1][:, 0:1], shaped[1][:, 1:2]],
        axis=1,
    )
    change = line_change(padded, 1, 1, 1)
    lower_side = shaped[2].reshape(FIELDS, 2, EDGE, EDGE)
    upper_side = shaped[3].reshape(FIELDS, 2, EDGE, EDGE)
    padded = jnp.concatenate(
        [lower_side[:, 1], lower_side[:, 0], prim_plane, upper_side[:, 0], upper_side[:, 1]], axis=2
    )
    change = change + line_change(padded, 2, EDGE, 2)
    lower_side = shaped[4].reshape(FIELDS, 2, EDGE, EDGE)
    upper_side = shaped[5].reshape(FIELDS, 2, EDGE, EDGE)
    padded = jnp.concatenate(
        [
            lower_side[:, 1],
            lower_side[:, 0],
            lane_swap(prim_plane),
            upper_side[:, 0],
            upper_side[:, 1],
        ],
        axis=2,
    )
    change = change + lane_swap(line_change(padded, 2, EDGE, 3))
    return (plane - courant * change).reshape(FIELDS, -1)


def update_live(blocks, ghosts, live_count):
    fresh = jax.vmap(update_block)(blocks, ghosts)
    live_mask = jnp.arange(blocks.shape[0], dtype=jnp.int32) < live_count
    return jnp.where(live_mask[:, None, None], fresh, jnp.zeros_like(fresh))


def send_blocks(buffers, bit_number):
    return (from_partner(buffers[0], "sub", bit_number),)


def rebalance(members, row_counts, sub_index, rounds, sender):
    positions = jnp.arange(row_counts.shape[0], dtype=jnp.int32)
    slot_range = jnp.arange(SLOTS, dtype=jnp.int32)
    counts_now = row_counts
    for bit_number in range(rounds):
        partner = positions ^ 1 << bit_number
        theirs_all = counts_now[partner]
        own_count = counts_now[sub_index]
        theirs = theirs_all[sub_index]
        handed = jnp.where(own_count > theirs, (own_count - theirs) // 2, 0)
        taken = jnp.where(theirs > own_count, (theirs - own_count) // 2, 0)
        outgoing = jnp.clip(own_count - handed + jnp.arange(MOVE, dtype=jnp.int32), 0, SLOTS - 1)
        buffers = tuple((jnp.take(member, outgoing, axis=0) for member in members))
        arrived = sender(buffers, bit_number)
        incoming = (slot_range >= own_count) & (slot_range < own_count + taken)
        source = jnp.clip(slot_range - own_count, 0, MOVE - 1)
        members = tuple(
            (
                jnp.where(
                    incoming.reshape((SLOTS,) + (1,) * (member.ndim - 1)),
                    jnp.take(received, source, axis=0),
                    member,
                )
                for member, received in zip(members, arrived)
            )
        )
        handed_all = jnp.where(counts_now > theirs_all, (counts_now - theirs_all) // 2, 0)
        taken_all = jnp.where(theirs_all > counts_now, (theirs_all - counts_now) // 2, 0)
        counts_now = counts_now - handed_all + taken_all
    return (members, counts_now[sub_index])


def body(state, neighbours, counts):
    blocks = state[0, 0]
    face_links = neighbours[0, 0]
    row_counts = counts[0]
    sub_index = lax.axis_index("sub")
    face_layers = jax.vmap(block_faces)(blocks)
    window = with_halo(face_layers[None], (("blocks", 0),), 1)
    ghosts = pick_ghosts(window, face_links, SLOTS)
    own_count = row_counts[sub_index]
    rounds = lax.axis_size("sub").bit_length() - 1
    updated_blocks = update_live(blocks, ghosts, own_count)
    moved_items, final_count = rebalance(
        (updated_blocks,), row_counts, sub_index, rounds, send_blocks
    )
    result = moved_items[0]
    live_mask = jnp.arange(SLOTS, dtype=jnp.int32) < final_count
    result = jnp.where(live_mask[:, None, None], result, jnp.zeros_like(result))
    return result[None, None]


def solution(mesh):
    return jax.shard_map(
        body,
        mesh=mesh,
        in_specs=(
            P("blocks", "sub", None, None, None),
            P("blocks", "sub", None, None, None),
            P("blocks", None),
        ),
        out_specs=P("blocks", "sub", None, None, None),
        check_vma=False,
    )
```

profile of v0, /device:TPU:112, one launch (start us, length us, event | category | flops | bytes accessed | tf_op | source)
XLA Modules:
  0.0 115.4 jit_solution(5623431105327625005)
XLA Ops:
  0.0 1.5 %reduce = f32[3,5,4096]{2,1,0:T(8,128)S(1)} reduce(f32[1,1,3,5,4096]{4,1,3,2,0:T(1,128)} %param.7, f32[]{:T(128)} %constant.229), dimensions={0,1}, to_apply=%param.7.reduce_sub_computation | reduce | bytes 491524 | tf_op args[0]
  1.5 0.7 reshape_squeeze.7
  2.2 0.8 fusion.10
  3.0 1.0 fusion.49
  4.0 2.6 %fusion.48 = (f32[3,5,16,16,2]{4,3,2,1,0:T(8,128)}, f32[3,5,16,16,2]{4,3,2,1,0:T(8,128)}) fusion(f32[3,5,16,16,16]{4,3,2,1,0:T(8,128)S(1)} %reshape_squeeze.7), kind=kLoop, calls=%fused_computation.239 | loop fusion | bytes 122880 | tf_op jit(solution)/shard_map/vmap()/slice | solution.py:42
  6.6 3.1 %copy.153 = f32[3,5,16,16,2]{3,2,4,1,0:T(8,128)S(1)} copy(f32[3,5,16,16,2]{4,3,2,1,0:T(8,128)} %get-tuple-element.40) | data formatting | bytes 61440
  9.8 1.5 %copy.154 = f32[3,5,16,16,2]{3,2,4,1,0:T(8,128)S(1)} copy(f32[3,5,16,16,2]{4,3,2,1,0:T(8,128)S(1)} %copy-done.2) | data formatting | bytes 61440
  11.3 0.8 bitcast_dynamic-update-slice_fusion.3
  12.1 1.7 %fusion.11 = f32[6,3,5,2,16,16]{5,4,3,0,2,1:T(8,128)} fusion(f32[6,3,5,2,16,16]{5,4,3,0,2,1:T(8,128)} %bitcast_dynamic-update-slice_fusion.3, f32[3,5,16,2,16]{4,3,2,1,0:T(2,128)} %get-tuple-element.42), kind=kLoop, calls=%fused_computation.45 | loop fusion | bytes 491520
  13.7 0.7 bitcast_dynamic-update-slice_fusion.2
  14.5 0.7 bitcast_dynamic-update-slice_fusion.1
  15.2 0.7 bitcast_dynamic-update-slice_fusion
  15.9 2.9 %reshape.2309 = f32[1,3,6,5,512]{4,2,3,1,0:T(8,128)} reshape(f32[3,6,5,2,16,16]{5,4,3,1,2,0:T(8,128)} %bitcast.578) | data formatting | bytes 368640 | tf_op jit(solution)/shard_map/broadcast_in_dim;vmap()/reshape | solution.py:218
  18.8 2.0 %collective-permute-start = (f32[1,3,6,5,512]{4,2,3,1,0:T(8,128)}, f32[1,3,6,5,512]{4,2,3,1,0:T(8,128)}, u32[]{:S(2)}, u32[]{:S(2)}) collective-permute-start(f32[1,3,6,5,512]{4,2,3,1,0:T(8,128)} %reshape.2309), channel_id=1, source_target_pairs={{0,8},{8,16},{16,24},{24,32},{32,40},{40,48},{48,56},{56,64},{64,7... | collective-permute-start | bytes 552968 | tf_op jit(solution)/shard_map/ppermute | solution.py:27
  20.9 17.6 %collective-permute-start.1 = (f32[1,3,6,5,512]{4,2,3,1,0:T(8,128)}, f32[1,3,6,5,512]{4,2,3,1,0:T(8,128)}, u32[]{:S(2)}, u32[]{:S(2)}) collective-permute-start(f32[1,3,6,5,512]{4,2,3,1,0:T(8,128)} %reshape.2309), channel_id=1, source_target_pairs={{8,0},{16,8},{24,16},{32,24},{40,32},{48,40},{56,48},{64,56},{72,6... | collective-permute-start | bytes 552968 | tf_op jit(solution)/shard_map/ppermute | solution.py:30
  38.7 0.7 constant_dynamic-slice_fusion
  39.3 0.7 iota_compare_fusion
  40.0 0.6 gather_fusion
  40.7 0.6 dynamic_slice.28
  46.5 1.2 %minimum_compare_fusion.2 = pred[3]{0:T(512)(128)(4,1)} fusion(s32[]{:T(128)} %bitcast.13), kind=kLoop, calls=%fused_computation.225 | loop fusion | flops 12 | bytes 7 | tf_op jit(solution)/shard_map/jit(_take)/le | solution.py:200
  47.6 0.6 dynamic_slice.25
  48.2 0.6 gather_fusion.1
  48.9 0.6 dynamic_slice.26
  55.5 1.1 minimum_compare_fusion.1
  56.7 0.6 dynamic_slice.23
  57.3 0.6 gather_fusion.2
  58.0 0.6 dynamic_slice.24
  64.2 0.5 fusion.38
  64.7 1.2 %minimum_compare_fusion = pred[3]{0:T(512)(128)(4,1)} fusion(s32[]{:T(128)} %bitcast.5), kind=kLoop, calls=%fused_computation.223 | loop fusion | flops 12 | bytes 7 | tf_op jit(solution)/shard_map/jit(_take)/le | solution.py:200
  66.6 0.9 copy.131
  67.7 0.9 copy.133
  68.6 0.4 concatenate.65
  69.0 0.4 copy.132
  69.3 1.3 %maximum_bitcast_fusion = f32[3,5,16,16,16]{4,3,2,0,1:T(8,128)S(1)} fusion(f32[3,1,16,16,16]{3,4,2,0,1:T(8,128)} %copy.133, f32[3,3,16,16,16]{3,4,2,0,1:T(8,128)S(1)} %copy.132, f32[3,1,16,16,16]{3,4,2,0,1:T(8,128)} %copy.131), kind=kLoop, calls=%fused_computation.4 | loop fusion | flops 122880 | bytes 491520 | tf_op jit(solution)/shard_map/vmap()/transpose | solution.py:133
  70.7 0.9 reshape.2311
  72.2 1.3 %compare_and_fusion.1 = pred[3]{0:T(512)(128)(4,1)} fusion(s32[]{:T(128)S(6)} %add.757, s32[]{:T(128)} %bitcast.13), kind=kLoop, calls=%fused_computation.173 | loop fusion | flops 9 | bytes 11 | tf_op jit(solution)/shard_map/and | solution.py:194
  74.8 0.6 dynamic_slice.22
  75.4 1.3 %pad_maximum_fusion = f32[3,3,6,5,512]{4,2,3,1,0:T(8,128)S(1)} fusion(f32[1,3,6,5,512]{4,2,3,1,0:T(8,128)} %collective-permute-done.1, f32[1,3,6,5,512]{4,2,3,1,0:T(8,128)} %reshape.2309, f32[1,3,6,5,512]{4,2,3,1,0:T(8,128)} %collective-permute-done), kind=kLoop, calls=%fused_computation.5 | loop fusion | flops 276480 | bytes 1105920 | tf_op jit(solution)/shard_map/concatenate | solution.py:31
  76.6 0.3 copy.143
  77.0 0.6 gather_fusion.3
  79.3 0.4 maximum_subtract_fusion
  79.7 0.3 fusion.15
  80.0 0.2 divide_dynamic-update-slice_fusion.7
  80.6 0.2 fusion.24
  80.8 0.7 copy-done.7
  81.9 0.4 maximum_subtract_fusion.1
  82.3 0.3 fusion.13
  83.2 0.2 fusion.20
  83.5 0.6 reshape.2312
  84.1 1.8 %copy.140 = f32[3,5,16,16,16]{3,4,2,0,1:T(8,128)} copy(f32[3,5,16,16,16]{4,3,2,0,1:T(8,128)S(1)} %reshape.2312) | data formatting | bytes 491520 | tf_op jit(solution)/shard_map/vmap()/reshape | solution.py:133
  85.9 2.5 %reshape.2313 = f32[3,5,16,256]{3,2,0,1:T(8,128)S(1)} reshape(f32[3,5,16,16,16]{4,3,2,0,1:T(8,128)} %bitcast.574) | data formatting | bytes 491520 | tf_op jit(solution)/shard_map/vmap()/reshape | solution.py:133
  89.0 3.4 %collective-permute-start.2 = (f32[1,5,4096]{2,0,1:T(1,128)S(1)}, f32[1,5,4096]{2,0,1:T(1,128)S(1)}, u32[]{:S(2)}, u32[]{:S(2)}) collective-permute-start(f32[1,5,4096]{2,0,1:T(1,128)S(1)} %broadcast_select_fusion.3), channel_id=1, source_target_pairs={{0,1},{1,0},{2,3},{3,2},{4,5},{5,4},{6,7},{7,6},{8,9},{9,8},{10,11... | collective-permute-start | bytes 245768 | tf_op jit(solution)/shard_map/ppermute | solution.py:19
  92.4 0.6 compare_and_fusion.2
  93.0 2.3 %collective-permute-done.2 = f32[1,5,4096]{2,0,1:T(1,128)S(1)} collective-permute-done((f32[1,5,4096]{2,0,1:T(1,128)S(1)}, f32[1,5,4096]{2,0,1:T(1,128)S(1)}, u32[]{:S(2)}, u32[]{:S(2)}) %collective-permute-start.2) | collective-permute-done | bytes 81952 | tf_op jit(solution)/shard_map/ppermute | solution.py:19
  95.4 0.2 select_select_fusion.2
  95.6 4.3 %collective-permute-start.3 = (f32[1,5,4096]{2,0,1:T(1,128)S(1)}, f32[1,5,4096]{2,0,1:T(1,128)S(1)}, u32[]{:S(2)}, u32[]{:S(2)}) collective-permute-start(f32[1,5,4096]{2,0,1:T(1,128)S(1)} %broadcast_select_fusion.2), channel_id=1, source_target_pairs={{0,2},{1,3},{2,0},{3,1},{4,6},{5,7},{6,4},{7,5},{8,10},{9,11},{10,... | collective-permute-start | bytes 245768 | tf_op jit(solution)/shard_map/ppermute | solution.py:19
  100.0 0.6 compare_and_fusion.3
  100.6 2.3 %collective-permute-done.3 = f32[1,5,4096]{2,0,1:T(1,128)S(1)} collective-permute-done((f32[1,5,4096]{2,0,1:T(1,128)S(1)}, f32[1,5,4096]{2,0,1:T(1,128)S(1)}, u32[]{:S(2)}, u32[]{:S(2)}) %collective-permute-start.3) | collective-permute-done | bytes 81952 | tf_op jit(solution)/shard_map/ppermute | solution.py:19
  102.9 0.2 select_select_fusion.1
  103.3 8.3 %collective-permute-start.4 = (f32[1,5,4096]{2,0,1:T(1,128)S(1)}, f32[1,5,4096]{2,0,1:T(1,128)S(1)}, u32[]{:S(2)}, u32[]{:S(2)}) collective-permute-start(f32[1,5,4096]{2,0,1:T(1,128)S(1)} %broadcast_select_fusion.1), channel_id=1, source_target_pairs={{0,4},{1,5},{2,6},{3,7},{4,0},{5,1},{6,2},{7,3},{8,12},{9,13},{10,... | collective-permute-start | bytes 245768 | tf_op jit(solution)/shard_map/ppermute | solution.py:19
  111.6 0.6 iota_compare_fusion.1
  112.1 1.9 %collective-permute-done.4 = f32[1,5,4096]{2,0,1:T(1,128)S(1)} collective-permute-done((f32[1,5,4096]{2,0,1:T(1,128)S(1)}, f32[1,5,4096]{2,0,1:T(1,128)S(1)}, u32[]{:S(2)}, u32[]{:S(2)}) %collective-permute-start.4) | collective-permute-done | bytes 81952 | tf_op jit(solution)/shard_map/ppermute | solution.py:19
  114.1 0.3 fusion.3
  114.4 0.9 copy.142
  (109 shorter events, 4.9 us)
Async XLA Ops:
  2.2 4.4 %copy-start.1 = (f32[3,5,16,16,16]{4,3,2,1,0:T(8,128)}, f32[3,5,16,16,16]{4,3,2,1,0:T(8,128)S(1)}, u32[]{:S(2)}) copy-start(f32[3,5,16,16,16]{4,3,2,1,0:T(8,128)S(1)} %reshape_squeeze.7) | copy-start | bytes 737284
  6.6 3.2 %copy-start.2 = (f32[3,5,16,16,2]{4,3,2,1,0:T(8,128)S(1)}, f32[3,5,16,16,2]{4,3,2,1,0:T(8,128)}, u32[]{:S(2)}) copy-start(f32[3,5,16,16,2]{4,3,2,1,0:T(8,128)} %get-tuple-element.39) | copy-start | bytes 92164
  9.8 1.5 %slice-start = ((f32[3,5,16,16,16]{4,3,2,1,0:T(8,128)}), f32[3,5,2,16,16]{4,3,2,1,0:T(8,128)S(1)}, s32[]{:S(2)}) async-start(f32[3,5,16,16,16]{4,3,2,1,0:T(8,128)} %copy-done.1), calls=%async_computation | async-start | bytes 491520 | tf_op jit(solution)/shard_map/vmap()/slice | solution.py:38
  15.2 23.5 %copy-start = (s32[1,8]{1,0:T(1,128)S(1)}, s32[1,8]{1,0:T(1,128)}, u32[]{:S(2)}) copy-start(s32[1,8]{1,0:T(1,128)} %param.9) | copy-start | bytes 100
  18.8 47.1 %copy-start.11 = (s32[1,1,3,6,2]{3,4,2,1,0:T(2,128)S(1)}, s32[1,1,3,6,2]{3,4,2,1,0:T(2,128)}, u32[]{:S(2)}) copy-start(s32[1,1,3,6,2]{3,4,2,1,0:T(2,128)} %param.8) | copy-start | bytes 436
  18.8 56.5 %collective-permute-start = (f32[1,3,6,5,512]{4,2,3,1,0:T(8,128)}, f32[1,3,6,5,512]{4,2,3,1,0:T(8,128)}, u32[]{:S(2)}, u32[]{:S(2)}) collective-permute-start(f32[1,3,6,5,512]{4,2,3,1,0:T(8,128)} %reshape.2309), channel_id=1, source_target_pairs={{0,8},{8,16},{16,24},{24,32},{32,40},{40,48},{48,56},{56,64},{64,7... | collective-permute-start | bytes 552968 | tf_op jit(solution)/shard_map/ppermute | solution.py:27
  20.9 54.5 %collective-permute-start.1 = (f32[1,3,6,5,512]{4,2,3,1,0:T(8,128)}, f32[1,3,6,5,512]{4,2,3,1,0:T(8,128)}, u32[]{:S(2)}, u32[]{:S(2)}) collective-permute-start(f32[1,3,6,5,512]{4,2,3,1,0:T(8,128)} %reshape.2309), channel_id=1, source_target_pairs={{8,0},{16,8},{24,16},{32,24},{40,32},{48,40},{56,48},{64,56},{72,6... | collective-permute-start | bytes 552968 | tf_op jit(solution)/shard_map/ppermute | solution.py:30
  38.5 27.9 %copy-start.13 = (s32[6]{0:T(128)}, s32[6]{0:T(128)S(1)}, u32[]{:S(2)}) copy-start(s32[6]{0:T(128)S(1)} %iota_xor_fusion) | copy-start | bytes 76
  66.4 2.2 %copy-start.3 = (f32[3,1,16,256]{3,2,0,1:T(8,128)}, f32[3,1,16,256]{3,2,0,1:T(8,128)S(1)}, u32[]{:S(2)}) copy-start(f32[3,1,16,256]{3,2,0,1:T(8,128)S(1)} %get-tuple-element.59) | copy-start | bytes 147460
  66.4 2.2 %copy-start.5 = (f32[3,1,16,256]{3,2,0,1:T(8,128)}, f32[3,1,16,256]{3,2,0,1:T(8,128)S(1)}, u32[]{:S(2)}) copy-start(f32[3,1,16,256]{3,2,0,1:T(8,128)S(1)} %get-tuple-element.60) | copy-start | bytes 147460
  70.7 4.1 %copy-start.16 = (s32[8]{0:T(128)S(1)}, s32[8]{0:T(128)}, u32[]{:S(2)}) copy-start(s32[8]{0:T(128)} %fusion.38) | copy-start | bytes 100
  70.7 4.7 %copy-start.14 = (s32[6]{0:T(128)S(1)}, s32[6]{0:T(128)}, u32[]{:S(2)}) copy-start(s32[6]{0:T(128)} %copy-done.13) | copy-start | bytes 76
  77.0 1.1 copy-start.4
  77.0 1.1 copy-start.6
  80.8 0.7 copy-start.7
  85.9 2.5 %copy-start.8 = (f32[5,3,16,272]{3,2,1,0:T(8,128)S(1)}, f32[5,3,16,272]{3,2,1,0:T(8,128)}, u32[]{:S(2)}) copy-start(f32[5,3,16,272]{3,2,1,0:T(8,128)} %copy-done.7) | copy-start | bytes 783364
  88.4 7.0 %copy-start.9 = (pred[3]{0:T(512)(128)(4,1)S(1)}, pred[3]{0:T(512)(128)(4,1)}, u32[]{:S(2)}) copy-start(pred[3]{0:T(512)(128)(4,1)} %minimum_compare_fusion.2) | copy-start | bytes 13
  88.4 7.0 %copy-start.10 = (pred[3]{0:T(512)(128)(4,1)S(1)}, pred[3]{0:T(512)(128)(4,1)}, u32[]{:S(2)}) copy-start(pred[3]{0:T(512)(128)(4,1)} %compare_and_fusion.1) | copy-start | bytes 13
  88.6 14.4 %copy-start.12 = (pred[3]{0:T(512)(128)(4,1)S(1)}, pred[3]{0:T(512)(128)(4,1)}, u32[]{:S(2)}) copy-start(pred[3]{0:T(512)(128)(4,1)} %minimum_compare_fusion.1) | copy-start | bytes 13
  88.8 25.3 %copy-start.15 = (pred[3]{0:T(512)(128)(4,1)S(1)}, pred[3]{0:T(512)(128)(4,1)}, u32[]{:S(2)}) copy-start(pred[3]{0:T(512)(128)(4,1)} %minimum_compare_fusion) | copy-start | bytes 13
  89.0 6.3 %collective-permute-start.2 = (f32[1,5,4096]{2,0,1:T(1,128)S(1)}, f32[1,5,4096]{2,0,1:T(1,128)S(1)}, u32[]{:S(2)}, u32[]{:S(2)}) collective-permute-start(f32[1,5,4096]{2,0,1:T(1,128)S(1)} %broadcast_select_fusion.3), channel_id=1, source_target_pairs={{0,1},{1,0},{2,3},{3,2},{4,5},{5,4},{6,7},{7,6},{8,9},{9,8},{10,11... | collective-permute-start | bytes 245768 | tf_op jit(solution)/shard_map/ppermute | solution.py:19
  95.6 7.2 %collective-permute-start.3 = (f32[1,5,4096]{2,0,1:T(1,128)S(1)}, f32[1,5,4096]{2,0,1:T(1,128)S(1)}, u32[]{:S(2)}, u32[]{:S(2)}) collective-permute-start(f32[1,5,4096]{2,0,1:T(1,128)S(1)} %broadcast_select_fusion.2), channel_id=1, source_target_pairs={{0,2},{1,3},{2,0},{3,1},{4,6},{5,7},{6,4},{7,5},{8,10},{9,11},{10,... | collective-permute-start | bytes 245768 | tf_op jit(solution)/shard_map/ppermute | solution.py:19
  103.3 10.8 %collective-permute-start.4 = (f32[1,5,4096]{2,0,1:T(1,128)S(1)}, f32[1,5,4096]{2,0,1:T(1,128)S(1)}, u32[]{:S(2)}, u32[]{:S(2)}) collective-permute-start(f32[1,5,4096]{2,0,1:T(1,128)S(1)} %broadcast_select_fusion.1), channel_id=1, source_target_pairs={{0,4},{1,5},{2,6},{3,7},{4,0},{5,1},{6,2},{7,3},{8,12},{9,13},{10,... | collective-permute-start | bytes 245768 | tf_op jit(solution)/shard_map/ppermute | solution.py:19
where the time goes:
time: 117 us; the launch traced here: 115 us
  local copies, waits for them, and re-layouts  36.4 us (31%)
  starting transfers between devices  35.6 us (30%)
  between operations  19.6 us (17%)
  other arithmetic  17.2 us (15%)
  waiting for transfers between devices  6.52 us (6%)
    ppermute x1, starting transfers between devices, with_halo(): lax.ppermute(lax.slice_in_dim(block, 0, width, axis=dim), axis, backward)  17.6 us
    ppermute x3, starting transfers between devices, from_partner(): return lax.ppermute(value, axis, pairs)  16 us
    unnamed x45, local copies, waits for them, and re-layouts  10.3 us
    ppermute x3, waiting for transfers between devices, from_partner(): return lax.ppermute(value, axis, pairs)  6.51 us
    le x3, other arithmetic, rebalance(): jnp.take(received, source, axis=0)  3.46 us
    reshape x2, local copies, waits for them, and re-layouts, lane_swap(): jnp.transpose(values.reshape(FIELDS, EDGE, EDGE, EDGE), (0, 1, 3, 2))  3.31 us
    unnamed x13, other arithmetic  3.02 us
    concatenate x9, local copies, waits for them, and re-layouts, primitives(): return jnp.concatenate([density[None], velocity, pressure[None]], axis=0)  3 us
  transfers between devices with their start and end apart: 5, of which 3 were waited for; matrix products, arithmetic and copies ran while one was open for 17% of the time, Pallas kernels for 0%

commit v1 on v0

v1 whole, which is shorter than its diff:
```python
import functools

import jax
import jax.numpy as jnp
from jax import lax
from jax.experimental import pallas as pl
from jax.experimental.pallas import tpu as pltpu
from jax.sharding import PartitionSpec as P

EDGE = 16
FIELDS = 5
SLOTS = 3
LANES = 128
ROWS = 2 * SLOTS
CHUNKS = 32
FACE_ROWS = 6 * 2 * FIELDS * ROWS

heat_ratio = 1.4
courant = 0.07

VMEM_LIMIT = 48 * 1024 * 1024


def swap_chunks(planes, width, lane):
    planes = list(planes)
    step = 1
    while step < len(planes):
        upper = (lane & (step * width)) != 0
        for low in range(len(planes)):
            if low & step:
                continue
            a, b = planes[low], planes[low + step]
            planes[low] = jnp.where(upper, pltpu.roll(b, step * width, 1), a)
            planes[low + step] = jnp.where(upper, b, pltpu.roll(a, LANES - step * width, 1))
        step *= 2
    return planes


def swap_halves(planes, row):
    odd = (row & 1) != 0
    half = len(planes) // 2
    first = [jnp.where(odd, pltpu.roll(b, 1, 0), a) for a, b in zip(planes[:half], planes[half:])]
    second = [jnp.where(odd, b, pltpu.roll(a, 7, 0)) for a, b in zip(planes[:half], planes[half:])]
    return first + second


def tile_iotas():
    return (
        lax.broadcasted_iota(jnp.int32, (8, LANES), 1),
        lax.broadcasted_iota(jnp.int32, (8, LANES), 0),
    )


def x_to_y(planes, lane, row):
    planes = swap_chunks(planes[:8], EDGE, lane) + swap_chunks(planes[8:], EDGE, lane)
    return swap_halves(planes, row)


def y_to_x(planes, lane, row):
    planes = swap_halves(planes, row)
    return swap_chunks(planes[:8], EDGE, lane) + swap_chunks(planes[8:], EDGE, lane)


def prepare_kernel(state, planes, faces, work):
    for slot in range(SLOTS):
        for chunk in range(CHUNKS):
            base = (chunk // 2) * FIELDS * 8 + 2 * slot + chunk % 2
            work[pl.ds(base, FIELDS, stride=8), :] = state[
                0, 0, slot, :, chunk * LANES : (chunk + 1) * LANES
            ]
    for number in range(EDGE):
        base = number * FIELDS * 8
        rows = [work[base + 8 * field : base + 8 * field + 8, :] for field in range(FIELDS)]
        inverse = 1.0 / rows[0]
        v1, v2, v3 = rows[1] * inverse, rows[2] * inverse, rows[3] * inverse
        pressure = (heat_ratio - 1.0) * (
            rows[4] - 0.5 * rows[0] * (v1 * v1 + v2 * v2 + v3 * v3)
        )
        for field, value in enumerate((rows[0], v1, v2, v3, pressure)):
            planes[0, number, field] = value

    lane, row = tile_iotas()

    def one_field(field, carry):
        x_planes = [planes[0, number, field] for number in range(EDGE)]
        y_planes = x_to_y(x_planes, lane, row)
        for number in range(EDGE):
            planes[1, number, field] = y_planes[number]
        z_planes = swap_chunks(y_planes, 1, lane)
        for number in range(EDGE):
            planes[2, number, field] = z_planes[number]
        return carry

    lax.fori_loop(0, FIELDS, one_field, 0)

    for axis in range(3):
        for side in range(2):
            for depth in range(2):
                number = depth if side == 0 else EDGE - 1 - depth
                for field in range(FIELDS):
                    base = (((2 * axis + side) * 2 + depth) * FIELDS + field) * ROWS
                    faces[base : base + ROWS, :] = planes[axis, number, field, 0:ROWS, :]


def prepare(state):
    return pl.pallas_call(
        prepare_kernel,
        out_shape=(
            jax.ShapeDtypeStruct((3, EDGE, FIELDS, 8, LANES), jnp.float32),
            jax.ShapeDtypeStruct((FACE_ROWS, LANES), jnp.float32),
        ),
        scratch_shapes=[pltpu.VMEM((EDGE * FIELDS * 8, LANES), jnp.float32)],
        compiler_params=pltpu.CompilerParams(vmem_limit_bytes=VMEM_LIMIT),
        name="prepare",
    )(state)


def minmod(first, second):
    return jnp.maximum(jnp.minimum(first, second), 0.0) + jnp.minimum(
        jnp.maximum(first, second), 0.0
    )


def side_speeds(prim, component):
    scaled = heat_ratio * prim[4]
    sound = scaled * lax.rsqrt(scaled * prim[0])
    return prim[component] - sound, prim[component] + sound


def hll_flux(left, right, component):
    slow_left, fast_left = side_speeds(left, component)
    slow_right, fast_right = side_speeds(right, component)
    slow = jnp.minimum(jnp.minimum(slow_left, slow_right), 0.0)
    fast = jnp.maximum(jnp.maximum(fast_left, fast_right), 0.0)
    inverse = 1.0 / (fast - slow)
    weight_left = fast * inverse
    weight_right = -slow * inverse
    product = slow * weight_left
    normal_left, normal_right = left[component], right[component]
    carry_left = weight_left * normal_left - product
    carry_right = weight_right * normal_right + product
    mass_left, mass_right = carry_left * left[0], carry_right * right[0]
    push_left, push_right = weight_left * left[4], weight_right * right[4]
    outputs = [mass_left + mass_right]
    for number in (1, 2, 3):
        value = mass_left * left[number] + mass_right * right[number]
        if number == component:
            value = value + (push_left + push_right)
        outputs.append(value)
    square_left = left[1] * left[1] + left[2] * left[2] + left[3] * left[3]
    square_right = right[1] * right[1] + right[2] * right[2] + right[3] * right[3]
    inner = 1.0 / (heat_ratio - 1.0)
    energy = 0.5 * (mass_left * square_left + mass_right * square_right)
    energy = energy + inner * (carry_left * left[4] + carry_right * right[4])
    energy = energy + (push_left * normal_left + push_right * normal_right)
    outputs.append(energy)
    return outputs


def final_counts(counts, sub_index, rounds):
    size = counts.shape[-1]
    now = [counts[0, position] for position in range(size)]

    def own(values):
        picked = values[0]
        for position in range(1, size):
            picked = jnp.where(sub_index == position, values[position], picked)
        return picked

    start = own(now)
    arrival = jnp.int32(-1)
    for bit in range(rounds):
        gains = [
            jnp.maximum(now[p ^ (1 << bit)] - now[p], 0) // 2
            - jnp.maximum(now[p] - now[p ^ (1 << bit)], 0) // 2
            for p in range(size)
        ]
        arrival = jnp.where(own(gains) > 0, bit, arrival)
        now = [value + gain for value, gain in zip(now, gains)]
    return start, own(now), arrival


def update_kernel(
    rounds, state, planes, own_faces, low_faces, high_faces, links, counts, out, moved, ghosts, change, work
):
    sub_index = lax.axis_index("sub")
    _, last_count, _ = final_counts(counts, sub_index, rounds)

    for face in range(6):
        for slot in range(SLOTS):
            owner = links[0, 0, slot, face, 0]
            boundary = owner == 3
            source = jnp.where(boundary, slot, links[0, 0, slot, face, 1])
            side = jnp.where(boundary, face, face ^ 1)
            for half in range(2):
                base = side * (2 * FIELDS * ROWS) + 2 * source + half
                rows = pl.ds(base, 2 * FIELDS, stride=ROWS)
                values = jnp.where(
                    owner == 0,
                    low_faces[rows, :],
                    jnp.where(owner == 2, high_faces[rows, :], own_faces[rows, :]),
                )
                target = face * (2 * FIELDS * 8) + 2 * slot + half
                ghosts[pl.ds(target, 2 * FIELDS, stride=8), :] = values

    def cell(axis, number):
        if 0 <= number < EDGE:
            return [planes[axis, number, field] for field in range(FIELDS)]
        face = 2 * axis if number < 0 else 2 * axis + 1
        depth = -1 - number if number < 0 else number - EDGE
        base = face * (2 * FIELDS * 8) + depth * FIELDS * 8
        return [ghosts[base + 8 * field : base + 8 * field + 8, :] for field in range(FIELDS)]

    for axis in range(3):
        here = cell(axis, -1)
        diff = [b - a for a, b in zip(cell(axis, -2), here)]
        left, flux = None, None
        for number in range(-1, EDGE + 1):
            after = cell(axis, number + 1)
            next_diff = [b - a for a, b in zip(here, after)]
            half_slope = [0.5 * minmod(a, b) for a, b in zip(diff, next_diff)]
            if left is not None:
                right = [a - b for a, b in zip(here, half_slope)]
                next_flux = hll_flux(left, right, axis + 1)
                if flux is not None:
                    for field in range(FIELDS):
                        change[axis, number - 1, field] = next_flux[field] - flux[field]
                flux = next_flux
            left = [a + b for a, b in zip(here, half_slope)]
            here, diff = after, next_diff

    lane, row = tile_iotas()

    def one_field(field, carry):
        z_change = swap_chunks([change[2, number, field] for number in range(EDGE)], 1, lane)
        y_change = [z_change[number] + change[1, number, field] for number in range(EDGE)]
        x_change = y_to_x(y_change, lane, row)
        for number in range(EDGE):
            base = pl.multiple_of(number * FIELDS * 8 + field * 8, 8)
            work[pl.ds(base, 8), :] = x_change[number] + change[0, number, field]
        return carry

    lax.fori_loop(0, FIELDS, one_field, 0)

    for slot in range(SLOTS):
        for chunk in range(CHUNKS):
            base = (chunk // 2) * FIELDS * 8 + 2 * slot + chunk % 2
            cells = slice(chunk * LANES, (chunk + 1) * LANES)
            fresh = (
                state[0, 0, slot, :, cells]
                - courant * work[pl.ds(base, FIELDS, stride=8), :]
            )
            if slot == SLOTS - 1:
                moved[chunk * FIELDS : (chunk + 1) * FIELDS, :] = fresh
            out[0, 0, slot, :, cells] = jnp.where(slot < last_count, fresh, 0.0)


def update(state, planes, own_faces, low_faces, high_faces, links, counts, rounds):
    vmem = pl.BlockSpec(memory_space=pltpu.VMEM)
    smem = pl.BlockSpec(memory_space=pltpu.SMEM)
    return pl.pallas_call(
        functools.partial(update_kernel, rounds),
        out_shape=(
            jax.ShapeDtypeStruct(state.shape, jnp.float32),
            jax.ShapeDtypeStruct((CHUNKS * FIELDS, LANES), jnp.float32),
        ),
        in_specs=[vmem] * 5 + [smem] * 2,
        out_specs=(vmem, vmem),
        scratch_shapes=[
            pltpu.VMEM((6 * 2 * FIELDS * 8, LANES), jnp.float32),
            pltpu.VMEM((3, EDGE, FIELDS, 8, LANES), jnp.float32),
            pltpu.VMEM((EDGE * FIELDS * 8, LANES), jnp.float32),
        ],
        compiler_params=pltpu.CompilerParams(vmem_limit_bytes=VMEM_LIMIT),
        name="update",
    )(state, planes, own_faces, low_faces, high_faces, links, counts)


def place_kernel(rounds, *refs):
    arrived, (_, counts, out, block, sem) = refs[:rounds], refs[rounds:]
    sub_index = lax.axis_index("sub")
    start, _, arrival = final_counts(counts, sub_index, rounds)

    @pl.when(arrival >= 0)
    def _():
        for chunk in range(CHUNKS):
            rows = slice(chunk * FIELDS, (chunk + 1) * FIELDS)
            value = arrived[0][rows, :]
            for bit in range(1, rounds):
                value = jnp.where(arrival == bit, arrived[bit][rows, :], value)
            block[:, chunk * LANES : (chunk + 1) * LANES] = value
        copy = pltpu.make_async_copy(block, out.at[0, 0, start], sem)
        copy.start()
        copy.wait()


def place(arrived, out, counts):
    rounds = len(arrived)
    vmem = pl.BlockSpec(memory_space=pltpu.VMEM)
    smem = pl.BlockSpec(memory_space=pltpu.SMEM)
    anywhere = pl.BlockSpec(memory_space=pl.ANY)
    return pl.pallas_call(
        functools.partial(place_kernel, rounds),
        out_shape=jax.ShapeDtypeStruct(out.shape, out.dtype),
        in_specs=[vmem] * rounds + [anywhere, smem],
        out_specs=anywhere,
        scratch_shapes=[
            pltpu.VMEM((FIELDS, EDGE**3), jnp.float32),
            pltpu.SemaphoreType.DMA,
        ],
        input_output_aliases={rounds: 0},
        compiler_params=pltpu.CompilerParams(vmem_limit_bytes=VMEM_LIMIT),
        name="place",
    )(*arrived, out, counts)


def body(state, neighbours, counts):
    size = lax.axis_size("blocks")
    rounds = lax.axis_size("sub").bit_length() - 1
    planes, faces = prepare(state)
    forward = [(i, i + 1) for i in range(size - 1)]
    backward = [(i + 1, i) for i in range(size - 1)]
    low = lax.ppermute(faces, "blocks", forward)
    high = lax.ppermute(faces, "blocks", backward)
    out, moved = update(state, planes, faces, low, high, neighbours, counts, rounds)
    arrived = [
        lax.ppermute(
            moved, "sub", [(s, s ^ (1 << bit)) for s in range(lax.axis_size("sub"))]
        )
        for bit in range(rounds)
    ]
    return place(arrived, out, counts)


def solution(mesh):
    return jax.shard_map(
        body,
        mesh=mesh,
        in_specs=(
            P("blocks", "sub", None, None, None),
            P("blocks", "sub", None, None, None),
            P("blocks", None),
        ),
        out_specs=P("blocks", "sub", None, None, None),
        check_vma=False,
    )
```

time: 117 us -> 53.4 us (0.46)
  local copies, waits for them, and re-layouts: 36.4 us -> 2.17 us
  between operations: 19.6 us -> 0.09 us
  other arithmetic: 17.2 us -> 0 us
  Pallas kernels: 0 us -> 7.95 us
  waiting for transfers between devices: 6.52 us -> 10.9 us
  starting transfers between devices: 35.6 us -> 31.8 us
    unnamed x45 -> x6, local copies, waits for them, and re-layouts: 10.3 us -> 1.21 us
    reshape x7 -> x0, local copies, waits for them, and re-layouts: 9.07 us -> none  [the longest x2 3.31 us: lane_swap(): jnp.transpose(values.reshape(FIELDS, EDGE, EDGE, EDGE), (0, 1, 3, 2))]
    pallas_call x0 -> x3, Pallas kernels: none -> 7.95 us  [the longest x1 4.53 us: update(): pl.pallas_call(functools.partial(update_kernel, rounds), out_shape=(jax.S...]
    ppermute x5, waiting for transfers between devices: 6.52 us -> 10.9 us  [the longest x1 5.93 us: body(): low = lax.ppermute(faces, 'blocks', forward)]
    dynamic_slice x7 -> x0, local copies, waits for them, and re-layouts: 4.29 us -> none  [the longest x3 1.89 us: rebalance(): own_count = counts_now[sub_index]]
    ppermute x5, starting transfers between devices: 35.6 us -> 31.8 us  [the longest x1 17.4 us: body(): high = lax.ppermute(faces, 'blocks', backward)]
    slice x10 -> x0, local copies, waits for them, and re-layouts: 3.66 us -> none  [the longest x1 2.62 us: block_faces(): block_cube[:, :, :, EDGE - 2:][:, :, :, ::-1]]
    le x3 -> x0, other arithmetic: 3.46 us -> none  [rebalance(): jnp.take(received, source, axis=0)]
  transfers between devices with their start and end apart: 5 -> 5, of which waited for: 3 -> 4; matrix products, arithmetic and copies ran while one was open for 17% -> 0% of each run, Pallas kernels for 0% -> 0%
where the time goes in v1:
time: 53.4 us; the launch traced here: 52.8 us
  starting transfers between devices  31.8 us (60%)
  waiting for transfers between devices  10.9 us (20%)
  Pallas kernels  7.95 us (15%)
  local copies, waits for them, and re-layouts  2.17 us (4%)
    ppermute x1, starting transfers between devices, body(): high = lax.ppermute(faces, 'blocks', backward)  17.4 us
    ppermute x3, starting transfers between devices, body(): lax.ppermute(moved, 'sub', [(s, s ^ 1 << bit) for s in range(lax.axis_siz...  12.4 us
    ppermute x1, waiting for transfers between devices, body(): low = lax.ppermute(faces, 'blocks', forward)  5.93 us
    pallas_call x1, Pallas kernels, update(): pl.pallas_call(functools.partial(update_kernel, rounds), out_shape=(jax.S...  4.53 us
    ppermute x3, waiting for transfers between devices, body(): lax.ppermute(moved, 'sub', [(s, s ^ 1 << bit) for s in range(lax.axis_siz...  3.94 us
    pallas_call x1, Pallas kernels, prepare(): pl.pallas_call(prepare_kernel, out_shape=(jax.ShapeDtypeStruct((3, EDGE,...  2.76 us
    ppermute x1, starting transfers between devices, body(): low = lax.ppermute(faces, 'blocks', forward)  1.92 us
    unnamed x6, local copies, waits for them, and re-layouts  1.21 us
  transfers between devices with their start and end apart: 5, of which 4 were waited for; matrix products, arithmetic and copies ran while one was open for 0% of the time, Pallas kernels for 0%

profile of v1, /device:TPU:112, one launch (start us, length us, event | category | flops | bytes accessed | tf_op | source)
XLA Modules:
  0.0 52.8 jit_solution(6172318363422333043)
XLA Ops:
  0.0 1.1 %copy.6.state = f32[1,1,3,5,4096]{4,3,2,1,0:T(8,128)S(1)} copy(f32[1,1,3,5,4096]{4,1,3,2,0:T(1,128)} %param.3) | data formatting | bytes 491520 | tf_op args[0]
  1.1 0.0 copy-start.1
  1.1 2.8 %prepare.1 = (f32[3,16,5,8,128]{4,3,2,1,0:T(8,128)S(1)}, f32[360,128]{1,0:T(8,128)S(1)}) custom-call(f32[1,1,3,5,4096]{4,3,2,1,0:T(8,128)S(1)} %copy.6.state), custom_call_target="tpu_custom_call" | custom-call | tf_op jit(solution)/shard_map/prepare/pallas_call | solution.py:106
  3.9 17.4 %collective-permute-start.1 = (f32[360,128]{1,0:T(8,128)S(1)}, f32[360,128]{1,0:T(8,128)S(1)}, u32[]{:S(2)}, u32[]{:S(2)}) collective-permute-start(f32[360,128]{1,0:T(8,128)S(1)} %get-tuple-element.10.own_faces), channel_id=1, source_target_pairs={{8,0},{16,8},{24,16},{32,24},{40,32},{48,40},{56,48},{64,56},{72,6... | collective-permute-start | bytes 552968 | tf_op jit(solution)/shard_map/ppermute | solution.py:324
  21.3 1.9 %collective-permute-start = (f32[360,128]{1,0:T(8,128)S(1)}, f32[360,128]{1,0:T(8,128)S(1)}, u32[]{:S(2)}, u32[]{:S(2)}) collective-permute-start(f32[360,128]{1,0:T(8,128)S(1)} %get-tuple-element.10.own_faces), channel_id=1, source_target_pairs={{0,8},{8,16},{16,24},{24,32},{32,40},{40,48},{48,56},{56,64},{64,7... | collective-permute-start | bytes 552968 | tf_op jit(solution)/shard_map/ppermute | solution.py:323
  23.2 0.0 copy-done.1
  23.2 0.1 copy.7.links
  23.4 0.0 copy-start
  23.4 1.0 %collective-permute-done.1.high_faces = f32[360,128]{1,0:T(8,128)S(1)} collective-permute-done((f32[360,128]{1,0:T(8,128)S(1)}, f32[360,128]{1,0:T(8,128)S(1)}, u32[]{:S(2)}, u32[]{:S(2)}) %collective-permute-start.1) | collective-permute-done | bytes 184352 | tf_op jit(solution)/shard_map/ppermute | solution.py:324
  24.3 5.9 %collective-permute-done.low_faces = f32[360,128]{1,0:T(8,128)S(1)} collective-permute-done((f32[360,128]{1,0:T(8,128)S(1)}, f32[360,128]{1,0:T(8,128)S(1)}, u32[]{:S(2)}, u32[]{:S(2)}) %collective-permute-start) | collective-permute-done | bytes 184352 | tf_op jit(solution)/shard_map/ppermute | solution.py:323
  30.3 0.0 copy-done
  30.3 4.5 %update.1 = (f32[1,1,3,5,4096]{4,3,2,1,0:T(8,128)S(1)}, f32[160,128]{1,0:T(8,128)S(1)}) custom-call(f32[1,1,3,5,4096]{4,3,2,1,0:T(8,128)S(1)} %copy.6.state, f32[3,16,5,8,128]{4,3,2,1,0:T(8,128)S(1)} %get-tuple-element.9.planes, f32[360,128]{1,0:T(8,128)S(1)} %get-tuple-element.10.own_faces, f32[360,128]{1,0:T(8,128)S(1)} %collective-permute-done.low_faces, ...), custom_call_target="tpu_custom_call" | custom-call | tf_op jit(solution)/shard_map/update/pallas_call | solution.py:261
  34.8 7.4 %collective-permute-start.4 = (f32[160,128]{1,0:T(8,128)S(1)}, f32[160,128]{1,0:T(8,128)S(1)}, u32[]{:S(2)}, u32[]{:S(2)}) collective-permute-start(f32[160,128]{1,0:T(8,128)S(1)} %get-tuple-element.11), channel_id=1, source_target_pairs={{0,4},{1,5},{2,6},{3,7},{4,0},{5,1},{6,2},{7,3},{8,12},{9,13},{10,... | collective-permute-start | bytes 245768 | tf_op jit(solution)/shard_map/ppermute | solution.py:327
  42.2 2.5 %collective-permute-start.3 = (f32[160,128]{1,0:T(8,128)S(1)}, f32[160,128]{1,0:T(8,128)S(1)}, u32[]{:S(2)}, u32[]{:S(2)}) collective-permute-start(f32[160,128]{1,0:T(8,128)S(1)} %get-tuple-element.11), channel_id=1, source_target_pairs={{0,2},{1,3},{2,0},{3,1},{4,6},{5,7},{6,4},{7,5},{8,10},{9,11},{10,... | collective-permute-start | bytes 245768 | tf_op jit(solution)/shard_map/ppermute | solution.py:327
  44.8 2.5 %collective-permute-start.2 = (f32[160,128]{1,0:T(8,128)S(1)}, f32[160,128]{1,0:T(8,128)S(1)}, u32[]{:S(2)}, u32[]{:S(2)}) collective-permute-start(f32[160,128]{1,0:T(8,128)S(1)} %get-tuple-element.11), channel_id=1, source_target_pairs={{0,1},{1,0},{2,3},{3,2},{4,5},{5,4},{6,7},{7,6},{8,9},{9,8},{10,11... | collective-permute-start | bytes 245768 | tf_op jit(solution)/shard_map/ppermute | solution.py:327
  47.3 0.0 collective-permute-done.4.refs_2_
  47.3 3.1 %collective-permute-done.3.refs_1_ = f32[160,128]{1,0:T(8,128)S(1)} collective-permute-done((f32[160,128]{1,0:T(8,128)S(1)}, f32[160,128]{1,0:T(8,128)S(1)}, u32[]{:S(2)}, u32[]{:S(2)}) %collective-permute-start.3) | collective-permute-done | bytes 81952 | tf_op jit(solution)/shard_map/ppermute | solution.py:327
  50.3 0.9 %collective-permute-done.2.refs_0_ = f32[160,128]{1,0:T(8,128)S(1)} collective-permute-done((f32[160,128]{1,0:T(8,128)S(1)}, f32[160,128]{1,0:T(8,128)S(1)}, u32[]{:S(2)}, u32[]{:S(2)}) %collective-permute-start.2) | collective-permute-done | bytes 81952 | tf_op jit(solution)/shard_map/ppermute | solution.py:327
  51.2 0.7 %place.1 = f32[1,1,3,5,4096]{4,3,2,1,0:T(8,128)S(1)} custom-call(f32[160,128]{1,0:T(8,128)S(1)} %collective-permute-done.2.refs_0_, f32[160,128]{1,0:T(8,128)S(1)} %collective-permute-done.3.refs_1_, f32[160,128]{1,0:T(8,128)S(1)} %collective-permute-done.4.refs_2_, ...), custom_call_target="tpu_custom_call", output_to_operand_aliasing={{}: (3, {})} | custom-call | tf_op jit(solution)/shard_map/place/pallas_call | solution.py:302
  51.9 1.0 %copy.8 = f32[1,1,3,5,4096]{4,1,3,2,0:T(1,128)} copy(f32[1,1,3,5,4096]{4,3,2,1,0:T(8,128)S(1)} %place.1) | data formatting | bytes 491520 | tf_op jit(solution)/shard_map/place/pallas_call | solution.py:302
Async XLA Ops:
  1.1 22.1 %copy-start.1 = (s32[1,1,3,6,2]{3,4,2,1,0:T(2,128)S(1)}, s32[1,1,3,6,2]{3,4,2,1,0:T(2,128)}, u32[]{:S(2)}) copy-start(s32[1,1,3,6,2]{3,4,2,1,0:T(2,128)} %param.4) | copy-start | bytes 436
  3.9 20.5 %collective-permute-start.1 = (f32[360,128]{1,0:T(8,128)S(1)}, f32[360,128]{1,0:T(8,128)S(1)}, u32[]{:S(2)}, u32[]{:S(2)}) collective-permute-start(f32[360,128]{1,0:T(8,128)S(1)} %get-tuple-element.10.own_faces), channel_id=1, source_target_pairs={{8,0},{16,8},{24,16},{32,24},{40,32},{48,40},{56,48},{64,56},{72,6... | collective-permute-start | bytes 552968 | tf_op jit(solution)/shard_map/ppermute | solution.py:324
  21.3 9.0 %collective-permute-start = (f32[360,128]{1,0:T(8,128)S(1)}, f32[360,128]{1,0:T(8,128)S(1)}, u32[]{:S(2)}, u32[]{:S(2)}) collective-permute-start(f32[360,128]{1,0:T(8,128)S(1)} %get-tuple-element.10.own_faces), channel_id=1, source_target_pairs={{0,8},{8,16},{16,24},{24,32},{32,40},{40,48},{48,56},{56,64},{64,7... | collective-permute-start | bytes 552968 | tf_op jit(solution)/shard_map/ppermute | solution.py:323
  23.4 6.9 %copy-start = (s32[1,8]{1,0:T(1,128)S(1)}, s32[1,8]{1,0:T(1,128)}, u32[]{:S(2)}) copy-start(s32[1,8]{1,0:T(1,128)} %refs_4_.1) | copy-start | bytes 100
  34.8 12.4 %collective-permute-start.4 = (f32[160,128]{1,0:T(8,128)S(1)}, f32[160,128]{1,0:T(8,128)S(1)}, u32[]{:S(2)}, u32[]{:S(2)}) collective-permute-start(f32[160,128]{1,0:T(8,128)S(1)} %get-tuple-element.11), channel_id=1, source_target_pairs={{0,4},{1,5},{2,6},{3,7},{4,0},{5,1},{6,2},{7,3},{8,12},{9,13},{10,... | collective-permute-start | bytes 245768 | tf_op jit(solution)/shard_map/ppermute | solution.py:327
  42.2 8.1 %collective-permute-start.3 = (f32[160,128]{1,0:T(8,128)S(1)}, f32[160,128]{1,0:T(8,128)S(1)}, u32[]{:S(2)}, u32[]{:S(2)}) collective-permute-start(f32[160,128]{1,0:T(8,128)S(1)} %get-tuple-element.11), channel_id=1, source_target_pairs={{0,2},{1,3},{2,0},{3,1},{4,6},{5,7},{6,4},{7,5},{8,10},{9,11},{10,... | collective-permute-start | bytes 245768 | tf_op jit(solution)/shard_map/ppermute | solution.py:327
  44.8 6.5 %collective-permute-start.2 = (f32[160,128]{1,0:T(8,128)S(1)}, f32[160,128]{1,0:T(8,128)S(1)}, u32[]{:S(2)}, u32[]{:S(2)}) collective-permute-start(f32[160,128]{1,0:T(8,128)S(1)} %get-tuple-element.11), channel_id=1, source_target_pairs={{0,1},{1,0},{2,3},{3,2},{4,5},{5,4},{6,7},{7,6},{8,9},{9,8},{10,11... | collective-permute-start | bytes 245768 | tf_op jit(solution)/shard_map/ppermute | solution.py:327

commit v2 on v1

--- a/solution.py
+++ b/solution.py
@@ -12,7 +12,7 @@
 SLOTS = 3
 LANES = 128
 ROWS = 2 * SLOTS
-CHUNKS = 32
+BLOCK_ROWS = 2 * EDGE * FIELDS
 FACE_ROWS = 6 * 2 * FIELDS * ROWS
 
 heat_ratio = 1.4
@@ -61,13 +61,24 @@
     return swap_chunks(planes[:8], EDGE, lane) + swap_chunks(planes[8:], EDGE, lane)
 
 
+def row_moves():
+    for slot in range(SLOTS):
+        for field in range(FIELDS):
+            for half in range(2):
+                here = slot * BLOCK_ROWS + field * 2 * EDGE + half
+                there = field * 8 + 2 * slot + half
+                yield (
+                    slot,
+                    field,
+                    half,
+                    pl.ds(here, EDGE, stride=2),
+                    pl.ds(there, EDGE, stride=FIELDS * 8),
+                )
+
+
 def prepare_kernel(state, planes, faces, work):
-    for slot in range(SLOTS):
-        for chunk in range(CHUNKS):
-            base = (chunk // 2) * FIELDS * 8 + 2 * slot + chunk % 2
-            work[pl.ds(base, FIELDS, stride=8), :] = state[
-                0, 0, slot, :, chunk * LANES : (chunk + 1) * LANES
-            ]
+    for slot, field, half, here, there in row_moves():
+        work[there, :] = state[here, :]
     for number in range(EDGE):
         base = number * FIELDS * 8
         rows = [work[base + 8 * field : base + 8 * field + 8, :] for field in range(FIELDS)]
@@ -86,7 +97,7 @@
         y_planes = x_to_y(x_planes, lane, row)
         for number in range(EDGE):
             planes[1, number, field] = y_planes[number]
-        z_planes = swap_chunks(y_planes, 1, lane)
+        z_planes = swap_chunks(x_planes, 1, lane)
         for number in range(EDGE):
             planes[2, number, field] = z_planes[number]
         return carry
@@ -181,7 +192,7 @@
 
 
 def update_kernel(
-    rounds, state, planes, own_faces, low_faces, high_faces, links, counts, out, moved, ghosts, change, work
+    rounds, state, planes, own_faces, high_faces, low_faces, links, counts, out, moved, ghosts, change, work
 ):
     sub_index = lax.axis_index("sub")
     _, last_count, _ = final_counts(counts, sub_index, rounds)
@@ -233,36 +244,29 @@
 
     def one_field(field, carry):
         z_change = swap_chunks([change[2, number, field] for number in range(EDGE)], 1, lane)
-        y_change = [z_change[number] + change[1, number, field] for number in range(EDGE)]
-        x_change = y_to_x(y_change, lane, row)
+        y_change = y_to_x([change[1, number, field] for number in range(EDGE)], lane, row)
         for number in range(EDGE):
             base = pl.multiple_of(number * FIELDS * 8 + field * 8, 8)
-            work[pl.ds(base, 8), :] = x_change[number] + change[0, number, field]
+            work[pl.ds(base, 8), :] = (change[0, number, field] + y_change[number]) + z_change[number]
         return carry
 
     lax.fori_loop(0, FIELDS, one_field, 0)
 
-    for slot in range(SLOTS):
-        for chunk in range(CHUNKS):
-            base = (chunk // 2) * FIELDS * 8 + 2 * slot + chunk % 2
-            cells = slice(chunk * LANES, (chunk + 1) * LANES)
-            fresh = (
-                state[0, 0, slot, :, cells]
-                - courant * work[pl.ds(base, FIELDS, stride=8), :]
-            )
-            if slot == SLOTS - 1:
-                moved[chunk * FIELDS : (chunk + 1) * FIELDS, :] = fresh
-            out[0, 0, slot, :, cells] = jnp.where(slot < last_count, fresh, 0.0)
-
-
-def update(state, planes, own_faces, low_faces, high_faces, links, counts, rounds):
+    for slot, field, half, here, there in row_moves():
+        fresh = state[here, :] - courant * work[there, :]
+        if slot == SLOTS - 1:
+            moved[pl.ds(field * 2 * EDGE + half, EDGE, stride=2), :] = fresh
+        out[here, :] = jnp.where(slot < last_count, fresh, 0.0)
+
+
+def update(state, planes, own_faces, high_faces, low_faces, links, counts, rounds):
     vmem = pl.BlockSpec(memory_space=pltpu.VMEM)
     smem = pl.BlockSpec(memory_space=pltpu.SMEM)
     return pl.pallas_call(
         functools.partial(update_kernel, rounds),
         out_shape=(
             jax.ShapeDtypeStruct(state.shape, jnp.float32),
-            jax.ShapeDtypeStruct((CHUNKS * FIELDS, LANES), jnp.float32),
+            jax.ShapeDtypeStruct((BLOCK_ROWS, LANES), jnp.float32),
         ),
         in_specs=[vmem] * 5 + [smem] * 2,
         out_specs=(vmem, vmem),
@@ -273,25 +277,20 @@
         ],
         compiler_params=pltpu.CompilerParams(vmem_limit_bytes=VMEM_LIMIT),
         name="update",
-    )(state, planes, own_faces, low_faces, high_faces, links, counts)
+    )(state, planes, own_faces, high_faces, low_faces, links, counts)
 
 
 def place_kernel(rounds, *refs):
-    arrived, (_, counts, out, block, sem) = refs[:rounds], refs[rounds:]
+    arrived, (_, counts, out, sem) = refs[:rounds], refs[rounds:]
     sub_index = lax.axis_index("sub")
-    start, _, arrival = final_counts(counts, sub_index, rounds)
-
-    @pl.when(arrival >= 0)
-    def _():
-        for chunk in range(CHUNKS):
-            rows = slice(chunk * FIELDS, (chunk + 1) * FIELDS)
-            value = arrived[0][rows, :]
-            for bit in range(1, rounds):
-                value = jnp.where(arrival == bit, arrived[bit][rows, :], value)
-            block[:, chunk * LANES : (chunk + 1) * LANES] = value
-        copy = pltpu.make_async_copy(block, out.at[0, 0, start], sem)
-        copy.start()
-        copy.wait()
+    _, _, arrival = final_counts(counts, sub_index, rounds)
+    for bit in range(rounds):
+
+        @pl.when(arrival == bit)
+        def _():
+            copy = pltpu.make_async_copy(arrived[bit], out.at[pl.ds(BLOCK_ROWS, BLOCK_ROWS)], sem)
+            copy.start()
+            copy.wait()
 
 
 def place(arrived, out, counts):
@@ -304,12 +303,8 @@
         out_shape=jax.ShapeDtypeStruct(out.shape, out.dtype),
         in_specs=[vmem] * rounds + [anywhere, smem],
         out_specs=anywhere,
-        scratch_shapes=[
-            pltpu.VMEM((FIELDS, EDGE**3), jnp.float32),
-            pltpu.SemaphoreType.DMA,
-        ],
+        scratch_shapes=[pltpu.SemaphoreType.DMA],
         input_output_aliases={rounds: 0},
-        compiler_params=pltpu.CompilerParams(vmem_limit_bytes=VMEM_LIMIT),
         name="place",
     )(*arrived, out, counts)
 
@@ -317,19 +312,21 @@
 def body(state, neighbours, counts):
     size = lax.axis_size("blocks")
     rounds = lax.axis_size("sub").bit_length() - 1
+    shape = state.shape
+    state = state.reshape(SLOTS * BLOCK_ROWS, LANES)
     planes, faces = prepare(state)
     forward = [(i, i + 1) for i in range(size - 1)]
     backward = [(i + 1, i) for i in range(size - 1)]
+    high = lax.ppermute(faces, "blocks", backward)
     low = lax.ppermute(faces, "blocks", forward)
-    high = lax.ppermute(faces, "blocks", backward)
-    out, moved = update(state, planes, faces, low, high, neighbours, counts, rounds)
+    out, moved = update(state, planes, faces, high, low, neighbours, counts, rounds)
     arrived = [
         lax.ppermute(
             moved, "sub", [(s, s ^ (1 << bit)) for s in range(lax.axis_size("sub"))]
         )
         for bit in range(rounds)
     ]
-    return place(arrived, out, counts)
+    return place(arrived, out, counts).reshape(shape)
 
 
 def solution(mesh):

time: 53.4 us -> 48.1 us (0.901)
  waiting for transfers between devices: 10.9 us -> 6.17 us
  Pallas kernels: 7.95 us -> 6.79 us
    ppermute x1, waiting for transfers between devices: 5.93 us -> 0.49 us  [body(): low = lax.ppermute(faces, 'blocks', forward)]
    unnamed x6 -> x13, local copies, waits for them, and re-layouts: 1.21 us -> 2.37 us
    pallas_call x1, Pallas kernels: 2.76 us -> 1.62 us  [prepare(): pl.pallas_call(prepare_kernel, out_shape=(jax.ShapeDtypeStruct((3, EDGE,...]
    pallas_call x1 -> x0, local copies, waits for them, and re-layouts: 0.96 us -> none  [place(): pl.pallas_call(functools.partial(place_kernel, rounds), out_shape=jax.Sha...]
    ppermute x1, waiting for transfers between devices: 0.99 us -> 1.76 us  [body(): high = lax.ppermute(faces, 'blocks', backward)]
  transfers between devices with their start and end apart: 5 -> 5, of which waited for: 4 -> 4; matrix products, arithmetic and copies ran while one was open for 0% -> 2% of each run, Pallas kernels for 0% -> 0%
where the time goes in v2:
time: 48.1 us; the launch traced here: 47.2 us
  starting transfers between devices  31.8 us (66%)
  Pallas kernels  6.79 us (14%)
  waiting for transfers between devices  6.17 us (13%)
  local copies, waits for them, and re-layouts  2.37 us (5%)
    ppermute x1, starting transfers between devices, body(): high = lax.ppermute(faces, 'blocks', backward)  17.4 us
    ppermute x3, starting transfers between devices, body(): lax.ppermute(moved, 'sub', [(s, s ^ 1 << bit) for s in range(lax.axis_siz...  12.4 us
    pallas_call x1, Pallas kernels, update(): pl.pallas_call(functools.partial(update_kernel, rounds), out_shape=(jax.S...  4.08 us
    ppermute x3, waiting for transfers between devices, body(): lax.ppermute(moved, 'sub', [(s, s ^ 1 << bit) for s in range(lax.axis_siz...  3.92 us
    unnamed x13, local copies, waits for them, and re-layouts  2.37 us
    ppermute x1, starting transfers between devices, body(): low = lax.ppermute(faces, 'blocks', forward)  1.92 us
    ppermute x1, waiting for transfers between devices, body(): high = lax.ppermute(faces, 'blocks', backward)  1.76 us
    pallas_call x1, Pallas kernels, prepare(): pl.pallas_call(prepare_kernel, out_shape=(jax.ShapeDtypeStruct((3, EDGE,...  1.62 us
  transfers between devices with their start and end apart: 5, of which 4 were waited for; matrix products, arithmetic and copies ran while one was open for 2% of the time, Pallas kernels for 0%

profile of v2, /device:TPU:112, one launch (start us, length us, event | category | flops | bytes accessed | tf_op | source)
XLA Modules:
  0.0 47.2 jit_solution(6838036049825946133)
XLA Ops:
  0.0 0.0 copy-start
  0.0 0.9 %copy-done = f32[1,1,3,5,4096]{4,1,3,2,0:T(1,128)S(1)} copy-done((f32[1,1,3,5,4096]{4,1,3,2,0:T(1,128)S(1)}, f32[1,1,3,5,4096]{4,1,3,2,0:T(1,128)}, u32[]{:S(2)}) %copy-start) | copy-done | bytes 245784
  0.9 0.0 copy-start.1
  0.9 1.6 %prepare.1 = (f32[3,16,5,8,128]{4,3,2,1,0:T(8,128)S(1)}, f32[360,128]{1,0:T(8,128)S(1)}) custom-call(f32[480,128]{1,0:T(8,128)S(1)} %bitcast.2), custom_call_target="tpu_custom_call" | custom-call | tf_op jit(solution)/shard_map/prepare/pallas_call | solution.py:117
  2.6 1.9 %collective-permute-start.1 = (f32[360,128]{1,0:T(8,128)S(1)}, f32[360,128]{1,0:T(8,128)S(1)}, u32[]{:S(2)}, u32[]{:S(2)}) collective-permute-start(f32[360,128]{1,0:T(8,128)S(1)} %get-tuple-element.10.own_faces), channel_id=1, source_target_pairs={{0,8},{8,16},{16,24},{24,32},{32,40},{40,48},{48,56},{56,64},{64,7... | collective-permute-start | bytes 552968 | tf_op jit(solution)/shard_map/ppermute | solution.py:321
  4.5 17.4 %collective-permute-start = (f32[360,128]{1,0:T(8,128)S(1)}, f32[360,128]{1,0:T(8,128)S(1)}, u32[]{:S(2)}, u32[]{:S(2)}) collective-permute-start(f32[360,128]{1,0:T(8,128)S(1)} %get-tuple-element.10.own_faces), channel_id=1, source_target_pairs={{8,0},{16,8},{24,16},{32,24},{40,32},{48,40},{56,48},{64,56},{72,6... | collective-permute-start | bytes 552968 | tf_op jit(solution)/shard_map/ppermute | solution.py:320
  21.9 0.8 %copy.7.links = s32[1,1,3,6,2]{4,3,2,1,0:T(8,128)S(1)} copy(s32[1,1,3,6,2]{3,4,2,1,0:T(2,128)} %param.4) | data formatting | bytes 288 | tf_op args[1]
  22.7 0.0 copy-start.2
  22.7 0.5 %collective-permute-done.1.low_faces = f32[360,128]{1,0:T(8,128)S(1)} collective-permute-done((f32[360,128]{1,0:T(8,128)S(1)}, f32[360,128]{1,0:T(8,128)S(1)}, u32[]{:S(2)}, u32[]{:S(2)}) %collective-permute-start.1) | collective-permute-done | bytes 184352 | tf_op jit(solution)/shard_map/ppermute | solution.py:321
  23.2 1.8 %collective-permute-done.high_faces = f32[360,128]{1,0:T(8,128)S(1)} collective-permute-done((f32[360,128]{1,0:T(8,128)S(1)}, f32[360,128]{1,0:T(8,128)S(1)}, u32[]{:S(2)}, u32[]{:S(2)}) %collective-permute-start) | collective-permute-done | bytes 184352 | tf_op jit(solution)/shard_map/ppermute | solution.py:320
  25.0 0.0 copy-done.1
  25.0 0.0 copy-done.2
  25.0 4.1 %update.1 = (f32[480,128]{1,0:T(8,128)}, f32[160,128]{1,0:T(8,128)S(1)}) custom-call(f32[480,128]{1,0:T(8,128)S(1)} %bitcast.3, f32[3,16,5,8,128]{4,3,2,1,0:T(8,128)S(1)} %get-tuple-element.9.planes, f32[360,128]{1,0:T(8,128)S(1)} %get-tuple-element.10.own_faces, f32[360,128]{1,0:T(8,128)S(1)} %collective-permute-done.high_faces, ...), custom_call_target="tpu_custom_call" | custom-call | tf_op jit(solution)/shard_map/update/pallas_call | solution.py:265
  29.1 7.4 %collective-permute-start.4 = (f32[160,128]{1,0:T(8,128)S(1)}, f32[160,128]{1,0:T(8,128)S(1)}, u32[]{:S(2)}, u32[]{:S(2)}) collective-permute-start(f32[160,128]{1,0:T(8,128)S(1)} %get-tuple-element.11), channel_id=1, source_target_pairs={{0,4},{1,5},{2,6},{3,7},{4,0},{5,1},{6,2},{7,3},{8,12},{9,13},{10,... | collective-permute-start | bytes 245768 | tf_op jit(solution)/shard_map/ppermute | solution.py:324
  36.4 2.5 %collective-permute-start.3 = (f32[160,128]{1,0:T(8,128)S(1)}, f32[160,128]{1,0:T(8,128)S(1)}, u32[]{:S(2)}, u32[]{:S(2)}) collective-permute-start(f32[160,128]{1,0:T(8,128)S(1)} %get-tuple-element.11), channel_id=1, source_target_pairs={{0,2},{1,3},{2,0},{3,1},{4,6},{5,7},{6,4},{7,5},{8,10},{9,11},{10,... | collective-permute-start | bytes 245768 | tf_op jit(solution)/shard_map/ppermute | solution.py:324
  39.0 2.5 %collective-permute-start.2 = (f32[160,128]{1,0:T(8,128)S(1)}, f32[160,128]{1,0:T(8,128)S(1)}, u32[]{:S(2)}, u32[]{:S(2)}) collective-permute-start(f32[160,128]{1,0:T(8,128)S(1)} %get-tuple-element.11), channel_id=1, source_target_pairs={{0,1},{1,0},{2,3},{3,2},{4,5},{5,4},{6,7},{7,6},{8,9},{9,8},{10,11... | collective-permute-start | bytes 245768 | tf_op jit(solution)/shard_map/ppermute | solution.py:324
  41.5 0.0 collective-permute-done.4.refs_2_
  41.5 0.0 copy-start.3
  41.5 3.1 %collective-permute-done.3.refs_1_ = f32[160,128]{1,0:T(8,128)S(1)} collective-permute-done((f32[160,128]{1,0:T(8,128)S(1)}, f32[160,128]{1,0:T(8,128)S(1)}, u32[]{:S(2)}, u32[]{:S(2)}) %collective-permute-start.3) | collective-permute-done | bytes 81952 | tf_op jit(solution)/shard_map/ppermute | solution.py:324
  44.6 0.0 copy-start.4
  44.6 0.9 %collective-permute-done.2.refs_0_ = f32[160,128]{1,0:T(8,128)S(1)} collective-permute-done((f32[160,128]{1,0:T(8,128)S(1)}, f32[160,128]{1,0:T(8,128)S(1)}, u32[]{:S(2)}, u32[]{:S(2)}) %collective-permute-start.2) | collective-permute-done | bytes 81952 | tf_op jit(solution)/shard_map/ppermute | solution.py:324
  45.4 0.0 copy-start.5
  45.4 0.0 copy-done.3
  45.4 0.0 copy-done.4
  45.4 0.6 %copy-done.5 = f32[160,128]{1,0:T(8,128)} copy-done((f32[160,128]{1,0:T(8,128)}, f32[160,128]{1,0:T(8,128)S(1)}, u32[]{:S(2)}) %copy-start.5) | copy-done | bytes 81944
  46.1 1.1 %place.1 = f32[480,128]{1,0:T(8,128)} custom-call(f32[160,128]{1,0:T(8,128)} %copy-done.5, f32[160,128]{1,0:T(8,128)} %copy-done.4, f32[160,128]{1,0:T(8,128)} %copy-done.3, f32[480,128]{1,0:T(8,128)} %get-tuple-element.12.refs_3_, s32[1,8]{1,0:T(1,128)} %refs_4_.1), custom_call_target="tpu_custom_call", output_to_operand_aliasing={{}: (3, {})} | custom-call | tf_op jit(solution)/shard_map/place/pallas_call | solution.py:301
Async XLA Ops:
  0.0 0.9 %copy-start = (f32[1,1,3,5,4096]{4,1,3,2,0:T(1,128)S(1)}, f32[1,1,3,5,4096]{4,1,3,2,0:T(1,128)}, u32[]{:S(2)}) copy-start(f32[1,1,3,5,4096]{4,1,3,2,0:T(1,128)} %param.3) | copy-start | bytes 737284
  0.9 24.0 %copy-start.1 = (f32[1,1,3,5,4096]{4,1,3,2,0:T(1,128)S(1)}, f32[1,1,3,5,4096]{4,1,3,2,0:T(1,128)}, u32[]{:S(2)}) copy-start(f32[1,1,3,5,4096]{4,1,3,2,0:T(1,128)} %param.3) | copy-start | bytes 737284
  2.6 20.6 %collective-permute-start.1 = (f32[360,128]{1,0:T(8,128)S(1)}, f32[360,128]{1,0:T(8,128)S(1)}, u32[]{:S(2)}, u32[]{:S(2)}) collective-permute-start(f32[360,128]{1,0:T(8,128)S(1)} %get-tuple-element.10.own_faces), channel_id=1, source_target_pairs={{0,8},{8,16},{16,24},{24,32},{32,40},{40,48},{48,56},{56,64},{64,7... | collective-permute-start | bytes 552968 | tf_op jit(solution)/shard_map/ppermute | solution.py:321
  4.5 20.5 %collective-permute-start = (f32[360,128]{1,0:T(8,128)S(1)}, f32[360,128]{1,0:T(8,128)S(1)}, u32[]{:S(2)}, u32[]{:S(2)}) collective-permute-start(f32[360,128]{1,0:T(8,128)S(1)} %get-tuple-element.10.own_faces), channel_id=1, source_target_pairs={{8,0},{16,8},{24,16},{32,24},{40,32},{48,40},{56,48},{64,56},{72,6... | collective-permute-start | bytes 552968 | tf_op jit(solution)/shard_map/ppermute | solution.py:320
  22.7 2.3 %copy-start.2 = (s32[1,8]{1,0:T(1,128)S(1)}, s32[1,8]{1,0:T(1,128)}, u32[]{:S(2)}) copy-start(s32[1,8]{1,0:T(1,128)} %refs_4_.1) | copy-start | bytes 100
  29.1 12.4 %collective-permute-start.4 = (f32[160,128]{1,0:T(8,128)S(1)}, f32[160,128]{1,0:T(8,128)S(1)}, u32[]{:S(2)}, u32[]{:S(2)}) collective-permute-start(f32[160,128]{1,0:T(8,128)S(1)} %get-tuple-element.11), channel_id=1, source_target_pairs={{0,4},{1,5},{2,6},{3,7},{4,0},{5,1},{6,2},{7,3},{8,12},{9,13},{10,... | collective-permute-start | bytes 245768 | tf_op jit(solution)/shard_map/ppermute | solution.py:324
  36.4 8.1 %collective-permute-start.3 = (f32[160,128]{1,0:T(8,128)S(1)}, f32[160,128]{1,0:T(8,128)S(1)}, u32[]{:S(2)}, u32[]{:S(2)}) collective-permute-start(f32[160,128]{1,0:T(8,128)S(1)} %get-tuple-element.11), channel_id=1, source_target_pairs={{0,2},{1,3},{2,0},{3,1},{4,6},{5,7},{6,4},{7,5},{8,10},{9,11},{10,... | collective-permute-start | bytes 245768 | tf_op jit(solution)/shard_map/ppermute | solution.py:324
  39.0 6.5 %collective-permute-start.2 = (f32[160,128]{1,0:T(8,128)S(1)}, f32[160,128]{1,0:T(8,128)S(1)}, u32[]{:S(2)}, u32[]{:S(2)}) collective-permute-start(f32[160,128]{1,0:T(8,128)S(1)} %get-tuple-element.11), channel_id=1, source_target_pairs={{0,1},{1,0},{2,3},{3,2},{4,5},{5,4},{6,7},{7,6},{8,9},{9,8},{10,11... | collective-permute-start | bytes 245768 | tf_op jit(solution)/shard_map/ppermute | solution.py:324
  41.5 3.9 %copy-start.3 = (f32[160,128]{1,0:T(8,128)}, f32[160,128]{1,0:T(8,128)S(1)}, u32[]{:S(2)}) copy-start(f32[160,128]{1,0:T(8,128)S(1)} %collective-permute-done.4.refs_2_) | copy-start | bytes 245764
  44.6 0.9 %copy-start.4 = (f32[160,128]{1,0:T(8,128)}, f32[160,128]{1,0:T(8,128)S(1)}, u32[]{:S(2)}) copy-start(f32[160,128]{1,0:T(8,128)S(1)} %collective-permute-done.3.refs_1_) | copy-start | bytes 245764
  45.4 0.6 %copy-start.5 = (f32[160,128]{1,0:T(8,128)}, f32[160,128]{1,0:T(8,128)S(1)}, u32[]{:S(2)}) copy-start(f32[160,128]{1,0:T(8,128)S(1)} %collective-permute-done.2.refs_0_) | copy-start | bytes 245764

commit v3 on v2

v3 whole, which is shorter than its diff:
```python
import functools

import jax
import jax.numpy as jnp
from jax import lax
from jax.experimental import pallas as pl
from jax.experimental.pallas import tpu as pltpu
from jax.sharding import PartitionSpec as P

EDGE = 16
FIELDS = 5
SLOTS = 3
LANES = 128
BLOCK_ROWS = 2 * EDGE * FIELDS
FACE_ROWS = 3 * 4 * FIELDS * 8
OUTER = (0, 1, EDGE - 1, EDGE - 2)

heat_ratio = 1.4
courant = 0.07

VMEM_LIMIT = 16 * 1024 * 1024


def square_moves():
    for slot in range(SLOTS):
        for field in range(FIELDS):
            for half in range(2):
                here = pl.ds((slot * FIELDS + field) * 2 * EDGE + half, EDGE, stride=2)
                there = slice(half * 64 + slot * EDGE, half * 64 + (slot + 1) * EDGE)
                yield slot, field, half, here, there


def comb(number):
    return pl.ds(number, 8, stride=EDGE)


def band(number):
    return slice(number * EDGE, (number + 1) * EDGE)


def face_rows(axis, place, field):
    base = axis * 4 * FIELDS * 8
    if axis == 1:
        return slice(base + (field * 2 + place) * EDGE, base + (field * 2 + place + 1) * EDGE)
    return slice(base + (place * FIELDS + field) * 8, base + (place * FIELDS + field + 1) * 8)


def lanes_of(rows):
    return lax.broadcasted_iota(jnp.int32, (rows, LANES), 1)


def primitives(cells):
    inverse = 1.0 / cells[0]
    v1, v2, v3 = cells[1] * inverse, cells[2] * inverse, cells[3] * inverse
    square = v1 * v1 + v2 * v2 + v3 * v3
    pressure = (heat_ratio - 1.0) * (cells[4] - 0.5 * cells[0] * square)
    return cells[0], v1, v2, v3, pressure


def prepare_kernel(state, upright, turned, faces):
    for half in range(2):
        for slot in range(SLOTS):
            cells = [
                state[pl.ds((slot * FIELDS + field) * 2 * EDGE + half, EDGE, stride=2), :]
                for field in range(FIELDS)
            ]
            for field, value in enumerate(primitives(cells)):
                upright[field, band(4 * half + slot), :] = value
                if slot == SLOTS - 1:
                    upright[field, band(4 * half + slot + 1), :] = value
    low_half = lanes_of(EDGE) < 64
    for field in range(FIELDS):
        turned[field] = upright[field].T
    for field in range(FIELDS):
        for place, number in enumerate(OUTER):
            faces[face_rows(0, place, field), :] = upright[field, comb(number), :]
            faces[face_rows(2, place, field), :] = turned[field, comb(number), :]
        for depth in range(2):
            faces[face_rows(1, depth, field), :] = jnp.where(
                low_half, turned[field, band(depth), :], turned[field, band(7 - depth), :]
            )


SQUARES = jax.ShapeDtypeStruct((FIELDS, LANES, LANES), jnp.float32)


def prepare(state):
    return pl.pallas_call(
        prepare_kernel,
        out_shape=(SQUARES, SQUARES, jax.ShapeDtypeStruct((FACE_ROWS, LANES), jnp.float32)),
        compiler_params=pltpu.CompilerParams(vmem_limit_bytes=VMEM_LIMIT),
        name="prepare",
    )(state)


def minmod(first, second):
    return jnp.maximum(jnp.minimum(first, second), 0.0) + jnp.minimum(
        jnp.maximum(first, second), 0.0
    )


def side_speeds(prim, component):
    scaled = heat_ratio * prim[4]
    sound = scaled * lax.rsqrt(scaled * prim[0])
    return prim[component] - sound, prim[component] + sound


def hll_flux(left, right, component):
    slow_left, fast_left = side_speeds(left, component)
    slow_right, fast_right = side_speeds(right, component)
    slow = jnp.minimum(jnp.minimum(slow_left, slow_right), 0.0)
    fast = jnp.maximum(jnp.maximum(fast_left, fast_right), 0.0)
    inverse = 1.0 / (fast - slow)
    weight_left = fast * inverse
    weight_right = -slow * inverse
    product = slow * weight_left
    normal_left, normal_right = left[component], right[component]
    carry_left = weight_left * normal_left - product
    carry_right = weight_right * normal_right + product
    mass_left, mass_right = carry_left * left[0], carry_right * right[0]
    push_left, push_right = weight_left * left[4], weight_right * right[4]
    outputs = [mass_left + mass_right]
    for number in (1, 2, 3):
        value = mass_left * left[number] + mass_right * right[number]
        if number == component:
            value = value + (push_left + push_right)
        outputs.append(value)
    square_left = left[1] * left[1] + left[2] * left[2] + left[3] * left[3]
    square_right = right[1] * right[1] + right[2] * right[2] + right[3] * right[3]
    inner = 1.0 / (heat_ratio - 1.0)
    energy = 0.5 * (mass_left * square_left + mass_right * square_right)
    energy = energy + inner * (carry_left * left[4] + carry_right * right[4])
    energy = energy + (push_left * normal_left + push_right * normal_right)
    outputs.append(energy)
    return outputs


def half_slopes(before, here, after):
    return [0.5 * minmod(b - a, c - b) for a, b, c in zip(before, here, after)]


def add(first, second):
    return [a + b for a, b in zip(first, second)]


def sub(first, second):
    return [a - b for a, b in zip(first, second)]


GROUPS = 5


def ghost_codes(links, codes):
    lane = lanes_of(EDGE)
    row = lax.broadcasted_iota(jnp.int32, (EDGE, LANES), 0)

    def by_slot(slot, face, part):
        last = links[2, part, face]
        return jnp.where(slot == 0, links[0, part, face], jnp.where(slot == 1, links[1, part, face], last))

    for side in range(2):
        slot = row & 3
        codes[side, 0] = by_slot(slot, side, 0)
        codes[side, 1] = (row & 4) + by_slot(slot, side, 1)
    slot = (lane >> 4) & 3
    inside = lane & (EDGE - 1)
    low_half = lane < 64
    for part in range(2):
        value = jnp.where(low_half, by_slot(slot, 2, part), by_slot(slot, 3, part))
        if part == 1:
            value = 64 - (lane & 64) + value * EDGE + inside
        codes[2, part] = value
    for side in range(2):
        codes[3 + side, 0] = by_slot(slot, 4 + side, 0)
        codes[3 + side, 1] = (lane & 64) + by_slot(slot, 4 + side, 1) * EDGE + inside


def inner_line(cell, size, component, store):
    before, here = cell(0), cell(1)
    left, flux = None, None
    for number in range(1, size - 1):
        after = cell(number + 1)
        slopes = half_slopes(before, here, after)
        if left is not None:
            next_flux = hll_flux(left, sub(here, slopes), component)
            store(number - 1, next_flux if flux is None else sub(next_flux, flux))
            flux = next_flux
        left = add(here, slopes)
        before, here = here, after
    store(size - 2, [-value for value in flux])


def inner_kernel(upright, turned, links, up_change, turned_change, codes):
    def store_comb(change):
        def store(number, values):
            for field in range(FIELDS):
                change[field, comb(number), :] = values[field]

        return store

    def add_band(number, values):
        for field in range(FIELDS):
            turned_change[field, band(number), :] += values[field]

    nothing = [jnp.zeros((8, LANES), jnp.float32)] * FIELDS
    for change in (up_change, turned_change):
        for number in (0, EDGE - 1):
            store_comb(change)(number, nothing)
    inner_line(
        lambda number: [upright[field, comb(number), :] for field in range(FIELDS)],
        EDGE,
        1,
        store_comb(up_change),
    )
    inner_line(
        lambda number: [turned[field, comb(number), :] for field in range(FIELDS)],
        EDGE,
        3,
        store_comb(turned_change),
    )
    inner_line(
        lambda number: [turned[field, band(number), :] for field in range(FIELDS)],
        8,
        2,
        add_band,
    )
    ghost_codes(links, codes)


def interior(upright, turned, links):
    vmem = pl.BlockSpec(memory_space=pltpu.VMEM)
    return pl.pallas_call(
        inner_kernel,
        out_shape=(
            SQUARES,
            SQUARES,
            jax.ShapeDtypeStruct((GROUPS, 2, EDGE, LANES), jnp.int32),
        ),
        in_specs=[vmem, vmem, pl.BlockSpec(memory_space=pltpu.SMEM)],
        out_specs=(vmem,) * 3,
        compiler_params=pltpu.CompilerParams(vmem_limit_bytes=VMEM_LIMIT),
        cost_estimate=pl.CostEstimate(flops=6_000_000, bytes_accessed=3_000_000, transcendentals=0),
        name="interior",
    )(upright, turned, links)


def final_counts(counts, sub_index, rounds):
    size = counts.shape[-1]
    now = [counts[0, position] for position in range(size)]

    def own(values):
        picked = values[0]
        for position in range(1, size):
            picked = jnp.where(sub_index == position, values[position], picked)
        return picked

    start = own(now)
    arrival = jnp.int32(-1)
    for bit in range(rounds):
        gains = [
            jnp.maximum(now[p ^ (1 << bit)] - now[p], 0) // 2
            - jnp.maximum(now[p] - now[p ^ (1 << bit)], 0) // 2
            for p in range(size)
        ]
        arrival = jnp.where(own(gains) > 0, bit, arrival)
        now = [value + gain for value, gain in zip(now, gains)]
    return start, own(now), arrival


def outer_side(near, far, first, second, third, side, component):
    slopes = half_slopes(near, first, second)
    if side == 0:
        beyond = add(near, half_slopes(far, near, first))
        within = sub(second, half_slopes(first, second, third))
        outside = hll_flux(beyond, sub(first, slopes), component)
        inside = hll_flux(add(first, slopes), within, component)
        return sub(inside, outside), [-value for value in inside]
    slopes = half_slopes(second, first, near)
    beyond = sub(near, half_slopes(first, near, far))
    within = add(second, half_slopes(third, second, first))
    outside = hll_flux(add(first, slopes), beyond, component)
    inside = hll_flux(within, sub(first, slopes), component)
    return sub(outside, inside), inside


def outer_kernel(
    state,
    upright,
    turned,
    up_change,
    turned_change,
    codes,
    own_faces,
    high_faces,
    low_faces,
    total,
    moved,
    fixed,
):
    def ghost(group, axis, place, mirror, field):
        rows = 8 if axis != 1 else EDGE
        owner, source = codes[group, 0, 0:rows, :], codes[group, 1, 0:rows, :]
        there = face_rows(axis, mirror, field)
        low, own, high = (
            jnp.take_along_axis(faces[there, :], source, axis=0 if axis == 0 else 1)
            for faces in (low_faces, own_faces, high_faces)
        )
        neighbour = jnp.where(owner == 0, low, jnp.where(owner == 1, own, high))
        return jnp.where(owner == 3, own_faces[face_rows(axis, place, field), :], neighbour)

    low_half = lanes_of(EDGE) < 64
    for field in range(FIELDS):
        fixed[field] = turned_change[field]

    cells = {
        number: [turned[field, band(number), :] for field in range(FIELDS)]
        for number in (0, 1, 2, 5, 6, 7)
    }
    ghosts = [[ghost(2, 1, depth, depth, field) for field in range(FIELDS)] for depth in range(2)]
    for side in range(2):
        numbers = (0, 1, 2) if side == 0 else (7, 6, 5)
        outside = []
        for depth in range(2):
            other = cells[7 - depth if side == 0 else depth]
            across = [pltpu.roll(value, 64, 1) for value in other]
            pair = (ghosts[depth], across) if side == 0 else (across, ghosts[depth])
            outside.append([jnp.where(low_half, a, b) for a, b in zip(*pair)])
        parts = outer_side(*outside, *(cells[number] for number in numbers), side, 2)
        for number, part in zip(numbers, parts):
            for field in range(FIELDS):
                fixed[field, band(number), :] += part[field]

    def comb_sides(square, axis, group, change):
        for side in range(2):
            numbers = (0, 1, 2) if side == 0 else (EDGE - 1, EDGE - 2, EDGE - 3)
            planes = [
                [square[field, comb(number), :] for field in range(FIELDS)] for number in numbers
            ]
            outside = [
                [
                    ghost(group + side, axis, 2 * side + depth, 2 * (1 - side) + depth, field)
                    for field in range(FIELDS)
                ]
                for depth in range(2)
            ]
            parts = outer_side(*outside, *planes, side, axis + 1)
            for number, part in zip(numbers, parts):
                for field in range(FIELDS):
                    change[field, comb(number), :] += part[field]

    comb_sides(turned, 2, 3, fixed)
    for field in range(FIELDS):
        total[field] = up_change[field] + fixed[field].T
    comb_sides(upright, 0, 0, total)

    for slot, field, half, here, there in square_moves():
        if slot == SLOTS - 1:
            moved[pl.ds(field * 2 * EDGE + half, EDGE, stride=2), :] = (
                state[here, :] - courant * total[field, there, :]
            )


def outer(*operands):
    vmem = pl.BlockSpec(memory_space=pltpu.VMEM)
    return pl.pallas_call(
        outer_kernel,
        out_shape=(SQUARES, jax.ShapeDtypeStruct((BLOCK_ROWS, LANES), jnp.float32)),
        in_specs=[vmem] * len(operands),
        out_specs=(vmem, vmem),
        scratch_shapes=[pltpu.VMEM(SQUARES.shape, jnp.float32)],
        compiler_params=pltpu.CompilerParams(vmem_limit_bytes=VMEM_LIMIT),
        name="outer",
    )(*operands)


def finish_kernel(rounds, state, total, counts, out):
    _, last_count, _ = final_counts(counts, lax.axis_index("sub"), rounds)
    for slot, field, _, here, there in square_moves():
        fresh = state[here, :] - courant * total[field, there, :]
        out[here, :] = jnp.where(slot < last_count, fresh, 0.0)


def finish(state, total, counts, rounds):
    vmem = pl.BlockSpec(memory_space=pltpu.VMEM)
    smem = pl.BlockSpec(memory_space=pltpu.SMEM)
    return pl.pallas_call(
        functools.partial(finish_kernel, rounds),
        out_shape=jax.ShapeDtypeStruct(state.shape, jnp.float32),
        in_specs=[vmem, vmem, smem],
        out_specs=vmem,
        compiler_params=pltpu.CompilerParams(vmem_limit_bytes=VMEM_LIMIT),
        cost_estimate=pl.CostEstimate(flops=200_000, bytes_accessed=1_000_000, transcendentals=0),
        name="finish",
    )(state, total, counts)


def place_kernel(rounds, *refs):
    arrived, (_, counts, out, sem) = refs[:rounds], refs[rounds:]
    sub_index = lax.axis_index("sub")
    _, _, arrival = final_counts(counts, sub_index, rounds)
    for bit in range(rounds):

        @pl.when(arrival == bit)
        def _():
            copy = pltpu.make_async_copy(arrived[bit], out.at[pl.ds(BLOCK_ROWS, BLOCK_ROWS)], sem)
            copy.start()
            copy.wait()


def place(arrived, out, counts):
    rounds = len(arrived)
    vmem = pl.BlockSpec(memory_space=pltpu.VMEM)
    smem = pl.BlockSpec(memory_space=pltpu.SMEM)
    anywhere = pl.BlockSpec(memory_space=pl.ANY)
    return pl.pallas_call(
        functools.partial(place_kernel, rounds),
        out_shape=jax.ShapeDtypeStruct(out.shape, out.dtype),
        in_specs=[vmem] * rounds + [anywhere, smem],
        out_specs=anywhere,
        scratch_shapes=[pltpu.SemaphoreType.DMA],
        input_output_aliases={rounds: 0},
        compiler_params=pltpu.CompilerParams(vmem_limit_bytes=1024 * 1024),
        name="place",
    )(*arrived, out, counts)


def body(state, neighbours, counts):
    size = lax.axis_size("blocks")
    rounds = lax.axis_size("sub").bit_length() - 1
    shape = state.shape
    state = state.reshape(SLOTS * BLOCK_ROWS, LANES)
    links = jnp.transpose(neighbours.reshape(SLOTS, 6, 2), (0, 2, 1))
    upright, turned, faces = prepare(state)
    forward = [(i, i + 1) for i in range(size - 1)]
    backward = [(i + 1, i) for i in range(size - 1)]
    high = lax.ppermute(faces, "blocks", backward)
    low = lax.ppermute(faces, "blocks", forward)
    changes = interior(upright, turned, links)
    total, moved = outer(state, upright, turned, *changes, faces, high, low)
    arrived = [
        lax.ppermute(
            moved, "sub", [(s, s ^ (1 << bit)) for s in range(lax.axis_size("sub"))]
        )
        for bit in range(rounds)
    ]
    out = finish(state, total, counts, rounds)
    return place(arrived, out, counts).reshape(shape)


def solution(mesh):
    return jax.shard_map(
        body,
        mesh=mesh,
        in_specs=(
            P("blocks", "sub", None, None, None),
            P("blocks", "sub", None, None, None),
            P("blocks", None),
        ),
        out_specs=P("blocks", "sub", None, None, None),
        check_vma=False,
    )
```

time: 48.1 us -> 42.2 us (0.88); the launches traced: 47.2 us -> 41.9 us
  Pallas kernels: 6.79 us -> 4.33 us
  waiting for transfers between devices: 6.17 us -> 4.75 us
  local copies, waits for them, and re-layouts: 2.37 us -> 0.96 us
    pallas_call x2 -> x4, Pallas kernels: 5.69 us -> 3.67 us  [the longest x1 1.49 us: interior(): pl.pallas_call(inner_kernel, out_shape=(SQUARES, SQUARES, jax.ShapeDtypeS...]
    unnamed x13 -> x8, local copies, waits for them, and re-layouts: 2.37 us -> 0.96 us
    ppermute x3, waiting for transfers between devices: 3.92 us -> 2.58 us  [body(): lax.ppermute(moved, 'sub', [(s, s ^ 1 << bit) for s in range(lax.axis_siz...]
  transfers between devices with their start and end apart: 5 -> 5, of which waited for: 4 -> 4; matrix products, arithmetic and copies ran while one was open for 2% -> 0% of each run, Pallas kernels for 0% -> 7%
where the time goes in v3:
time: 42.2 us; the launch traced here: 41.9 us
  starting transfers between devices  31.8 us (75%)
  waiting for transfers between devices  4.75 us (11%)
  Pallas kernels  4.33 us (10%)
  local copies, waits for them, and re-layouts  0.96 us (2%)
    ppermute x1, starting transfers between devices, body(): high = lax.ppermute(faces, 'blocks', backward)  17.4 us
    ppermute x3, starting transfers between devices, body(): lax.ppermute(moved, 'sub', [(s, s ^ 1 << bit) for s in range(lax.axis_siz...  12.4 us
    ppermute x3, waiting for transfers between devices, body(): lax.ppermute(moved, 'sub', [(s, s ^ 1 << bit) for s in range(lax.axis_siz...  2.58 us
    ppermute x1, starting transfers between devices, body(): low = lax.ppermute(faces, 'blocks', forward)  1.92 us
    ppermute x1, waiting for transfers between devices, body(): high = lax.ppermute(faces, 'blocks', backward)  1.76 us
    pallas_call x1, Pallas kernels, interior(): pl.pallas_call(inner_kernel, out_shape=(SQUARES, SQUARES, jax.ShapeDtypeS...  1.49 us
    pallas_call x1, Pallas kernels, finish(): pl.pallas_call(functools.partial(finish_kernel, rounds), out_shape=jax.Sh...  1.35 us
    unnamed x8, local copies, waits for them, and re-layouts  0.96 us
  transfers between devices with their start and end apart: 5, of which 4 were waited for; matrix products, arithmetic and copies ran while one was open for 0% of the time, Pallas kernels for 7%

profile of v3, /device:TPU:112, one launch (start us, length us, event | category | flops | bytes accessed | tf_op | source)
XLA Modules:
  0.0 41.9 jit_solution(8273500786942209695)
XLA Ops:
  0.0 0.0 copy-start
  0.0 0.9 %copy-done = f32[1,1,3,5,4096]{4,1,3,2,0:T(1,128)S(1)} copy-done((f32[1,1,3,5,4096]{4,1,3,2,0:T(1,128)S(1)}, f32[1,1,3,5,4096]{4,1,3,2,0:T(1,128)}, u32[]{:S(2)}) %copy-start) | copy-done | bytes 245784
  0.9 0.2 prepare.1
  1.2 0.0 copy-start.2
  1.2 1.9 %collective-permute-start.1 = (f32[480,128]{1,0:T(8,128)S(1)}, f32[480,128]{1,0:T(8,128)S(1)}, u32[]{:S(2)}, u32[]{:S(2)}) collective-permute-start(f32[480,128]{1,0:T(8,128)S(1)} %get-tuple-element.18.own_faces), channel_id=1, source_target_pairs={{0,8},{8,16},{16,24},{24,32},{32,40},{40,48},{48,56},{56,64},{64,7... | collective-permute-start | bytes 737288 | tf_op jit(solution)/shard_map/ppermute | solution.py:437
  3.1 17.4 %collective-permute-start = (f32[480,128]{1,0:T(8,128)S(1)}, f32[480,128]{1,0:T(8,128)S(1)}, u32[]{:S(2)}, u32[]{:S(2)}) collective-permute-start(f32[480,128]{1,0:T(8,128)S(1)} %get-tuple-element.18.own_faces), channel_id=1, source_target_pairs={{8,0},{16,8},{24,16},{32,24},{40,32},{48,40},{56,48},{64,56},{72,6... | collective-permute-start | bytes 737288 | tf_op jit(solution)/shard_map/ppermute | solution.py:436
  20.5 0.0 copy-done.2
  20.5 0.0 copy-start.1
  20.6 1.5 %interior.1 = (f32[5,128,128]{2,1,0:T(8,128)S(1)}, f32[5,128,128]{2,1,0:T(8,128)S(1)}, s32[5,2,16,128]{3,2,1,0:T(8,128)S(1)}) custom-call(f32[5,128,128]{2,1,0:T(8,128)S(1)} %get-tuple-element.13.upright, f32[5,128,128]{2,1,0:T(8,128)S(1)} %get-tuple-element.14.turned, s32[3,2,6]{2,1,0:T(2,128)S(1)} %bitcast.8), custom_call_target="tpu_custom_call" | custom-call | flops 6000000 | bytes 3000000 | tf_op jit(solution)/shard_map/interior/pallas_call | solution.py:232
  22.1 0.4 collective-permute-done.1.low_faces
  22.5 1.8 %collective-permute-done.high_faces = f32[480,128]{1,0:T(8,128)S(1)} collective-permute-done((f32[480,128]{1,0:T(8,128)S(1)}, f32[480,128]{1,0:T(8,128)S(1)}, u32[]{:S(2)}, u32[]{:S(2)}) %collective-permute-start) | collective-permute-done | bytes 245792 | tf_op jit(solution)/shard_map/ppermute | solution.py:436
  24.2 0.0 copy-done.1
  24.2 0.6 %outer.1 = (f32[5,128,128]{2,1,0:T(8,128)S(1)}, f32[160,128]{1,0:T(8,128)S(1)}) custom-call(f32[480,128]{1,0:T(8,128)S(1)} %bitcast.6, f32[5,128,128]{2,1,0:T(8,128)S(1)} %get-tuple-element.13.upright, f32[5,128,128]{2,1,0:T(8,128)S(1)} %get-tuple-element.14.turned, f32[5,128,128]{2,1,0:T(8,128)S(1)} %get-tuple-element.15.up_change, ...), custom_call_target="tpu_custom_call" | custom-call | tf_op jit(solution)/shard_map/outer/pallas_call | solution.py:365
  24.9 0.0 copy-start.3
  24.9 7.4 %collective-permute-start.4 = (f32[160,128]{1,0:T(8,128)S(1)}, f32[160,128]{1,0:T(8,128)S(1)}, u32[]{:S(2)}, u32[]{:S(2)}) collective-permute-start(f32[160,128]{1,0:T(8,128)S(1)} %get-tuple-element.19), channel_id=1, source_target_pairs={{0,4},{1,5},{2,6},{3,7},{4,0},{5,1},{6,2},{7,3},{8,12},{9,13},{10,... | collective-permute-start | bytes 245768 | tf_op jit(solution)/shard_map/ppermute | solution.py:441
  32.3 2.5 %collective-permute-start.3 = (f32[160,128]{1,0:T(8,128)S(1)}, f32[160,128]{1,0:T(8,128)S(1)}, u32[]{:S(2)}, u32[]{:S(2)}) collective-permute-start(f32[160,128]{1,0:T(8,128)S(1)} %get-tuple-element.19), channel_id=1, source_target_pairs={{0,2},{1,3},{2,0},{3,1},{4,6},{5,7},{6,4},{7,5},{8,10},{9,11},{10,... | collective-permute-start | bytes 245768 | tf_op jit(solution)/shard_map/ppermute | solution.py:441
  34.8 2.5 %collective-permute-start.2 = (f32[160,128]{1,0:T(8,128)S(1)}, f32[160,128]{1,0:T(8,128)S(1)}, u32[]{:S(2)}, u32[]{:S(2)}) collective-permute-start(f32[160,128]{1,0:T(8,128)S(1)} %get-tuple-element.19), channel_id=1, source_target_pairs={{0,1},{1,0},{2,3},{3,2},{4,5},{5,4},{6,7},{7,6},{8,9},{9,8},{10,11... | collective-permute-start | bytes 245768 | tf_op jit(solution)/shard_map/ppermute | solution.py:441
  37.3 0.0 copy-done.3
  37.3 1.4 %finish.1.refs_3_ = f32[480,128]{1,0:T(8,128)} custom-call(f32[480,128]{1,0:T(8,128)S(1)} %bitcast.7, f32[5,128,128]{2,1,0:T(8,128)S(1)} %get-tuple-element.20.total, s32[1,8]{1,0:T(1,128)S(1)} %copy-done.3), custom_call_target="tpu_custom_call" | custom-call | flops 200000 | bytes 1000000 | tf_op jit(solution)/shard_map/finish/pallas_call | solution.py:386
  38.7 0.0 collective-permute-done.4.refs_2_
  38.7 1.7 %collective-permute-done.3.refs_1_ = f32[160,128]{1,0:T(8,128)S(1)} collective-permute-done((f32[160,128]{1,0:T(8,128)S(1)}, f32[160,128]{1,0:T(8,128)S(1)}, u32[]{:S(2)}, u32[]{:S(2)}) %collective-permute-start.3) | collective-permute-done | bytes 81952 | tf_op jit(solution)/shard_map/ppermute | solution.py:441
  40.4 0.9 %collective-permute-done.2.refs_0_ = f32[160,128]{1,0:T(8,128)S(1)} collective-permute-done((f32[160,128]{1,0:T(8,128)S(1)}, f32[160,128]{1,0:T(8,128)S(1)}, u32[]{:S(2)}, u32[]{:S(2)}) %collective-permute-start.2) | collective-permute-done | bytes 81952 | tf_op jit(solution)/shard_map/ppermute | solution.py:441
  41.3 0.7 %place.1 = f32[480,128]{1,0:T(8,128)} custom-call(f32[160,128]{1,0:T(8,128)S(1)} %collective-permute-done.2.refs_0_, f32[160,128]{1,0:T(8,128)S(1)} %collective-permute-done.3.refs_1_, f32[160,128]{1,0:T(8,128)S(1)} %collective-permute-done.4.refs_2_, f32[480,128]{1,0:T(8,128)} %finish.1.refs_3_, s32[1,8]{1,0:T(1,128)S(1)} %copy-done.3), custom_call_target="tpu_custom_call", output_to_operand_aliasing={{}: (3, {})} | custom-call | tf_op jit(solution)/shard_map/place/pallas_call | solution.py:415
Async XLA Ops:
  0.0 0.9 %copy-start = (f32[1,1,3,5,4096]{4,1,3,2,0:T(1,128)S(1)}, f32[1,1,3,5,4096]{4,1,3,2,0:T(1,128)}, u32[]{:S(2)}) copy-start(f32[1,1,3,5,4096]{4,1,3,2,0:T(1,128)} %param.3) | copy-start | bytes 737284
  1.2 19.4 %copy-start.2 = (s32[1,1,3,6,2]{3,4,2,1,0:T(2,128)S(1)}, s32[1,1,3,6,2]{3,4,2,1,0:T(2,128)}, u32[]{:S(2)}) copy-start(s32[1,1,3,6,2]{3,4,2,1,0:T(2,128)} %param.4) | copy-start | bytes 436
  1.2 21.3 %collective-permute-start.1 = (f32[480,128]{1,0:T(8,128)S(1)}, f32[480,128]{1,0:T(8,128)S(1)}, u32[]{:S(2)}, u32[]{:S(2)}) collective-permute-start(f32[480,128]{1,0:T(8,128)S(1)} %get-tuple-element.18.own_faces), channel_id=1, source_target_pairs={{0,8},{8,16},{16,24},{24,32},{32,40},{40,48},{48,56},{56,64},{64,7... | collective-permute-start | bytes 737288 | tf_op jit(solution)/shard_map/ppermute | solution.py:437
  3.1 21.1 %collective-permute-start = (f32[480,128]{1,0:T(8,128)S(1)}, f32[480,128]{1,0:T(8,128)S(1)}, u32[]{:S(2)}, u32[]{:S(2)}) collective-permute-start(f32[480,128]{1,0:T(8,128)S(1)} %get-tuple-element.18.own_faces), channel_id=1, source_target_pairs={{8,0},{16,8},{24,16},{32,24},{40,32},{48,40},{56,48},{64,56},{72,6... | collective-permute-start | bytes 737288 | tf_op jit(solution)/shard_map/ppermute | solution.py:436
  20.5 3.7 %copy-start.1 = (f32[1,1,3,5,4096]{4,1,3,2,0:T(1,128)S(1)}, f32[1,1,3,5,4096]{4,1,3,2,0:T(1,128)}, u32[]{:S(2)}) copy-start(f32[1,1,3,5,4096]{4,1,3,2,0:T(1,128)} %param.3) | copy-start | bytes 737284
  24.9 12.5 %copy-start.3 = (s32[1,8]{1,0:T(1,128)S(1)}, s32[1,8]{1,0:T(1,128)}, u32[]{:S(2)}) copy-start(s32[1,8]{1,0:T(1,128)} %refs_4_.1) | copy-start | bytes 100
  24.9 13.8 %collective-permute-start.4 = (f32[160,128]{1,0:T(8,128)S(1)}, f32[160,128]{1,0:T(8,128)S(1)}, u32[]{:S(2)}, u32[]{:S(2)}) collective-permute-start(f32[160,128]{1,0:T(8,128)S(1)} %get-tuple-element.19), channel_id=1, source_target_pairs={{0,4},{1,5},{2,6},{3,7},{4,0},{5,1},{6,2},{7,3},{8,12},{9,13},{10,... | collective-permute-start | bytes 245768 | tf_op jit(solution)/shard_map/ppermute | solution.py:441
  32.3 8.1 %collective-permute-start.3 = (f32[160,128]{1,0:T(8,128)S(1)}, f32[160,128]{1,0:T(8,128)S(1)}, u32[]{:S(2)}, u32[]{:S(2)}) collective-permute-start(f32[160,128]{1,0:T(8,128)S(1)} %get-tuple-element.19), channel_id=1, source_target_pairs={{0,2},{1,3},{2,0},{3,1},{4,6},{5,7},{6,4},{7,5},{8,10},{9,11},{10,... | collective-permute-start | bytes 245768 | tf_op jit(solution)/shard_map/ppermute | solution.py:441
  34.8 6.5 %collective-permute-start.2 = (f32[160,128]{1,0:T(8,128)S(1)}, f32[160,128]{1,0:T(8,128)S(1)}, u32[]{:S(2)}, u32[]{:S(2)}) collective-permute-start(f32[160,128]{1,0:T(8,128)S(1)} %get-tuple-element.19), channel_id=1, source_target_pairs={{0,1},{1,0},{2,3},{3,2},{4,5},{5,4},{6,7},{7,6},{8,9},{9,8},{10,11... | collective-permute-start | bytes 245768 | tf_op jit(solution)/shard_map/ppermute | solution.py:441

commit v4 on v3

--- a/solution.py
+++ b/solution.py
@@ -12,8 +12,10 @@
 SLOTS = 3
 LANES = 128
 BLOCK_ROWS = 2 * EDGE * FIELDS
-FACE_ROWS = 3 * 4 * FIELDS * 8
 OUTER = (0, 1, EDGE - 1, EDGE - 2)
+
+ROW = 16
+RELAY = 5
 
 heat_ratio = 1.4
 courant = 0.07
@@ -38,11 +40,35 @@
     return slice(number * EDGE, (number + 1) * EDGE)
 
 
-def face_rows(axis, place, field):
-    base = axis * 4 * FIELDS * 8
-    if axis == 1:
-        return slice(base + (field * 2 + place) * EDGE, base + (field * 2 + place + 1) * EDGE)
-    return slice(base + (place * FIELDS + field) * 8, base + (place * FIELDS + field + 1) * 8)
+def face_planes(axis):
+    return [(field, place) for field in range(FIELDS) for place in range(2 if axis == 1 else 4)]
+
+
+def carried(axis, number):
+    return number % 4 == 3
+
+
+def face_rows(axis, number):
+    size = EDGE if axis == 1 else 8
+    base = (0, 15 * 8, 15 * 8 + 8 * EDGE)[axis] + (number - number // 4) * size
+    return slice(base, base + size)
+
+
+FACE_ROWS = 15 * 8 + 8 * EDGE + 15 * 8
+
+
+def face_plane(upright, turned, axis, field, place):
+    if axis == 0:
+        return upright[field, comb(OUTER[place]), :]
+    if axis == 2:
+        return turned[field, comb(OUTER[place]), :]
+    return jnp.where(lanes_of(EDGE) < 64, turned[field, band(place), :], turned[field, band(7 - place), :])
+
+
+def fourth_slot(axis):
+    if axis == 0:
+        return (lax.broadcasted_iota(jnp.int32, (8, LANES), 0) & 3) == 3
+    return ((lanes_of(EDGE if axis == 1 else 8) >> 4) & 3) == 3
 
 
 def lanes_of(rows):
@@ -68,17 +94,22 @@
                 upright[field, band(4 * half + slot), :] = value
                 if slot == SLOTS - 1:
                     upright[field, band(4 * half + slot + 1), :] = value
-    low_half = lanes_of(EDGE) < 64
     for field in range(FIELDS):
         turned[field] = upright[field].T
-    for field in range(FIELDS):
-        for place, number in enumerate(OUTER):
-            faces[face_rows(0, place, field), :] = upright[field, comb(number), :]
-            faces[face_rows(2, place, field), :] = turned[field, comb(number), :]
-        for depth in range(2):
-            faces[face_rows(1, depth, field), :] = jnp.where(
-                low_half, turned[field, band(depth), :], turned[field, band(7 - depth), :]
-            )
+    for axis in range(3):
+        planes = face_planes(axis)
+        fourth = fourth_slot(axis)
+        for number, (field, place) in enumerate(planes):
+            if carried(axis, number):
+                continue
+            value = face_plane(upright, turned, axis, field, place)
+            rider = number | 3
+            if rider < len(planes):
+                other = face_plane(upright, turned, axis, *planes[rider])
+                shift = 3 - number % 4
+                other = pltpu.roll(other, shift, 0) if axis == 0 else pltpu.roll(other, shift * EDGE, 1)
+                value = jnp.where(fourth, other, value)
+            faces[face_rows(axis, number), :] = value
 
 
 SQUARES = jax.ShapeDtypeStruct((FIELDS, LANES, LANES), jnp.float32)
@@ -291,6 +322,7 @@
     turned_change,
     codes,
     own_faces,
+    high_crossing,
     high_faces,
     low_faces,
     total,
@@ -300,13 +332,25 @@
     def ghost(group, axis, place, mirror, field):
         rows = 8 if axis != 1 else EDGE
         owner, source = codes[group, 0, 0:rows, :], codes[group, 1, 0:rows, :]
-        there = face_rows(axis, mirror, field)
-        low, own, high = (
-            jnp.take_along_axis(faces[there, :], source, axis=0 if axis == 0 else 1)
-            for faces in (low_faces, own_faces, high_faces)
-        )
-        neighbour = jnp.where(owner == 0, low, jnp.where(owner == 1, own, high))
-        return jnp.where(owner == 3, own_faces[face_rows(axis, place, field), :], neighbour)
+        number = face_planes(axis).index((field, mirror))
+
+        def fetch(stored, index):
+            there = face_rows(axis, stored)
+            above = high_faces[there, :] + high_crossing[there, :]
+            low, own, high = (
+                jnp.take_along_axis(values, index, axis=0 if axis == 0 else 1)
+                for values in (low_faces[there, :], own_faces[there, :], above)
+            )
+            return jnp.where(owner == 0, low, jnp.where(owner == 1, own, high))
+
+        if carried(axis, number):
+            slot = source & 3 if axis == 0 else (source >> 4) & 3
+            index = source | (3 if axis == 0 else 3 * EDGE)
+            first, second, third = (fetch(number - 3 + carrier, index) for carrier in range(3))
+            neighbour = jnp.where(slot == 0, first, jnp.where(slot == 1, second, third))
+        else:
+            neighbour = fetch(number, source)
+        return jnp.where(owner == 3, face_plane(upright, turned, axis, field, place), neighbour)
 
     low_half = lanes_of(EDGE) < 64
     for field in range(FIELDS):
@@ -373,11 +417,15 @@
     )(*operands)
 
 
-def finish_kernel(rounds, state, total, counts, out):
-    _, last_count, _ = final_counts(counts, lax.axis_index("sub"), rounds)
-    for slot, field, _, here, there in square_moves():
+def finish_kernel(rounds, state, total, counts, out, second, arrival):
+    _, last_count, arrival_round = final_counts(counts, lax.axis_index("sub"), rounds)
+    arrival[...] = jnp.full(arrival.shape, arrival_round, jnp.int32)
+    for slot, field, half, here, there in square_moves():
         fresh = state[here, :] - courant * total[field, there, :]
-        out[here, :] = jnp.where(slot < last_count, fresh, 0.0)
+        fresh = jnp.where(slot < last_count, fresh, 0.0)
+        out[here, :] = fresh
+        if slot == 1:
+            second[pl.ds(field * 2 * EDGE + half, EDGE, stride=2), :] = fresh
 
 
 def finish(state, total, counts, rounds):
@@ -385,9 +433,13 @@
     smem = pl.BlockSpec(memory_space=pltpu.SMEM)
     return pl.pallas_call(
         functools.partial(finish_kernel, rounds),
-        out_shape=jax.ShapeDtypeStruct(state.shape, jnp.float32),
+        out_shape=(
+            jax.ShapeDtypeStruct(state.shape, jnp.float32),
+            jax.ShapeDtypeStruct((BLOCK_ROWS, LANES), jnp.float32),
+            jax.ShapeDtypeStruct((8, LANES), jnp.int32),
+        ),
         in_specs=[vmem, vmem, smem],
-        out_specs=vmem,
+        out_specs=(vmem,) * 3,
         compiler_params=pltpu.CompilerParams(vmem_limit_bytes=VMEM_LIMIT),
         cost_estimate=pl.CostEstimate(flops=200_000, bytes_accessed=1_000_000, transcendentals=0),
         name="finish",
@@ -395,33 +447,36 @@
 
 
 def place_kernel(rounds, *refs):
-    arrived, (_, counts, out, sem) = refs[:rounds], refs[rounds:]
-    sub_index = lax.axis_index("sub")
-    _, _, arrival = final_counts(counts, sub_index, rounds)
-    for bit in range(rounds):
-
-        @pl.when(arrival == bit)
-        def _():
-            copy = pltpu.make_async_copy(arrived[bit], out.at[pl.ds(BLOCK_ROWS, BLOCK_ROWS)], sem)
-            copy.start()
-            copy.wait()
-
-
-def place(arrived, out, counts):
+    arrived, (second, arrival, _, out, block, sem) = refs[:rounds], refs[rounds:]
+    arrival_round = arrival[...]
+    for row in range(0, BLOCK_ROWS, 8):
+        rows = slice(row, row + 8)
+        value = second[rows, :]
+        for bit in range(rounds):
+            value = jnp.where(arrival_round == bit, arrived[bit][rows, :], value)
+        block[rows, :] = value
+    copy = pltpu.make_async_copy(block, out.at[pl.ds(BLOCK_ROWS, BLOCK_ROWS)], sem)
+    copy.start()
+    copy.wait()
+
+
+def place(arrived, out, second, arrival):
     rounds = len(arrived)
     vmem = pl.BlockSpec(memory_space=pltpu.VMEM)
-    smem = pl.BlockSpec(memory_space=pltpu.SMEM)
     anywhere = pl.BlockSpec(memory_space=pl.ANY)
     return pl.pallas_call(
         functools.partial(place_kernel, rounds),
         out_shape=jax.ShapeDtypeStruct(out.shape, out.dtype),
-        in_specs=[vmem] * rounds + [anywhere, smem],
+        in_specs=[vmem] * (rounds + 2) + [anywhere],
         out_specs=anywhere,
-        scratch_shapes=[pltpu.SemaphoreType.DMA],
-        input_output_aliases={rounds: 0},
+        scratch_shapes=[
+            pltpu.VMEM((BLOCK_ROWS, LANES), jnp.float32),
+            pltpu.SemaphoreType.DMA,
+        ],
+        input_output_aliases={rounds + 2: 0},
         compiler_params=pltpu.CompilerParams(vmem_limit_bytes=1024 * 1024),
         name="place",
-    )(*arrived, out, counts)
+    )(*arrived, second, arrival, out)
 
 
 def body(state, neighbours, counts):
@@ -432,19 +487,22 @@
     links = jnp.transpose(neighbours.reshape(SLOTS, 6, 2), (0, 2, 1))
     upright, turned, faces = prepare(state)
     forward = [(i, i + 1) for i in range(size - 1)]
-    backward = [(i + 1, i) for i in range(size - 1)]
+    firsts = range(ROW, size, ROW)
+    backward = [(i + 1, i) for i in range(size - 1) if i + 1 not in firsts]
+    low = lax.ppermute(faces, "blocks", forward)
     high = lax.ppermute(faces, "blocks", backward)
-    low = lax.ppermute(faces, "blocks", forward)
     changes = interior(upright, turned, links)
-    total, moved = outer(state, upright, turned, *changes, faces, high, low)
+    relayed = lax.ppermute(faces, "blocks", [(i, i - ROW + RELAY) for i in firsts])
+    crossing = lax.ppermute(relayed, "blocks", [(i - ROW + RELAY, i - 1) for i in firsts])
+    total, moved = outer(state, upright, turned, *changes, faces, crossing, high, low)
     arrived = [
         lax.ppermute(
             moved, "sub", [(s, s ^ (1 << bit)) for s in range(lax.axis_size("sub"))]
         )
         for bit in range(rounds)
     ]
-    out = finish(state, total, counts, rounds)
-    return place(arrived, out, counts).reshape(shape)
+    out, second, arrival = finish(state, total, counts, rounds)
+    return place(arrived, out, second, arrival).reshape(shape)
 
 
 def solution(mesh):

time: 42.2 us -> 40.7 us (0.964)
  starting transfers between devices: 31.8 us -> 24.3 us
  waiting for transfers between devices: 4.75 us -> 10.5 us
    ppermute x1, starting transfers between devices: 17.4 us -> 1.29 us  [body(): high = lax.ppermute(faces, 'blocks', backward)]
    ppermute x0 -> x2, starting transfers between devices: none -> 8.7 us  [the longest x1 8.03 us: body(): lax.ppermute(faces, 'blocks', [(i, i - ROW + RELAY) for i in firsts])]
    ppermute x1, waiting for transfers between devices: 0.41 us -> 7.89 us  [body(): low = lax.ppermute(faces, 'blocks', forward)]
    ppermute x1, waiting for transfers between devices: 1.76 us -> 0.01 us  [body(): high = lax.ppermute(faces, 'blocks', backward)]
  transfers between devices with their start and end apart: 5 -> 7, of which waited for: 4 -> 3; matrix products, arithmetic and copies ran while one was open for 0% -> 0% of each run, Pallas kernels for 7% -> 7%
where the time goes in v4:
time: 40.7 us; the launch traced here: 40.4 us
  starting transfers between devices  24.3 us (60%)
  waiting for transfers between devices  10.5 us (26%)
  Pallas kernels  4.48 us (11%)
  local copies, waits for them, and re-layouts  0.96 us (2%)
    ppermute x3, starting transfers between devices, body(): lax.ppermute(moved, 'sub', [(s, s ^ 1 << bit) for s in range(lax.axis_siz...  12.4 us
    ppermute x1, starting transfers between devices, body(): lax.ppermute(faces, 'blocks', [(i, i - ROW + RELAY) for i in firsts])  8.03 us
    ppermute x1, waiting for transfers between devices, body(): low = lax.ppermute(faces, 'blocks', forward)  7.89 us
    ppermute x3, waiting for transfers between devices, body(): lax.ppermute(moved, 'sub', [(s, s ^ 1 << bit) for s in range(lax.axis_siz...  2.57 us
    ppermute x1, starting transfers between devices, body(): low = lax.ppermute(faces, 'blocks', forward)  1.92 us
    pallas_call x1, Pallas kernels, interior(): pl.pallas_call(inner_kernel, out_shape=(SQUARES, SQUARES, jax.ShapeDtypeS...  1.49 us
    pallas_call x1, Pallas kernels, finish(): pl.pallas_call(functools.partial(finish_kernel, rounds), out_shape=(jax.S...  1.37 us
    ppermute x1, starting transfers between devices, body(): high = lax.ppermute(faces, 'blocks', backward)  1.29 us
  transfers between devices with their start and end apart: 7, of which 3 were waited for; matrix products, arithmetic and copies ran while one was open for 0% of the time, Pallas kernels for 7%

profile of v4, /device:TPU:112, one launch (start us, length us, event | category | flops | bytes accessed | tf_op | source)
XLA Modules:
  0.0 40.4 jit_solution(70673168276475167)
XLA Ops:
  0.0 0.0 copy-start
  0.0 0.9 %copy-done = f32[1,1,3,5,4096]{4,1,3,2,0:T(1,128)S(1)} copy-done((f32[1,1,3,5,4096]{4,1,3,2,0:T(1,128)S(1)}, f32[1,1,3,5,4096]{4,1,3,2,0:T(1,128)}, u32[]{:S(2)}) %copy-start) | copy-done | bytes 245784
  0.9 0.3 prepare.1
  1.2 0.0 copy-start.2
  1.2 8.0 %collective-permute-start = (f32[368,128]{1,0:T(8,128)S(1)}, f32[368,128]{1,0:T(8,128)S(1)}, u32[]{:S(2)}, u32[]{:S(2)}) collective-permute-start(f32[368,128]{1,0:T(8,128)S(1)} %get-tuple-element.21.own_faces), channel_id=1, source_target_pairs={{128,40},{256,168},{384,296},{512,424},{640,552},{768,680},{896,80... | collective-permute-start | bytes 565256 | tf_op jit(solution)/shard_map/ppermute | solution.py:495
  9.3 1.9 %collective-permute-start.3 = (f32[368,128]{1,0:T(8,128)S(1)}, f32[368,128]{1,0:T(8,128)S(1)}, u32[]{:S(2)}, u32[]{:S(2)}) collective-permute-start(f32[368,128]{1,0:T(8,128)S(1)} %get-tuple-element.21.own_faces), channel_id=1, source_target_pairs={{0,8},{8,16},{16,24},{24,32},{32,40},{40,48},{48,56},{56,64},{64,7... | collective-permute-start | bytes 565256 | tf_op jit(solution)/shard_map/ppermute | solution.py:492
  11.2 1.3 %collective-permute-start.2 = (f32[368,128]{1,0:T(8,128)S(1)}, f32[368,128]{1,0:T(8,128)S(1)}, u32[]{:S(2)}, u32[]{:S(2)}) collective-permute-start(f32[368,128]{1,0:T(8,128)S(1)} %get-tuple-element.21.own_faces), channel_id=1, source_target_pairs={{8,0},{16,8},{24,16},{32,24},{40,32},{48,40},{56,48},{64,56},{72,6... | collective-permute-start | bytes 565256 | tf_op jit(solution)/shard_map/ppermute | solution.py:493
  12.5 0.0 collective-permute-done
  12.5 0.7 %collective-permute-start.1 = (f32[368,128]{1,0:T(8,128)S(1)}, f32[368,128]{1,0:T(8,128)S(1)}, u32[]{:S(2)}, u32[]{:S(2)}) collective-permute-start(f32[368,128]{1,0:T(8,128)S(1)} %collective-permute-done), channel_id=1, source_target_pairs={{40,120},{168,248},{296,376},{424,504},{552,632},{680,760},{808,88... | collective-permute-start | bytes 565256 | tf_op jit(solution)/shard_map/ppermute | solution.py:496
  13.2 0.0 copy-done.2
  13.2 0.0 copy-start.1
  13.2 1.5 %interior.1 = (f32[5,128,128]{2,1,0:T(8,128)S(1)}, f32[5,128,128]{2,1,0:T(8,128)S(1)}, s32[5,2,16,128]{3,2,1,0:T(8,128)S(1)}) custom-call(f32[5,128,128]{2,1,0:T(8,128)S(1)} %get-tuple-element.16.upright, f32[5,128,128]{2,1,0:T(8,128)S(1)} %get-tuple-element.17.turned, s32[3,2,6]{2,1,0:T(2,128)S(1)} %bitcast.8), custom_call_target="tpu_custom_call" | custom-call | flops 6000000 | bytes 3000000 | tf_op jit(solution)/shard_map/interior/pallas_call | solution.py:263
  14.7 7.9 %collective-permute-done.3.low_faces = f32[368,128]{1,0:T(8,128)S(1)} collective-permute-done((f32[368,128]{1,0:T(8,128)S(1)}, f32[368,128]{1,0:T(8,128)S(1)}, u32[]{:S(2)}, u32[]{:S(2)}) %collective-permute-start.3) | collective-permute-done | bytes 188448 | tf_op jit(solution)/shard_map/ppermute | solution.py:492
  22.6 0.0 collective-permute-done.2.high_faces
  22.6 0.0 collective-permute-done.1.high_crossing
  22.6 0.0 copy-done.1
  22.6 0.7 %outer.1 = (f32[5,128,128]{2,1,0:T(8,128)S(1)}, f32[160,128]{1,0:T(8,128)S(1)}) custom-call(f32[480,128]{1,0:T(8,128)S(1)} %bitcast.6, f32[5,128,128]{2,1,0:T(8,128)S(1)} %get-tuple-element.16.upright, f32[5,128,128]{2,1,0:T(8,128)S(1)} %get-tuple-element.17.turned, f32[5,128,128]{2,1,0:T(8,128)S(1)} %get-tuple-element.18.up_change, ...), custom_call_target="tpu_custom_call" | custom-call | tf_op jit(solution)/shard_map/outer/pallas_call | solution.py:409
  23.3 0.0 copy-start.3
  23.3 7.4 %collective-permute-start.6 = (f32[160,128]{1,0:T(8,128)S(1)}, f32[160,128]{1,0:T(8,128)S(1)}, u32[]{:S(2)}, u32[]{:S(2)}) collective-permute-start(f32[160,128]{1,0:T(8,128)S(1)} %get-tuple-element.22), channel_id=1, source_target_pairs={{0,4},{1,5},{2,6},{3,7},{4,0},{5,1},{6,2},{7,3},{8,12},{9,13},{10,... | collective-permute-start | bytes 245768 | tf_op jit(solution)/shard_map/ppermute | solution.py:499
  30.7 2.5 %collective-permute-start.5 = (f32[160,128]{1,0:T(8,128)S(1)}, f32[160,128]{1,0:T(8,128)S(1)}, u32[]{:S(2)}, u32[]{:S(2)}) collective-permute-start(f32[160,128]{1,0:T(8,128)S(1)} %get-tuple-element.22), channel_id=1, source_target_pairs={{0,2},{1,3},{2,0},{3,1},{4,6},{5,7},{6,4},{7,5},{8,10},{9,11},{10,... | collective-permute-start | bytes 245768 | tf_op jit(solution)/shard_map/ppermute | solution.py:499
  33.3 2.5 %collective-permute-start.4 = (f32[160,128]{1,0:T(8,128)S(1)}, f32[160,128]{1,0:T(8,128)S(1)}, u32[]{:S(2)}, u32[]{:S(2)}) collective-permute-start(f32[160,128]{1,0:T(8,128)S(1)} %get-tuple-element.22), channel_id=1, source_target_pairs={{0,1},{1,0},{2,3},{3,2},{4,5},{5,4},{6,7},{7,6},{8,9},{9,8},{10,11... | collective-permute-start | bytes 245768 | tf_op jit(solution)/shard_map/ppermute | solution.py:499
  35.8 0.0 copy-done.3
  35.8 1.4 %finish.1 = (f32[480,128]{1,0:T(8,128)}, f32[160,128]{1,0:T(8,128)S(1)}, s32[8,128]{1,0:T(8,128)S(1)}) custom-call(f32[480,128]{1,0:T(8,128)S(1)} %bitcast.7, f32[5,128,128]{2,1,0:T(8,128)S(1)} %get-tuple-element.23.total, s32[1,8]{1,0:T(1,128)S(1)} %copy-done.3), custom_call_target="tpu_custom_call" | custom-call | flops 200000 | bytes 1000000 | tf_op jit(solution)/shard_map/finish/pallas_call | solution.py:434
  37.1 0.0 collective-permute-done.6.refs_2_
  37.2 1.7 %collective-permute-done.5.refs_1_ = f32[160,128]{1,0:T(8,128)S(1)} collective-permute-done((f32[160,128]{1,0:T(8,128)S(1)}, f32[160,128]{1,0:T(8,128)S(1)}, u32[]{:S(2)}, u32[]{:S(2)}) %collective-permute-start.5) | collective-permute-done | bytes 81952 | tf_op jit(solution)/shard_map/ppermute | solution.py:499
  38.9 0.9 %collective-permute-done.4.refs_0_ = f32[160,128]{1,0:T(8,128)S(1)} collective-permute-done((f32[160,128]{1,0:T(8,128)S(1)}, f32[160,128]{1,0:T(8,128)S(1)}, u32[]{:S(2)}, u32[]{:S(2)}) %collective-permute-start.4) | collective-permute-done | bytes 81952 | tf_op jit(solution)/shard_map/ppermute | solution.py:499
  39.7 0.7 %place.1 = f32[480,128]{1,0:T(8,128)} custom-call(f32[160,128]{1,0:T(8,128)S(1)} %collective-permute-done.4.refs_0_, f32[160,128]{1,0:T(8,128)S(1)} %collective-permute-done.5.refs_1_, f32[160,128]{1,0:T(8,128)S(1)} %collective-permute-done.6.refs_2_, f32[160,128]{1,0:T(8,128)S(1)} %get-tuple-element.24.refs_3_, ...), custom_call_target="tpu_custom_call", output_to_operand_aliasing={{}: (5, {})} | custom-call | tf_op jit(solution)/shard_map/place/pallas_call | solution.py:467
Async XLA Ops:
  0.0 0.9 %copy-start = (f32[1,1,3,5,4096]{4,1,3,2,0:T(1,128)S(1)}, f32[1,1,3,5,4096]{4,1,3,2,0:T(1,128)}, u32[]{:S(2)}) copy-start(f32[1,1,3,5,4096]{4,1,3,2,0:T(1,128)} %param.3) | copy-start | bytes 737284
  1.2 12.0 %copy-start.2 = (s32[1,1,3,6,2]{3,4,2,1,0:T(2,128)S(1)}, s32[1,1,3,6,2]{3,4,2,1,0:T(2,128)}, u32[]{:S(2)}) copy-start(s32[1,1,3,6,2]{3,4,2,1,0:T(2,128)} %param.4) | copy-start | bytes 436
  1.2 11.3 %collective-permute-start = (f32[368,128]{1,0:T(8,128)S(1)}, f32[368,128]{1,0:T(8,128)S(1)}, u32[]{:S(2)}, u32[]{:S(2)}) collective-permute-start(f32[368,128]{1,0:T(8,128)S(1)} %get-tuple-element.21.own_faces), channel_id=1, source_target_pairs={{128,40},{256,168},{384,296},{512,424},{640,552},{768,680},{896,80... | collective-permute-start | bytes 565256 | tf_op jit(solution)/shard_map/ppermute | solution.py:495
  9.3 13.3 %collective-permute-start.3 = (f32[368,128]{1,0:T(8,128)S(1)}, f32[368,128]{1,0:T(8,128)S(1)}, u32[]{:S(2)}, u32[]{:S(2)}) collective-permute-start(f32[368,128]{1,0:T(8,128)S(1)} %get-tuple-element.21.own_faces), channel_id=1, source_target_pairs={{0,8},{8,16},{16,24},{24,32},{32,40},{40,48},{48,56},{56,64},{64,7... | collective-permute-start | bytes 565256 | tf_op jit(solution)/shard_map/ppermute | solution.py:492
  11.2 11.4 %collective-permute-start.2 = (f32[368,128]{1,0:T(8,128)S(1)}, f32[368,128]{1,0:T(8,128)S(1)}, u32[]{:S(2)}, u32[]{:S(2)}) collective-permute-start(f32[368,128]{1,0:T(8,128)S(1)} %get-tuple-element.21.own_faces), channel_id=1, source_target_pairs={{8,0},{16,8},{24,16},{32,24},{40,32},{48,40},{56,48},{64,56},{72,6... | collective-permute-start | bytes 565256 | tf_op jit(solution)/shard_map/ppermute | solution.py:493
  12.5 10.1 %collective-permute-start.1 = (f32[368,128]{1,0:T(8,128)S(1)}, f32[368,128]{1,0:T(8,128)S(1)}, u32[]{:S(2)}, u32[]{:S(2)}) collective-permute-start(f32[368,128]{1,0:T(8,128)S(1)} %collective-permute-done), channel_id=1, source_target_pairs={{40,120},{168,248},{296,376},{424,504},{552,632},{680,760},{808,88... | collective-permute-start | bytes 565256 | tf_op jit(solution)/shard_map/ppermute | solution.py:496
  13.2 9.4 %copy-start.1 = (f32[1,1,3,5,4096]{4,1,3,2,0:T(1,128)S(1)}, f32[1,1,3,5,4096]{4,1,3,2,0:T(1,128)}, u32[]{:S(2)}) copy-start(f32[1,1,3,5,4096]{4,1,3,2,0:T(1,128)} %param.3) | copy-start | bytes 737284
  23.3 12.5 %copy-start.3 = (s32[1,8]{1,0:T(1,128)S(1)}, s32[1,8]{1,0:T(1,128)}, u32[]{:S(2)}) copy-start(s32[1,8]{1,0:T(1,128)} %counts.1) | copy-start | bytes 100
  23.3 13.8 %collective-permute-start.6 = (f32[160,128]{1,0:T(8,128)S(1)}, f32[160,128]{1,0:T(8,128)S(1)}, u32[]{:S(2)}, u32[]{:S(2)}) collective-permute-start(f32[160,128]{1,0:T(8,128)S(1)} %get-tuple-element.22), channel_id=1, source_target_pairs={{0,4},{1,5},{2,6},{3,7},{4,0},{5,1},{6,2},{7,3},{8,12},{9,13},{10,... | collective-permute-start | bytes 245768 | tf_op jit(solution)/shard_map/ppermute | solution.py:499
  30.7 8.1 %collective-permute-start.5 = (f32[160,128]{1,0:T(8,128)S(1)}, f32[160,128]{1,0:T(8,128)S(1)}, u32[]{:S(2)}, u32[]{:S(2)}) collective-permute-start(f32[160,128]{1,0:T(8,128)S(1)} %get-tuple-element.22), channel_id=1, source_target_pairs={{0,2},{1,3},{2,0},{3,1},{4,6},{5,7},{6,4},{7,5},{8,10},{9,11},{10,... | collective-permute-start | bytes 245768 | tf_op jit(solution)/shard_map/ppermute | solution.py:499
  33.3 6.5 %collective-permute-start.4 = (f32[160,128]{1,0:T(8,128)S(1)}, f32[160,128]{1,0:T(8,128)S(1)}, u32[]{:S(2)}, u32[]{:S(2)}) collective-permute-start(f32[160,128]{1,0:T(8,128)S(1)} %get-tuple-element.22), channel_id=1, source_target_pairs={{0,1},{1,0},{2,3},{3,2},{4,5},{5,4},{6,7},{7,6},{8,9},{9,8},{10,11... | collective-permute-start | bytes 245768 | tf_op jit(solution)/shard_map/ppermute | solution.py:499

commit v5 on v4

--- a/solution.py
+++ b/solution.py
@@ -15,7 +15,7 @@
 OUTER = (0, 1, EDGE - 1, EDGE - 2)
 
 ROW = 16
-RELAY = 5
+RELAY = 7
 
 heat_ratio = 1.4
 courant = 0.07
@@ -325,10 +325,14 @@
     high_crossing,
     high_faces,
     low_faces,
+    early_faces,
     total,
     moved,
     fixed,
 ):
+    block = lax.axis_index("blocks")
+    first_of_row = (block > 0) & (block % ROW == 0)
+
     def ghost(group, axis, place, mirror, field):
         rows = 8 if axis != 1 else EDGE
         owner, source = codes[group, 0, 0:rows, :], codes[group, 1, 0:rows, :]
@@ -337,9 +341,10 @@
         def fetch(stored, index):
             there = face_rows(axis, stored)
             above = high_faces[there, :] + high_crossing[there, :]
+            below = jnp.where(first_of_row, early_faces[there, :], low_faces[there, :])
             low, own, high = (
                 jnp.take_along_axis(values, index, axis=0 if axis == 0 else 1)
-                for values in (low_faces[there, :], own_faces[there, :], above)
+                for values in (below, own_faces[there, :], above)
             )
             return jnp.where(owner == 0, low, jnp.where(owner == 1, own, high))
 
@@ -486,15 +491,17 @@
     state = state.reshape(SLOTS * BLOCK_ROWS, LANES)
     links = jnp.transpose(neighbours.reshape(SLOTS, 6, 2), (0, 2, 1))
     upright, turned, faces = prepare(state)
-    forward = [(i, i + 1) for i in range(size - 1)]
     firsts = range(ROW, size, ROW)
+    forward = [(i, i + 1) for i in range(size - 1) if i + 1 not in firsts]
     backward = [(i + 1, i) for i in range(size - 1) if i + 1 not in firsts]
     low = lax.ppermute(faces, "blocks", forward)
     high = lax.ppermute(faces, "blocks", backward)
     changes = interior(upright, turned, links)
-    relayed = lax.ppermute(faces, "blocks", [(i, i - ROW + RELAY) for i in firsts])
-    crossing = lax.ppermute(relayed, "blocks", [(i - ROW + RELAY, i - 1) for i in firsts])
-    total, moved = outer(state, upright, turned, *changes, faces, crossing, high, low)
+    early = [(i, i - ROW + RELAY) for i in firsts] + [(i - 1, i) for i in firsts]
+    relayed = lax.ppermute(faces, "blocks", early)
+    held, *changes = lax.optimization_barrier((relayed, *changes))
+    crossing = lax.ppermute(held, "blocks", [(i - ROW + RELAY, i - 1) for i in firsts])
+    total, moved = outer(state, upright, turned, *changes, faces, crossing, high, low, relayed)
     arrived = [
         lax.ppermute(
             moved, "sub", [(s, s ^ (1 << bit)) for s in range(lax.axis_size("sub"))]

time: 40.7 us -> 40.1 us (0.985)
  waiting for transfers between devices: 10.5 us -> 7.76 us
  starting transfers between devices: 24.3 us -> 26.4 us
    ppermute x1, waiting for transfers between devices: 7.89 us -> 0.01 us  [body(): low = lax.ppermute(faces, 'blocks', forward)]
    ppermute x2, waiting for transfers between devices: 0.01 us -> 5.18 us  [the longest x1 5.18 us: body(): relayed = lax.ppermute(faces, 'blocks', early)]
    ppermute x2, starting transfers between devices: 8.7 us -> 11.4 us  [the longest x1 10.7 us: body(): relayed = lax.ppermute(faces, 'blocks', early)]
    ppermute x1, starting transfers between devices: 1.92 us -> 1.3 us  [body(): low = lax.ppermute(faces, 'blocks', forward)]
where the time goes in v5:
time: 40.1 us; the launch traced here: 39.8 us
  starting transfers between devices  26.4 us (66%)
  waiting for transfers between devices  7.76 us (19%)
  Pallas kernels  4.49 us (11%)
  local copies, waits for them, and re-layouts  0.96 us (2%)
    ppermute x3, starting transfers between devices, body(): lax.ppermute(moved, 'sub', [(s, s ^ 1 << bit) for s in range(lax.axis_siz...  12.4 us
    ppermute x1, starting transfers between devices, body(): relayed = lax.ppermute(faces, 'blocks', early)  10.7 us
    ppermute x1, waiting for transfers between devices, body(): relayed = lax.ppermute(faces, 'blocks', early)  5.18 us
    ppermute x3, waiting for transfers between devices, body(): lax.ppermute(moved, 'sub', [(s, s ^ 1 << bit) for s in range(lax.axis_siz...  2.57 us
    pallas_call x1, Pallas kernels, interior(): pl.pallas_call(inner_kernel, out_shape=(SQUARES, SQUARES, jax.ShapeDtypeS...  1.49 us
    pallas_call x1, Pallas kernels, finish(): pl.pallas_call(functools.partial(finish_kernel, rounds), out_shape=(jax.S...  1.37 us
    ppermute x1, starting transfers between devices, body(): low = lax.ppermute(faces, 'blocks', forward)  1.3 us
    ppermute x1, starting transfers between devices, body(): high = lax.ppermute(faces, 'blocks', backward)  1.29 us
  transfers between devices with their start and end apart: 7, of which 3 were waited for; matrix products, arithmetic and copies ran while one was open for 0% of the time, Pallas kernels for 7%

profile of v5, /device:TPU:112, one launch (start us, length us, event | category | flops | bytes accessed | tf_op | source)
XLA Modules:
  0.0 39.8 jit_solution(5881296678362431724)
XLA Ops:
  0.0 0.0 copy-start
  0.0 0.9 %copy-done = f32[1,1,3,5,4096]{4,1,3,2,0:T(1,128)S(1)} copy-done((f32[1,1,3,5,4096]{4,1,3,2,0:T(1,128)S(1)}, f32[1,1,3,5,4096]{4,1,3,2,0:T(1,128)}, u32[]{:S(2)}) %copy-start) | copy-done | bytes 245784
  0.9 0.3 prepare.1
  1.2 0.0 copy-start.2
  1.2 10.7 %collective-permute-start = (f32[368,128]{1,0:T(8,128)S(1)}, f32[368,128]{1,0:T(8,128)S(1)}, u32[]{:S(2)}, u32[]{:S(2)}) collective-permute-start(f32[368,128]{1,0:T(8,128)S(1)} %get-tuple-element.22.own_faces), channel_id=1, source_target_pairs={{128,56},{256,184},{384,312},{512,440},{640,568},{768,696},{896,82... | collective-permute-start | bytes 565256 | tf_op jit(solution)/shard_map/ppermute | solution.py:501
  12.0 1.3 %collective-permute-start.3 = (f32[368,128]{1,0:T(8,128)S(1)}, f32[368,128]{1,0:T(8,128)S(1)}, u32[]{:S(2)}, u32[]{:S(2)}) collective-permute-start(f32[368,128]{1,0:T(8,128)S(1)} %get-tuple-element.22.own_faces), channel_id=1, source_target_pairs={{0,8},{8,16},{16,24},{24,32},{32,40},{40,48},{48,56},{56,64},{64,7... | collective-permute-start | bytes 565256 | tf_op jit(solution)/shard_map/ppermute | solution.py:497
  13.3 1.3 %collective-permute-start.2 = (f32[368,128]{1,0:T(8,128)S(1)}, f32[368,128]{1,0:T(8,128)S(1)}, u32[]{:S(2)}, u32[]{:S(2)}) collective-permute-start(f32[368,128]{1,0:T(8,128)S(1)} %get-tuple-element.22.own_faces), channel_id=1, source_target_pairs={{8,0},{16,8},{24,16},{32,24},{40,32},{48,40},{56,48},{64,56},{72,6... | collective-permute-start | bytes 565256 | tf_op jit(solution)/shard_map/ppermute | solution.py:498
  14.6 0.0 copy-done.2
  14.6 0.0 copy-start.1
  14.6 1.5 %interior.1 = (f32[5,128,128]{2,1,0:T(8,128)S(1)}, f32[5,128,128]{2,1,0:T(8,128)S(1)}, s32[5,2,16,128]{3,2,1,0:T(8,128)S(1)}) custom-call(f32[5,128,128]{2,1,0:T(8,128)S(1)} %get-tuple-element.20.upright, f32[5,128,128]{2,1,0:T(8,128)S(1)} %get-tuple-element.21.turned, s32[3,2,6]{2,1,0:T(2,128)S(1)} %bitcast.8), custom_call_target="tpu_custom_call" | custom-call | flops 6000000 | bytes 3000000 | tf_op jit(solution)/shard_map/interior/pallas_call | solution.py:263
  16.1 5.2 %collective-permute-done.early_faces = f32[368,128]{1,0:T(8,128)S(1)} collective-permute-done((f32[368,128]{1,0:T(8,128)S(1)}, f32[368,128]{1,0:T(8,128)S(1)}, u32[]{:S(2)}, u32[]{:S(2)}) %collective-permute-start) | collective-permute-done | bytes 188448 | tf_op jit(solution)/shard_map/ppermute | solution.py:501
  21.3 0.7 %collective-permute-start.1 = (f32[368,128]{1,0:T(8,128)S(1)}, f32[368,128]{1,0:T(8,128)S(1)}, u32[]{:S(2)}, u32[]{:S(2)}) collective-permute-start(f32[368,128]{1,0:T(8,128)S(1)} %collective-permute-done.early_faces), channel_id=1, source_target_pairs={{56,120},{184,248},{312,376},{440,504},{568,632},{696,760},{824,88... | collective-permute-start | bytes 565256 | tf_op jit(solution)/shard_map/ppermute | solution.py:503
  22.0 0.0 collective-permute-done.3.low_faces
  22.0 0.0 collective-permute-done.2.high_faces
  22.0 0.0 collective-permute-done.1.high_crossing
  22.0 0.0 copy-done.1
  22.0 0.7 %outer.1 = (f32[5,128,128]{2,1,0:T(8,128)S(1)}, f32[160,128]{1,0:T(8,128)S(1)}) custom-call(f32[480,128]{1,0:T(8,128)S(1)} %bitcast.6, f32[5,128,128]{2,1,0:T(8,128)S(1)} %get-tuple-element.20.upright, f32[5,128,128]{2,1,0:T(8,128)S(1)} %get-tuple-element.21.turned, f32[5,128,128]{2,1,0:T(8,128)S(1)} %get-tuple-element.26.up_change, ...), custom_call_target="tpu_custom_call" | custom-call | tf_op jit(solution)/shard_map/outer/pallas_call | solution.py:414
  22.7 0.0 copy-start.3
  22.7 7.4 %collective-permute-start.6 = (f32[160,128]{1,0:T(8,128)S(1)}, f32[160,128]{1,0:T(8,128)S(1)}, u32[]{:S(2)}, u32[]{:S(2)}) collective-permute-start(f32[160,128]{1,0:T(8,128)S(1)} %get-tuple-element.30), channel_id=1, source_target_pairs={{0,4},{1,5},{2,6},{3,7},{4,0},{5,1},{6,2},{7,3},{8,12},{9,13},{10,... | collective-permute-start | bytes 245768 | tf_op jit(solution)/shard_map/ppermute | solution.py:506
  30.1 2.5 %collective-permute-start.5 = (f32[160,128]{1,0:T(8,128)S(1)}, f32[160,128]{1,0:T(8,128)S(1)}, u32[]{:S(2)}, u32[]{:S(2)}) collective-permute-start(f32[160,128]{1,0:T(8,128)S(1)} %get-tuple-element.30), channel_id=1, source_target_pairs={{0,2},{1,3},{2,0},{3,1},{4,6},{5,7},{6,4},{7,5},{8,10},{9,11},{10,... | collective-permute-start | bytes 245768 | tf_op jit(solution)/shard_map/ppermute | solution.py:506
  32.7 2.5 %collective-permute-start.4 = (f32[160,128]{1,0:T(8,128)S(1)}, f32[160,128]{1,0:T(8,128)S(1)}, u32[]{:S(2)}, u32[]{:S(2)}) collective-permute-start(f32[160,128]{1,0:T(8,128)S(1)} %get-tuple-element.30), channel_id=1, source_target_pairs={{0,1},{1,0},{2,3},{3,2},{4,5},{5,4},{6,7},{7,6},{8,9},{9,8},{10,11... | collective-permute-start | bytes 245768 | tf_op jit(solution)/shard_map/ppermute | solution.py:506
  35.2 0.0 copy-done.3
  35.2 1.4 %finish.1 = (f32[480,128]{1,0:T(8,128)}, f32[160,128]{1,0:T(8,128)S(1)}, s32[8,128]{1,0:T(8,128)S(1)}) custom-call(f32[480,128]{1,0:T(8,128)S(1)} %bitcast.7, f32[5,128,128]{2,1,0:T(8,128)S(1)} %get-tuple-element.31.total, s32[1,8]{1,0:T(1,128)S(1)} %copy-done.3), custom_call_target="tpu_custom_call" | custom-call | flops 200000 | bytes 1000000 | tf_op jit(solution)/shard_map/finish/pallas_call | solution.py:439
  36.5 0.0 collective-permute-done.6.refs_2_
  36.5 1.7 %collective-permute-done.5.refs_1_ = f32[160,128]{1,0:T(8,128)S(1)} collective-permute-done((f32[160,128]{1,0:T(8,128)S(1)}, f32[160,128]{1,0:T(8,128)S(1)}, u32[]{:S(2)}, u32[]{:S(2)}) %collective-permute-start.5) | collective-permute-done | bytes 81952 | tf_op jit(solution)/shard_map/ppermute | solution.py:506
  38.2 0.9 %collective-permute-done.4.refs_0_ = f32[160,128]{1,0:T(8,128)S(1)} collective-permute-done((f32[160,128]{1,0:T(8,128)S(1)}, f32[160,128]{1,0:T(8,128)S(1)}, u32[]{:S(2)}, u32[]{:S(2)}) %collective-permute-start.4) | collective-permute-done | bytes 81952 | tf_op jit(solution)/shard_map/ppermute | solution.py:506
  39.1 0.7 %place.1 = f32[480,128]{1,0:T(8,128)} custom-call(f32[160,128]{1,0:T(8,128)S(1)} %collective-permute-done.4.refs_0_, f32[160,128]{1,0:T(8,128)S(1)} %collective-permute-done.5.refs_1_, f32[160,128]{1,0:T(8,128)S(1)} %collective-permute-done.6.refs_2_, f32[160,128]{1,0:T(8,128)S(1)} %get-tuple-element.32.refs_3_, ...), custom_call_target="tpu_custom_call", output_to_operand_aliasing={{}: (5, {})} | custom-call | tf_op jit(solution)/shard_map/place/pallas_call | solution.py:472
Async XLA Ops:
  0.0 0.9 %copy-start = (f32[1,1,3,5,4096]{4,1,3,2,0:T(1,128)S(1)}, f32[1,1,3,5,4096]{4,1,3,2,0:T(1,128)}, u32[]{:S(2)}) copy-start(f32[1,1,3,5,4096]{4,1,3,2,0:T(1,128)} %param.3) | copy-start | bytes 737284
  1.2 13.4 %copy-start.2 = (s32[1,1,3,6,2]{3,4,2,1,0:T(2,128)S(1)}, s32[1,1,3,6,2]{3,4,2,1,0:T(2,128)}, u32[]{:S(2)}) copy-start(s32[1,1,3,6,2]{3,4,2,1,0:T(2,128)} %param.4) | copy-start | bytes 436
  1.2 20.1 %collective-permute-start = (f32[368,128]{1,0:T(8,128)S(1)}, f32[368,128]{1,0:T(8,128)S(1)}, u32[]{:S(2)}, u32[]{:S(2)}) collective-permute-start(f32[368,128]{1,0:T(8,128)S(1)} %get-tuple-element.22.own_faces), channel_id=1, source_target_pairs={{128,56},{256,184},{384,312},{512,440},{640,568},{768,696},{896,82... | collective-permute-start | bytes 565256 | tf_op jit(solution)/shard_map/ppermute | solution.py:501
  12.0 10.0 %collective-permute-start.3 = (f32[368,128]{1,0:T(8,128)S(1)}, f32[368,128]{1,0:T(8,128)S(1)}, u32[]{:S(2)}, u32[]{:S(2)}) collective-permute-start(f32[368,128]{1,0:T(8,128)S(1)} %get-tuple-element.22.own_faces), channel_id=1, source_target_pairs={{0,8},{8,16},{16,24},{24,32},{32,40},{40,48},{48,56},{56,64},{64,7... | collective-permute-start | bytes 565256 | tf_op jit(solution)/shard_map/ppermute | solution.py:497
  13.3 8.7 %collective-permute-start.2 = (f32[368,128]{1,0:T(8,128)S(1)}, f32[368,128]{1,0:T(8,128)S(1)}, u32[]{:S(2)}, u32[]{:S(2)}) collective-permute-start(f32[368,128]{1,0:T(8,128)S(1)} %get-tuple-element.22.own_faces), channel_id=1, source_target_pairs={{8,0},{16,8},{24,16},{32,24},{40,32},{48,40},{56,48},{64,56},{72,6... | collective-permute-start | bytes 565256 | tf_op jit(solution)/shard_map/ppermute | solution.py:498
  14.6 7.4 %copy-start.1 = (f32[1,1,3,5,4096]{4,1,3,2,0:T(1,128)S(1)}, f32[1,1,3,5,4096]{4,1,3,2,0:T(1,128)}, u32[]{:S(2)}) copy-start(f32[1,1,3,5,4096]{4,1,3,2,0:T(1,128)} %param.3) | copy-start | bytes 737284
  21.3 0.7 %collective-permute-start.1 = (f32[368,128]{1,0:T(8,128)S(1)}, f32[368,128]{1,0:T(8,128)S(1)}, u32[]{:S(2)}, u32[]{:S(2)}) collective-permute-start(f32[368,128]{1,0:T(8,128)S(1)} %collective-permute-done.early_faces), channel_id=1, source_target_pairs={{56,120},{184,248},{312,376},{440,504},{568,632},{696,760},{824,88... | collective-permute-start | bytes 565256 | tf_op jit(solution)/shard_map/ppermute | solution.py:503
  22.7 12.5 %copy-start.3 = (s32[1,8]{1,0:T(1,128)S(1)}, s32[1,8]{1,0:T(1,128)}, u32[]{:S(2)}) copy-start(s32[1,8]{1,0:T(1,128)} %counts.1) | copy-start | bytes 100
  22.7 13.8 %collective-permute-start.6 = (f32[160,128]{1,0:T(8,128)S(1)}, f32[160,128]{1,0:T(8,128)S(1)}, u32[]{:S(2)}, u32[]{:S(2)}) collective-permute-start(f32[160,128]{1,0:T(8,128)S(1)} %get-tuple-element.30), channel_id=1, source_target_pairs={{0,4},{1,5},{2,6},{3,7},{4,0},{5,1},{6,2},{7,3},{8,12},{9,13},{10,... | collective-permute-start | bytes 245768 | tf_op jit(solution)/shard_map/ppermute | solution.py:506
  30.1 8.1 %collective-permute-start.5 = (f32[160,128]{1,0:T(8,128)S(1)}, f32[160,128]{1,0:T(8,128)S(1)}, u32[]{:S(2)}, u32[]{:S(2)}) collective-permute-start(f32[160,128]{1,0:T(8,128)S(1)} %get-tuple-element.30), channel_id=1, source_target_pairs={{0,2},{1,3},{2,0},{3,1},{4,6},{5,7},{6,4},{7,5},{8,10},{9,11},{10,... | collective-permute-start | bytes 245768 | tf_op jit(solution)/shard_map/ppermute | solution.py:506
  32.7 6.5 %collective-permute-start.4 = (f32[160,128]{1,0:T(8,128)S(1)}, f32[160,128]{1,0:T(8,128)S(1)}, u32[]{:S(2)}, u32[]{:S(2)}) collective-permute-start(f32[160,128]{1,0:T(8,128)S(1)} %get-tuple-element.30), channel_id=1, source_target_pairs={{0,1},{1,0},{2,3},{3,2},{4,5},{5,4},{6,7},{7,6},{8,9},{9,8},{10,11... | collective-permute-start | bytes 245768 | tf_op jit(solution)/shard_map/ppermute | solution.py:506

commit v6 on v5

--- a/solution.py
+++ b/solution.py
@@ -14,6 +14,7 @@
 BLOCK_ROWS = 2 * EDGE * FIELDS
 OUTER = (0, 1, EDGE - 1, EDGE - 2)
 
+SEND_ORDER = (0, 2, 1)
 ROW = 16
 RELAY = 7
 
@@ -453,6 +454,7 @@
 
 def place_kernel(rounds, *refs):
     arrived, (second, arrival, _, out, block, sem) = refs[:rounds], refs[rounds:]
+    arrived = dict(zip(SEND_ORDER, arrived))
     arrival_round = arrival[...]
     for row in range(0, BLOCK_ROWS, 8):
         rows = slice(row, row + 8)
@@ -481,7 +483,7 @@
         input_output_aliases={rounds + 2: 0},
         compiler_params=pltpu.CompilerParams(vmem_limit_bytes=1024 * 1024),
         name="place",
-    )(*arrived, second, arrival, out)
+    )(*arrived.values(), second, arrival, out)
 
 
 def body(state, neighbours, counts):
@@ -502,12 +504,12 @@
     held, *changes = lax.optimization_barrier((relayed, *changes))
     crossing = lax.ppermute(held, "blocks", [(i - ROW + RELAY, i - 1) for i in firsts])
     total, moved = outer(state, upright, turned, *changes, faces, crossing, high, low, relayed)
-    arrived = [
-        lax.ppermute(
+    arrived = {
+        bit: lax.ppermute(
             moved, "sub", [(s, s ^ (1 << bit)) for s in range(lax.axis_size("sub"))]
         )
-        for bit in range(rounds)
-    ]
+        for bit in SEND_ORDER
+    }
     out, second, arrival = finish(state, total, counts, rounds)
     return place(arrived, out, second, arrival).reshape(shape)
 

time: 40.1 us -> 39.9 us (level)
  no operation moved by 1% of the time
where the time goes in v6:
time: 39.9 us; the launch traced here: 39.7 us
  starting transfers between devices  26.4 us (66%)
  waiting for transfers between devices  7.64 us (19%)
  Pallas kernels  4.49 us (11%)
  local copies, waits for them, and re-layouts  0.96 us (2%)
    ppermute x3, starting transfers between devices, body(): lax.ppermute(moved, 'sub', [(s, s ^ 1 << bit) for s in range(lax.axis_siz...  12.4 us
    ppermute x1, starting transfers between devices, body(): relayed = lax.ppermute(faces, 'blocks', early)  10.7 us
    ppermute x1, waiting for transfers between devices, body(): relayed = lax.ppermute(faces, 'blocks', early)  5.18 us
    ppermute x3, waiting for transfers between devices, body(): lax.ppermute(moved, 'sub', [(s, s ^ 1 << bit) for s in range(lax.axis_siz...  2.45 us
    pallas_call x1, Pallas kernels, interior(): pl.pallas_call(inner_kernel, out_shape=(SQUARES, SQUARES, jax.ShapeDtypeS...  1.49 us
    pallas_call x1, Pallas kernels, finish(): pl.pallas_call(functools.partial(finish_kernel, rounds), out_shape=(jax.S...  1.37 us
    ppermute x1, starting transfers between devices, body(): low = lax.ppermute(faces, 'blocks', forward)  1.3 us
    ppermute x1, starting transfers between devices, body(): high = lax.ppermute(faces, 'blocks', backward)  1.29 us
  transfers between devices with their start and end apart: 7, of which 3 were waited for; matrix products, arithmetic and copies ran while one was open for 0% of the time, Pallas kernels for 7%

profile of v6, /device:TPU:112, one launch (start us, length us, event | category | flops | bytes accessed | tf_op | source)
XLA Modules:
  0.0 39.7 jit_solution(12859318639686341241)
XLA Ops:
  0.0 0.0 copy-start
  0.0 0.9 %copy-done = f32[1,1,3,5,4096]{4,1,3,2,0:T(1,128)S(1)} copy-done((f32[1,1,3,5,4096]{4,1,3,2,0:T(1,128)S(1)}, f32[1,1,3,5,4096]{4,1,3,2,0:T(1,128)}, u32[]{:S(2)}) %copy-start) | copy-done | bytes 245784
  0.9 0.3 prepare.1
  1.2 0.0 copy-start.2
  1.2 10.7 %collective-permute-start = (f32[368,128]{1,0:T(8,128)S(1)}, f32[368,128]{1,0:T(8,128)S(1)}, u32[]{:S(2)}, u32[]{:S(2)}) collective-permute-start(f32[368,128]{1,0:T(8,128)S(1)} %get-tuple-element.22.own_faces), channel_id=1, source_target_pairs={{128,56},{256,184},{384,312},{512,440},{640,568},{768,696},{896,82... | collective-permute-start | bytes 565256 | tf_op jit(solution)/shard_map/ppermute | solution.py:503
  12.0 1.3 %collective-permute-start.3 = (f32[368,128]{1,0:T(8,128)S(1)}, f32[368,128]{1,0:T(8,128)S(1)}, u32[]{:S(2)}, u32[]{:S(2)}) collective-permute-start(f32[368,128]{1,0:T(8,128)S(1)} %get-tuple-element.22.own_faces), channel_id=1, source_target_pairs={{0,8},{8,16},{16,24},{24,32},{32,40},{40,48},{48,56},{56,64},{64,7... | collective-permute-start | bytes 565256 | tf_op jit(solution)/shard_map/ppermute | solution.py:499
  13.3 1.3 %collective-permute-start.2 = (f32[368,128]{1,0:T(8,128)S(1)}, f32[368,128]{1,0:T(8,128)S(1)}, u32[]{:S(2)}, u32[]{:S(2)}) collective-permute-start(f32[368,128]{1,0:T(8,128)S(1)} %get-tuple-element.22.own_faces), channel_id=1, source_target_pairs={{8,0},{16,8},{24,16},{32,24},{40,32},{48,40},{56,48},{64,56},{72,6... | collective-permute-start | bytes 565256 | tf_op jit(solution)/shard_map/ppermute | solution.py:500
  14.6 0.0 copy-done.2
  14.6 0.0 copy-start.1
  14.6 1.5 %interior.1 = (f32[5,128,128]{2,1,0:T(8,128)S(1)}, f32[5,128,128]{2,1,0:T(8,128)S(1)}, s32[5,2,16,128]{3,2,1,0:T(8,128)S(1)}) custom-call(f32[5,128,128]{2,1,0:T(8,128)S(1)} %get-tuple-element.20.upright, f32[5,128,128]{2,1,0:T(8,128)S(1)} %get-tuple-element.21.turned, s32[3,2,6]{2,1,0:T(2,128)S(1)} %bitcast.8), custom_call_target="tpu_custom_call" | custom-call | flops 6000000 | bytes 3000000 | tf_op jit(solution)/shard_map/interior/pallas_call | solution.py:264
  16.1 5.2 %collective-permute-done.early_faces = f32[368,128]{1,0:T(8,128)S(1)} collective-permute-done((f32[368,128]{1,0:T(8,128)S(1)}, f32[368,128]{1,0:T(8,128)S(1)}, u32[]{:S(2)}, u32[]{:S(2)}) %collective-permute-start) | collective-permute-done | bytes 188448 | tf_op jit(solution)/shard_map/ppermute | solution.py:503
  21.3 0.7 %collective-permute-start.1 = (f32[368,128]{1,0:T(8,128)S(1)}, f32[368,128]{1,0:T(8,128)S(1)}, u32[]{:S(2)}, u32[]{:S(2)}) collective-permute-start(f32[368,128]{1,0:T(8,128)S(1)} %collective-permute-done.early_faces), channel_id=1, source_target_pairs={{56,120},{184,248},{312,376},{440,504},{568,632},{696,760},{824,88... | collective-permute-start | bytes 565256 | tf_op jit(solution)/shard_map/ppermute | solution.py:505
  22.0 0.0 collective-permute-done.3.low_faces
  22.0 0.0 collective-permute-done.2.high_faces
  22.0 0.0 collective-permute-done.1.high_crossing
  22.0 0.0 copy-done.1
  22.0 0.7 %outer.1 = (f32[5,128,128]{2,1,0:T(8,128)S(1)}, f32[160,128]{1,0:T(8,128)S(1)}) custom-call(f32[480,128]{1,0:T(8,128)S(1)} %bitcast.6, f32[5,128,128]{2,1,0:T(8,128)S(1)} %get-tuple-element.20.upright, f32[5,128,128]{2,1,0:T(8,128)S(1)} %get-tuple-element.21.turned, f32[5,128,128]{2,1,0:T(8,128)S(1)} %get-tuple-element.26.up_change, ...), custom_call_target="tpu_custom_call" | custom-call | tf_op jit(solution)/shard_map/outer/pallas_call | solution.py:415
  22.7 0.0 copy-start.3
  22.7 4.3 %collective-permute-start.6 = (f32[160,128]{1,0:T(8,128)S(1)}, f32[160,128]{1,0:T(8,128)S(1)}, u32[]{:S(2)}, u32[]{:S(2)}) collective-permute-start(f32[160,128]{1,0:T(8,128)S(1)} %get-tuple-element.30), channel_id=1, source_target_pairs={{0,2},{1,3},{2,0},{3,1},{4,6},{5,7},{6,4},{7,5},{8,10},{9,11},{10,... | collective-permute-start | bytes 245768 | tf_op jit(solution)/shard_map/ppermute | solution.py:508
  27.1 5.6 %collective-permute-start.5 = (f32[160,128]{1,0:T(8,128)S(1)}, f32[160,128]{1,0:T(8,128)S(1)}, u32[]{:S(2)}, u32[]{:S(2)}) collective-permute-start(f32[160,128]{1,0:T(8,128)S(1)} %get-tuple-element.30), channel_id=1, source_target_pairs={{0,4},{1,5},{2,6},{3,7},{4,0},{5,1},{6,2},{7,3},{8,12},{9,13},{10,... | collective-permute-start | bytes 245768 | tf_op jit(solution)/shard_map/ppermute | solution.py:508
  32.7 2.5 %collective-permute-start.4 = (f32[160,128]{1,0:T(8,128)S(1)}, f32[160,128]{1,0:T(8,128)S(1)}, u32[]{:S(2)}, u32[]{:S(2)}) collective-permute-start(f32[160,128]{1,0:T(8,128)S(1)} %get-tuple-element.30), channel_id=1, source_target_pairs={{0,1},{1,0},{2,3},{3,2},{4,5},{5,4},{6,7},{7,6},{8,9},{9,8},{10,11... | collective-permute-start | bytes 245768 | tf_op jit(solution)/shard_map/ppermute | solution.py:508
  35.2 0.0 copy-done.3
  35.2 1.4 %finish.1 = (f32[480,128]{1,0:T(8,128)}, f32[160,128]{1,0:T(8,128)S(1)}, s32[8,128]{1,0:T(8,128)S(1)}) custom-call(f32[480,128]{1,0:T(8,128)S(1)} %bitcast.7, f32[5,128,128]{2,1,0:T(8,128)S(1)} %get-tuple-element.31.total, s32[1,8]{1,0:T(1,128)S(1)} %copy-done.3), custom_call_target="tpu_custom_call" | custom-call | flops 200000 | bytes 1000000 | tf_op jit(solution)/shard_map/finish/pallas_call | solution.py:440
  36.5 0.0 collective-permute-done.6.refs_2_
  36.5 0.8 %collective-permute-done.5.refs_1_ = f32[160,128]{1,0:T(8,128)S(1)} collective-permute-done((f32[160,128]{1,0:T(8,128)S(1)}, f32[160,128]{1,0:T(8,128)S(1)}, u32[]{:S(2)}, u32[]{:S(2)}) %collective-permute-start.5) | collective-permute-done | bytes 81952 | tf_op jit(solution)/shard_map/ppermute | solution.py:508
  37.3 1.7 %collective-permute-done.4.refs_0_ = f32[160,128]{1,0:T(8,128)S(1)} collective-permute-done((f32[160,128]{1,0:T(8,128)S(1)}, f32[160,128]{1,0:T(8,128)S(1)}, u32[]{:S(2)}, u32[]{:S(2)}) %collective-permute-start.4) | collective-permute-done | bytes 81952 | tf_op jit(solution)/shard_map/ppermute | solution.py:508
  39.0 0.7 %place.1 = f32[480,128]{1,0:T(8,128)} custom-call(f32[160,128]{1,0:T(8,128)S(1)} %collective-permute-done.4.refs_0_, f32[160,128]{1,0:T(8,128)S(1)} %collective-permute-done.5.refs_1_, f32[160,128]{1,0:T(8,128)S(1)} %collective-permute-done.6.refs_2_, f32[160,128]{1,0:T(8,128)S(1)} %get-tuple-element.32.refs_3_, ...), custom_call_target="tpu_custom_call", output_to_operand_aliasing={{}: (5, {})} | custom-call | tf_op jit(solution)/shard_map/place/pallas_call | solution.py:474
Async XLA Ops:
  0.0 0.9 %copy-start = (f32[1,1,3,5,4096]{4,1,3,2,0:T(1,128)S(1)}, f32[1,1,3,5,4096]{4,1,3,2,0:T(1,128)}, u32[]{:S(2)}) copy-start(f32[1,1,3,5,4096]{4,1,3,2,0:T(1,128)} %param.3) | copy-start | bytes 737284
  1.2 13.4 %copy-start.2 = (s32[1,1,3,6,2]{3,4,2,1,0:T(2,128)S(1)}, s32[1,1,3,6,2]{3,4,2,1,0:T(2,128)}, u32[]{:S(2)}) copy-start(s32[1,1,3,6,2]{3,4,2,1,0:T(2,128)} %param.4) | copy-start | bytes 436
  1.2 20.1 %collective-permute-start = (f32[368,128]{1,0:T(8,128)S(1)}, f32[368,128]{1,0:T(8,128)S(1)}, u32[]{:S(2)}, u32[]{:S(2)}) collective-permute-start(f32[368,128]{1,0:T(8,128)S(1)} %get-tuple-element.22.own_faces), channel_id=1, source_target_pairs={{128,56},{256,184},{384,312},{512,440},{640,568},{768,696},{896,82... | collective-permute-start | bytes 565256 | tf_op jit(solution)/shard_map/ppermute | solution.py:503
  12.0 10.0 %collective-permute-start.3 = (f32[368,128]{1,0:T(8,128)S(1)}, f32[368,128]{1,0:T(8,128)S(1)}, u32[]{:S(2)}, u32[]{:S(2)}) collective-permute-start(f32[368,128]{1,0:T(8,128)S(1)} %get-tuple-element.22.own_faces), channel_id=1, source_target_pairs={{0,8},{8,16},{16,24},{24,32},{32,40},{40,48},{48,56},{56,64},{64,7... | collective-permute-start | bytes 565256 | tf_op jit(solution)/shard_map/ppermute | solution.py:499
  13.3 8.7 %collective-permute-start.2 = (f32[368,128]{1,0:T(8,128)S(1)}, f32[368,128]{1,0:T(8,128)S(1)}, u32[]{:S(2)}, u32[]{:S(2)}) collective-permute-start(f32[368,128]{1,0:T(8,128)S(1)} %get-tuple-element.22.own_faces), channel_id=1, source_target_pairs={{8,0},{16,8},{24,16},{32,24},{40,32},{48,40},{56,48},{64,56},{72,6... | collective-permute-start | bytes 565256 | tf_op jit(solution)/shard_map/ppermute | solution.py:500
  14.6 7.4 %copy-start.1 = (f32[1,1,3,5,4096]{4,1,3,2,0:T(1,128)S(1)}, f32[1,1,3,5,4096]{4,1,3,2,0:T(1,128)}, u32[]{:S(2)}) copy-start(f32[1,1,3,5,4096]{4,1,3,2,0:T(1,128)} %param.3) | copy-start | bytes 737284
  21.3 0.7 %collective-permute-start.1 = (f32[368,128]{1,0:T(8,128)S(1)}, f32[368,128]{1,0:T(8,128)S(1)}, u32[]{:S(2)}, u32[]{:S(2)}) collective-permute-start(f32[368,128]{1,0:T(8,128)S(1)} %collective-permute-done.early_faces), channel_id=1, source_target_pairs={{56,120},{184,248},{312,376},{440,504},{568,632},{696,760},{824,88... | collective-permute-start | bytes 565256 | tf_op jit(solution)/shard_map/ppermute | solution.py:505
  22.7 12.5 %copy-start.3 = (s32[1,8]{1,0:T(1,128)S(1)}, s32[1,8]{1,0:T(1,128)}, u32[]{:S(2)}) copy-start(s32[1,8]{1,0:T(1,128)} %counts.1) | copy-start | bytes 100
  22.7 13.8 %collective-permute-start.6 = (f32[160,128]{1,0:T(8,128)S(1)}, f32[160,128]{1,0:T(8,128)S(1)}, u32[]{:S(2)}, u32[]{:S(2)}) collective-permute-start(f32[160,128]{1,0:T(8,128)S(1)} %get-tuple-element.30), channel_id=1, source_target_pairs={{0,2},{1,3},{2,0},{3,1},{4,6},{5,7},{6,4},{7,5},{8,10},{9,11},{10,... | collective-permute-start | bytes 245768 | tf_op jit(solution)/shard_map/ppermute | solution.py:508
  27.1 10.2 %collective-permute-start.5 = (f32[160,128]{1,0:T(8,128)S(1)}, f32[160,128]{1,0:T(8,128)S(1)}, u32[]{:S(2)}, u32[]{:S(2)}) collective-permute-start(f32[160,128]{1,0:T(8,128)S(1)} %get-tuple-element.30), channel_id=1, source_target_pairs={{0,4},{1,5},{2,6},{3,7},{4,0},{5,1},{6,2},{7,3},{8,12},{9,13},{10,... | collective-permute-start | bytes 245768 | tf_op jit(solution)/shard_map/ppermute | solution.py:508
  32.7 6.3 %collective-permute-start.4 = (f32[160,128]{1,0:T(8,128)S(1)}, f32[160,128]{1,0:T(8,128)S(1)}, u32[]{:S(2)}, u32[]{:S(2)}) collective-permute-start(f32[160,128]{1,0:T(8,128)S(1)} %get-tuple-element.30), channel_id=1, source_target_pairs={{0,1},{1,0},{2,3},{3,2},{4,5},{5,4},{6,7},{7,6},{8,9},{9,8},{10,11... | collective-permute-start | bytes 245768 | tf_op jit(solution)/shard_map/ppermute | solution.py:508

commit v7 on v6

--- a/solution.py
+++ b/solution.py
@@ -423,15 +423,12 @@
     )(*operands)
 
 
-def finish_kernel(rounds, state, total, counts, out, second, arrival):
+def finish_kernel(rounds, state, total, counts, out, arrival):
     _, last_count, arrival_round = final_counts(counts, lax.axis_index("sub"), rounds)
     arrival[...] = jnp.full(arrival.shape, arrival_round, jnp.int32)
-    for slot, field, half, here, there in square_moves():
+    for slot, field, _, here, there in square_moves():
         fresh = state[here, :] - courant * total[field, there, :]
-        fresh = jnp.where(slot < last_count, fresh, 0.0)
-        out[here, :] = fresh
-        if slot == 1:
-            second[pl.ds(field * 2 * EDGE + half, EDGE, stride=2), :] = fresh
+        out[here, :] = jnp.where(slot < last_count, fresh, 0.0)
 
 
 def finish(state, total, counts, rounds):
@@ -441,11 +438,10 @@
         functools.partial(finish_kernel, rounds),
         out_shape=(
             jax.ShapeDtypeStruct(state.shape, jnp.float32),
-            jax.ShapeDtypeStruct((BLOCK_ROWS, LANES), jnp.float32),
             jax.ShapeDtypeStruct((8, LANES), jnp.int32),
         ),
         in_specs=[vmem, vmem, smem],
-        out_specs=(vmem,) * 3,
+        out_specs=(vmem,) * 2,
         compiler_params=pltpu.CompilerParams(vmem_limit_bytes=VMEM_LIMIT),
         cost_estimate=pl.CostEstimate(flops=200_000, bytes_accessed=1_000_000, transcendentals=0),
         name="finish",
@@ -453,37 +449,33 @@
 
 
 def place_kernel(rounds, *refs):
-    arrived, (second, arrival, _, out, block, sem) = refs[:rounds], refs[rounds:]
+    arrived, (arrival, _, out, sem) = refs[:rounds], refs[rounds:]
     arrived = dict(zip(SEND_ORDER, arrived))
-    arrival_round = arrival[...]
-    for row in range(0, BLOCK_ROWS, 8):
-        rows = slice(row, row + 8)
-        value = second[rows, :]
-        for bit in range(rounds):
-            value = jnp.where(arrival_round == bit, arrived[bit][rows, :], value)
-        block[rows, :] = value
-    copy = pltpu.make_async_copy(block, out.at[pl.ds(BLOCK_ROWS, BLOCK_ROWS)], sem)
-    copy.start()
-    copy.wait()
-
-
-def place(arrived, out, second, arrival):
+    arrival_round = arrival[0, 0]
+    for bit in range(rounds):
+        @pl.when(arrival_round == bit)
+        def _():
+            copy = pltpu.make_async_copy(
+                arrived[bit], out.at[pl.ds(BLOCK_ROWS, BLOCK_ROWS)], sem
+            )
+            copy.start()
+            copy.wait()
+
+
+def place(arrived, out, arrival):
     rounds = len(arrived)
     vmem = pl.BlockSpec(memory_space=pltpu.VMEM)
     anywhere = pl.BlockSpec(memory_space=pl.ANY)
     return pl.pallas_call(
         functools.partial(place_kernel, rounds),
         out_shape=jax.ShapeDtypeStruct(out.shape, out.dtype),
-        in_specs=[vmem] * (rounds + 2) + [anywhere],
+        in_specs=[vmem] * (rounds + 1) + [anywhere],
         out_specs=anywhere,
-        scratch_shapes=[
-            pltpu.VMEM((BLOCK_ROWS, LANES), jnp.float32),
-            pltpu.SemaphoreType.DMA,
-        ],
-        input_output_aliases={rounds + 2: 0},
+        scratch_shapes=[pltpu.SemaphoreType.DMA],
+        input_output_aliases={rounds + 1: 0},
         compiler_params=pltpu.CompilerParams(vmem_limit_bytes=1024 * 1024),
         name="place",
-    )(*arrived.values(), second, arrival, out)
+    )(*arrived.values(), arrival, out)
 
 
 def body(state, neighbours, counts):
@@ -510,8 +502,8 @@
         )
         for bit in SEND_ORDER
     }
-    out, second, arrival = finish(state, total, counts, rounds)
-    return place(arrived, out, second, arrival).reshape(shape)
+    out, arrival = finish(state, total, counts, rounds)
+    return place(arrived, out, arrival).reshape(shape)
 
 
 def solution(mesh):

time: 39.9 us -> 40 us (level)
  no operation moved by 1% of the time
where the time goes in v7:
time: 40 us; the launch traced here: 39.7 us
  starting transfers between devices  26.4 us (66%)
  waiting for transfers between devices  7.64 us (19%)
  Pallas kernels  4.51 us (11%)
  local copies, waits for them, and re-layouts  0.96 us (2%)
    ppermute x3, starting transfers between devices, body(): lax.ppermute(moved, 'sub', [(s, s ^ 1 << bit) for s in range(lax.axis_siz...  12.4 us
    ppermute x1, starting transfers between devices, body(): relayed = lax.ppermute(faces, 'blocks', early)  10.7 us
    ppermute x1, waiting for transfers between devices, body(): relayed = lax.ppermute(faces, 'blocks', early)  5.18 us
    ppermute x3, waiting for transfers between devices, body(): lax.ppermute(moved, 'sub', [(s, s ^ 1 << bit) for s in range(lax.axis_siz...  2.45 us
    pallas_call x1, Pallas kernels, interior(): pl.pallas_call(inner_kernel, out_shape=(SQUARES, SQUARES, jax.ShapeDtypeS...  1.49 us
    pallas_call x1, Pallas kernels, finish(): pl.pallas_call(functools.partial(finish_kernel, rounds), out_shape=(jax.S...  1.36 us
    ppermute x1, starting transfers between devices, body(): low = lax.ppermute(faces, 'blocks', forward)  1.3 us
    ppermute x1, starting transfers between devices, body(): high = lax.ppermute(faces, 'blocks', backward)  1.29 us
  transfers between devices with their start and end apart: 7, of which 3 were waited for; matrix products, arithmetic and copies ran while one was open for 0% of the time, Pallas kernels for 7%

profile of v7, /device:TPU:112, one launch (start us, length us, event | category | flops | bytes accessed | tf_op | source)
XLA Modules:
  0.0 39.7 jit_solution(12171292309711842449)
XLA Ops:
  0.0 0.0 copy-start
  0.0 0.9 %copy-done = f32[1,1,3,5,4096]{4,1,3,2,0:T(1,128)S(1)} copy-done((f32[1,1,3,5,4096]{4,1,3,2,0:T(1,128)S(1)}, f32[1,1,3,5,4096]{4,1,3,2,0:T(1,128)}, u32[]{:S(2)}) %copy-start) | copy-done | bytes 245784
  0.9 0.3 prepare.1
  1.2 0.0 copy-start.2
  1.2 10.7 %collective-permute-start = (f32[368,128]{1,0:T(8,128)S(1)}, f32[368,128]{1,0:T(8,128)S(1)}, u32[]{:S(2)}, u32[]{:S(2)}) collective-permute-start(f32[368,128]{1,0:T(8,128)S(1)} %get-tuple-element.21.own_faces), channel_id=1, source_target_pairs={{128,56},{256,184},{384,312},{512,440},{640,568},{768,696},{896,82... | collective-permute-start | bytes 565256 | tf_op jit(solution)/shard_map/ppermute | solution.py:495
  12.0 1.3 %collective-permute-start.3 = (f32[368,128]{1,0:T(8,128)S(1)}, f32[368,128]{1,0:T(8,128)S(1)}, u32[]{:S(2)}, u32[]{:S(2)}) collective-permute-start(f32[368,128]{1,0:T(8,128)S(1)} %get-tuple-element.21.own_faces), channel_id=1, source_target_pairs={{0,8},{8,16},{16,24},{24,32},{32,40},{40,48},{48,56},{56,64},{64,7... | collective-permute-start | bytes 565256 | tf_op jit(solution)/shard_map/ppermute | solution.py:491
  13.3 1.3 %collective-permute-start.2 = (f32[368,128]{1,0:T(8,128)S(1)}, f32[368,128]{1,0:T(8,128)S(1)}, u32[]{:S(2)}, u32[]{:S(2)}) collective-permute-start(f32[368,128]{1,0:T(8,128)S(1)} %get-tuple-element.21.own_faces), channel_id=1, source_target_pairs={{8,0},{16,8},{24,16},{32,24},{40,32},{48,40},{56,48},{64,56},{72,6... | collective-permute-start | bytes 565256 | tf_op jit(solution)/shard_map/ppermute | solution.py:492
  14.6 0.0 copy-done.2
  14.6 0.0 copy-start.1
  14.6 1.5 %interior.1 = (f32[5,128,128]{2,1,0:T(8,128)S(1)}, f32[5,128,128]{2,1,0:T(8,128)S(1)}, s32[5,2,16,128]{3,2,1,0:T(8,128)S(1)}) custom-call(f32[5,128,128]{2,1,0:T(8,128)S(1)} %get-tuple-element.19.upright, f32[5,128,128]{2,1,0:T(8,128)S(1)} %get-tuple-element.20.turned, s32[3,2,6]{2,1,0:T(2,128)S(1)} %bitcast.8), custom_call_target="tpu_custom_call" | custom-call | flops 6000000 | bytes 3000000 | tf_op jit(solution)/shard_map/interior/pallas_call | solution.py:264
  16.1 5.2 %collective-permute-done.early_faces = f32[368,128]{1,0:T(8,128)S(1)} collective-permute-done((f32[368,128]{1,0:T(8,128)S(1)}, f32[368,128]{1,0:T(8,128)S(1)}, u32[]{:S(2)}, u32[]{:S(2)}) %collective-permute-start) | collective-permute-done | bytes 188448 | tf_op jit(solution)/shard_map/ppermute | solution.py:495
  21.3 0.7 %collective-permute-start.1 = (f32[368,128]{1,0:T(8,128)S(1)}, f32[368,128]{1,0:T(8,128)S(1)}, u32[]{:S(2)}, u32[]{:S(2)}) collective-permute-start(f32[368,128]{1,0:T(8,128)S(1)} %collective-permute-done.early_faces), channel_id=1, source_target_pairs={{56,120},{184,248},{312,376},{440,504},{568,632},{696,760},{824,88... | collective-permute-start | bytes 565256 | tf_op jit(solution)/shard_map/ppermute | solution.py:497
  22.0 0.0 collective-permute-done.3.low_faces
  22.0 0.0 collective-permute-done.2.high_faces
  22.0 0.0 collective-permute-done.1.high_crossing
  22.0 0.0 copy-done.1
  22.0 0.7 %outer.1 = (f32[5,128,128]{2,1,0:T(8,128)S(1)}, f32[160,128]{1,0:T(8,128)S(1)}) custom-call(f32[480,128]{1,0:T(8,128)S(1)} %bitcast.6, f32[5,128,128]{2,1,0:T(8,128)S(1)} %get-tuple-element.19.upright, f32[5,128,128]{2,1,0:T(8,128)S(1)} %get-tuple-element.20.turned, f32[5,128,128]{2,1,0:T(8,128)S(1)} %get-tuple-element.25.up_change, ...), custom_call_target="tpu_custom_call" | custom-call | tf_op jit(solution)/shard_map/outer/pallas_call | solution.py:415
  22.7 0.0 copy-start.3
  22.7 4.3 %collective-permute-start.6 = (f32[160,128]{1,0:T(8,128)S(1)}, f32[160,128]{1,0:T(8,128)S(1)}, u32[]{:S(2)}, u32[]{:S(2)}) collective-permute-start(f32[160,128]{1,0:T(8,128)S(1)} %get-tuple-element.29), channel_id=1, source_target_pairs={{0,2},{1,3},{2,0},{3,1},{4,6},{5,7},{6,4},{7,5},{8,10},{9,11},{10,... | collective-permute-start | bytes 245768 | tf_op jit(solution)/shard_map/ppermute | solution.py:500
  27.1 5.6 %collective-permute-start.5 = (f32[160,128]{1,0:T(8,128)S(1)}, f32[160,128]{1,0:T(8,128)S(1)}, u32[]{:S(2)}, u32[]{:S(2)}) collective-permute-start(f32[160,128]{1,0:T(8,128)S(1)} %get-tuple-element.29), channel_id=1, source_target_pairs={{0,4},{1,5},{2,6},{3,7},{4,0},{5,1},{6,2},{7,3},{8,12},{9,13},{10,... | collective-permute-start | bytes 245768 | tf_op jit(solution)/shard_map/ppermute | solution.py:500
  32.7 2.5 %collective-permute-start.4 = (f32[160,128]{1,0:T(8,128)S(1)}, f32[160,128]{1,0:T(8,128)S(1)}, u32[]{:S(2)}, u32[]{:S(2)}) collective-permute-start(f32[160,128]{1,0:T(8,128)S(1)} %get-tuple-element.29), channel_id=1, source_target_pairs={{0,1},{1,0},{2,3},{3,2},{4,5},{5,4},{6,7},{7,6},{8,9},{9,8},{10,11... | collective-permute-start | bytes 245768 | tf_op jit(solution)/shard_map/ppermute | solution.py:500
  35.2 0.0 copy-done.3
  35.2 1.4 %finish.1 = (f32[480,128]{1,0:T(8,128)}, s32[8,128]{1,0:T(8,128)S(1)}) custom-call(f32[480,128]{1,0:T(8,128)S(1)} %bitcast.7, f32[5,128,128]{2,1,0:T(8,128)S(1)} %get-tuple-element.30.total, s32[1,8]{1,0:T(1,128)S(1)} %copy-done.3), custom_call_target="tpu_custom_call" | custom-call | flops 200000 | bytes 1000000 | tf_op jit(solution)/shard_map/finish/pallas_call | solution.py:437
  36.5 0.0 collective-permute-done.6.refs_2_
  36.5 0.8 %collective-permute-done.5.refs_1_ = f32[160,128]{1,0:T(8,128)S(1)} collective-permute-done((f32[160,128]{1,0:T(8,128)S(1)}, f32[160,128]{1,0:T(8,128)S(1)}, u32[]{:S(2)}, u32[]{:S(2)}) %collective-permute-start.5) | collective-permute-done | bytes 81952 | tf_op jit(solution)/shard_map/ppermute | solution.py:500
  37.3 1.7 %collective-permute-done.4.refs_0_ = f32[160,128]{1,0:T(8,128)S(1)} collective-permute-done((f32[160,128]{1,0:T(8,128)S(1)}, f32[160,128]{1,0:T(8,128)S(1)}, u32[]{:S(2)}, u32[]{:S(2)}) %collective-permute-start.4) | collective-permute-done | bytes 81952 | tf_op jit(solution)/shard_map/ppermute | solution.py:500
  39.0 0.7 %place.1 = f32[480,128]{1,0:T(8,128)} custom-call(f32[160,128]{1,0:T(8,128)S(1)} %collective-permute-done.4.refs_0_, f32[160,128]{1,0:T(8,128)S(1)} %collective-permute-done.5.refs_1_, f32[160,128]{1,0:T(8,128)S(1)} %collective-permute-done.6.refs_2_, s32[8,128]{1,0:T(8,128)S(1)} %get-tuple-element.31.refs_3_, ...), custom_call_target="tpu_custom_call", output_to_operand_aliasing={{}: (4, {})} | custom-call | tf_op jit(solution)/shard_map/place/pallas_call | solution.py:469
Async XLA Ops:
  0.0 0.9 %copy-start = (f32[1,1,3,5,4096]{4,1,3,2,0:T(1,128)S(1)}, f32[1,1,3,5,4096]{4,1,3,2,0:T(1,128)}, u32[]{:S(2)}) copy-start(f32[1,1,3,5,4096]{4,1,3,2,0:T(1,128)} %param.3) | copy-start | bytes 737284
  1.2 13.4 %copy-start.2 = (s32[1,1,3,6,2]{3,4,2,1,0:T(2,128)S(1)}, s32[1,1,3,6,2]{3,4,2,1,0:T(2,128)}, u32[]{:S(2)}) copy-start(s32[1,1,3,6,2]{3,4,2,1,0:T(2,128)} %param.4) | copy-start | bytes 436
  1.2 20.1 %collective-permute-start = (f32[368,128]{1,0:T(8,128)S(1)}, f32[368,128]{1,0:T(8,128)S(1)}, u32[]{:S(2)}, u32[]{:S(2)}) collective-permute-start(f32[368,128]{1,0:T(8,128)S(1)} %get-tuple-element.21.own_faces), channel_id=1, source_target_pairs={{128,56},{256,184},{384,312},{512,440},{640,568},{768,696},{896,82... | collective-permute-start | bytes 565256 | tf_op jit(solution)/shard_map/ppermute | solution.py:495
  12.0 10.0 %collective-permute-start.3 = (f32[368,128]{1,0:T(8,128)S(1)}, f32[368,128]{1,0:T(8,128)S(1)}, u32[]{:S(2)}, u32[]{:S(2)}) collective-permute-start(f32[368,128]{1,0:T(8,128)S(1)} %get-tuple-element.21.own_faces), channel_id=1, source_target_pairs={{0,8},{8,16},{16,24},{24,32},{32,40},{40,48},{48,56},{56,64},{64,7... | collective-permute-start | bytes 565256 | tf_op jit(solution)/shard_map/ppermute | solution.py:491
  13.3 8.7 %collective-permute-start.2 = (f32[368,128]{1,0:T(8,128)S(1)}, f32[368,128]{1,0:T(8,128)S(1)}, u32[]{:S(2)}, u32[]{:S(2)}) collective-permute-start(f32[368,128]{1,0:T(8,128)S(1)} %get-tuple-element.21.own_faces), channel_id=1, source_target_pairs={{8,0},{16,8},{24,16},{32,24},{40,32},{48,40},{56,48},{64,56},{72,6... | collective-permute-start | bytes 565256 | tf_op jit(solution)/shard_map/ppermute | solution.py:492
  14.6 7.4 %copy-start.1 = (f32[1,1,3,5,4096]{4,1,3,2,0:T(1,128)S(1)}, f32[1,1,3,5,4096]{4,1,3,2,0:T(1,128)}, u32[]{:S(2)}) copy-start(f32[1,1,3,5,4096]{4,1,3,2,0:T(1,128)} %param.3) | copy-start | bytes 737284
  21.3 0.7 %collective-permute-start.1 = (f32[368,128]{1,0:T(8,128)S(1)}, f32[368,128]{1,0:T(8,128)S(1)}, u32[]{:S(2)}, u32[]{:S(2)}) collective-permute-start(f32[368,128]{1,0:T(8,128)S(1)} %collective-permute-done.early_faces), channel_id=1, source_target_pairs={{56,120},{184,248},{312,376},{440,504},{568,632},{696,760},{824,88... | collective-permute-start | bytes 565256 | tf_op jit(solution)/shard_map/ppermute | solution.py:497
  22.7 12.5 %copy-start.3 = (s32[1,8]{1,0:T(1,128)S(1)}, s32[1,8]{1,0:T(1,128)}, u32[]{:S(2)}) copy-start(s32[1,8]{1,0:T(1,128)} %counts.1) | copy-start | bytes 100
  22.7 13.8 %collective-permute-start.6 = (f32[160,128]{1,0:T(8,128)S(1)}, f32[160,128]{1,0:T(8,128)S(1)}, u32[]{:S(2)}, u32[]{:S(2)}) collective-permute-start(f32[160,128]{1,0:T(8,128)S(1)} %get-tuple-element.29), channel_id=1, source_target_pairs={{0,2},{1,3},{2,0},{3,1},{4,6},{5,7},{6,4},{7,5},{8,10},{9,11},{10,... | collective-permute-start | bytes 245768 | tf_op jit(solution)/shard_map/ppermute | solution.py:500
  27.1 10.2 %collective-permute-start.5 = (f32[160,128]{1,0:T(8,128)S(1)}, f32[160,128]{1,0:T(8,128)S(1)}, u32[]{:S(2)}, u32[]{:S(2)}) collective-permute-start(f32[160,128]{1,0:T(8,128)S(1)} %get-tuple-element.29), channel_id=1, source_target_pairs={{0,4},{1,5},{2,6},{3,7},{4,0},{5,1},{6,2},{7,3},{8,12},{9,13},{10,... | collective-permute-start | bytes 245768 | tf_op jit(solution)/shard_map/ppermute | solution.py:500
  32.7 6.3 %collective-permute-start.4 = (f32[160,128]{1,0:T(8,128)S(1)}, f32[160,128]{1,0:T(8,128)S(1)}, u32[]{:S(2)}, u32[]{:S(2)}) collective-permute-start(f32[160,128]{1,0:T(8,128)S(1)} %get-tuple-element.29), channel_id=1, source_target_pairs={{0,1},{1,0},{2,3},{3,2},{4,5},{5,4},{6,7},{7,6},{8,9},{9,8},{10,11... | collective-permute-start | bytes 245768 | tf_op jit(solution)/shard_map/ppermute | solution.py:500
